TPU v7x, 32 devices: a whole 2x2x4 slice. The times are simulated.
32 devices in a mesh: gx: 4 (over y, x), gy: 8 (over z, core).
Axes of the slice: x: 2, y: 2, z: 4, core: 2. Of those that a mesh axis runs over, the one named last changes fastest.
Arguments:
- charges: float32 [256, 128, 128], P('gx', 'gy'), may hold values from -6 to 6
- kernel_fine: bfloat16 [9, 9, 9], replicated, may hold values from -0.21875 to 0.21875
- kernel_mid: bfloat16 [9, 9, 9], replicated, may hold values from -0.109375 to 0.109375
- kernel_coarse: bfloat16 [9, 9, 9], replicated, may hold values from -0.0546875 to 0.0546875
Outputs:
- potential: float32 [256, 128, 128], P('gx', 'gy')
All inputs are finite; a program needn't handle non-finite values.
Results may differ from a plain program's by a relative error of at most 0.0028.
Values may be sent and summed in bfloat16 or wider, within the bound.
No kernel may reach another device: no remote copies, remote signals or barrier semaphores. Data moves between devices by JAX's collectives and lax.ppermute only.
A program may use at most 128 MiB of HBM per device.

v0:
```python
import functools

import jax
import jax.numpy as jnp
import numpy as np
from jax import lax
from jax.experimental import pallas as pl
from jax.experimental.pallas import tpu as pltpu
from jax.sharding import PartitionSpec as P

F32 = jnp.float32
BF16 = jnp.bfloat16
WIDE = 256
HALF = 128
VMEM_LIMIT = 56 * 1024 * 1024


def split_pair(v):
    high = v.astype(BF16).astype(F32)
    low = (v - high).astype(BF16).astype(F32)
    return high, low


def pair_lanes(v):
    return jnp.concatenate(split_pair(v), axis=-1)


def exact_dot(v, matrix):
    high, low = split_pair(v)
    return jnp.dot(high.astype(BF16), matrix, preferred_element_type=F32) + jnp.dot(
        low.astype(BF16), matrix, preferred_element_type=F32
    )


def transfer_matrix(fine, coarse, transpose):
    shape = (coarse, fine) if transpose else (fine, coarse)
    fine_at = lax.broadcasted_iota(jnp.int32, shape, 1 if transpose else 0)
    coarse_at = lax.broadcasted_iota(jnp.int32, shape, 0 if transpose else 1)
    d = fine_at - 2 * coarse_at
    one = jnp.where(d == 0, F32(1.0), F32(0.0))
    near = jnp.where((d == 1) | (d == -1), F32(0.5625), F32(0.0))
    far = jnp.where((d == 3) | (d == -3), F32(-0.0625), F32(0.0))
    return (one + near + far).astype(BF16)


def dot_last(v, matrix):
    lead = v.shape[:-1]
    return exact_dot(v.reshape(-1, v.shape[-1]), matrix).reshape(lead + (matrix.shape[1],))


def rows_at(v, first, low, count):
    begin, end = low - first, low - first + count
    inner = v[max(begin, 0) : min(end, v.shape[0])]
    parts = []
    if begin < 0:
        parts.append(jnp.zeros((-begin,) + v.shape[1:], v.dtype))
    parts.append(inner)
    if end > v.shape[0]:
        parts.append(jnp.zeros((end - v.shape[0],) + v.shape[1:], v.dtype))
    return jnp.concatenate(parts, axis=0) if len(parts) > 1 else inner


def weigh_restrict(even, odd0, odd_m1, odd_p1, odd_m2):
    return even + 0.5625 * (odd0 + odd_m1) - 0.0625 * (odd_p1 + odd_m2)


def restrict_rows(even, even_at, odd, odd_at, low, count):
    return weigh_restrict(
        rows_at(even, even_at, low, count),
        *(rows_at(odd, odd_at, low + s, count) for s in (0, -1, 1, -2)),
    )


def pairs_of_rows(v):
    v = v.reshape((v.shape[0] // 2, 2) + v.shape[1:])
    return v[:, 0], v[:, 1]


def inside(shape, axis, first, cells, index, count):
    at = lax.broadcasted_iota(jnp.int32, shape, axis) + first
    return ((at >= 0) | (index > 0)) & ((at < cells) | (index < count - 1))


def spread_kernel(counts, charges, up, down, mid_own, coarse_own, even_pad, odd_pad, crs):
    gx, gy = lax.axis_index("gx"), lax.axis_index("gy")
    nx, ny = counts
    cells_x, cells_y, cells_z = charges.shape
    mx, my, mz = cells_x // 2, cells_y // 2, cells_z // 2
    cx, cy, cz = cells_x // 4, cells_y // 4, cells_z // 4
    frame = mid_own.shape[1]
    even, odd = pairs_of_rows(charges[...])
    mid = restrict_rows(even, 0, odd, 0, -1, mx + 3)
    mid = dot_last(mid, transfer_matrix(cells_z, mz, False))
    even_pad[...] = jnp.zeros_like(even_pad)
    odd_pad[...] = jnp.zeros_like(odd_pad)
    mid_own[...] = mid
    even_pad[:, 8 : 8 + my] = mid_own[:, pl.ds(0, my, stride=2), :]
    odd_pad[:, 8 : 8 + my] = mid_own[:, pl.ds(1, my, stride=2), :]
    mid = weigh_restrict(
        even_pad[:, 7 : 7 + frame],
        *(odd_pad[:, 7 + s : 7 + s + frame] for s in (0, -1, 1, -2)),
    )
    keep = inside(mid.shape, 0, -1, mx, gx, nx) & inside(mid.shape, 1, -1, my, gy, ny)
    mid = jnp.where(keep, mid, 0.0)
    mid_own[...] = mid
    odd, even = pairs_of_rows(jnp.concatenate([mid, jnp.zeros_like(mid[:1])], axis=0))
    crs[...] = restrict_rows(even, 0, odd, -1, -2, cx + 5)
    n = cx + 5
    odd_pad[:n, 8 : 8 + frame // 2] = crs[:, pl.ds(0, frame // 2, stride=2), :]
    even_pad[:n, 8 : 8 + frame // 2] = crs[:, pl.ds(1, frame // 2, stride=2), :]
    coarse = weigh_restrict(
        even_pad[:n, 6 : 6 + frame],
        *(odd_pad[:n, 7 + s : 7 + s + frame] for s in (0, -1, 1, -2)),
    )
    coarse = dot_last(coarse, transfer_matrix(mz, cz, False))
    keep = inside(coarse.shape, 0, -2, cx, gx, nx) & inside(coarse.shape, 1, -2, cy, gy, ny)
    coarse = jnp.where(keep, coarse, 0.0)
    coarse_own[...] = coarse
    for out, fine_at, mid_at, coarse_at in ((up, cells_x - 4, mx - 4, cx - 4), (down, 0, 0, 0)):
        out[0:4] = charges[fine_at : fine_at + 4].astype(BF16)
        out[4:11] = pair_lanes(mid[mid_at : mid_at + 7]).astype(BF16)
        packed = pair_lanes(coarse[coarse_at : coarse_at + 9])
        blank = jnp.zeros(packed.shape[:-1] + (out.shape[2] - packed.shape[2],), F32)
        out[11:20] = jnp.concatenate([packed, blank], axis=-1).astype(BF16)


def unpair(v, width):
    return v[..., :width] + v[..., width : 2 * width]


def join_x_kernel(charges, mid_own, coarse_own, before, after, fine_x, mid_x, coarse_x, up, down, buf):
    cells_x, cells_y, _ = charges.shape
    mx, cx = cells_x // 2, cells_x // 4
    mz, cz = mid_own.shape[2], coarse_own.shape[2]
    my = cells_y // 2
    fine_x[0:4] = before[0:4].astype(F32)
    fine_x[4 : 4 + cells_x] = charges[...].astype(BF16).astype(F32)
    fine_x[4 + cells_x : 8 + cells_x] = after[0:4].astype(F32)
    low, high = before[4:11].astype(F32), after[4:11].astype(F32)
    mid = (
        rows_at(mid_own[...], -1, -5, mx + 11)
        + rows_at(unpair(low, mz), -5, -5, mx + 11)
        + rows_at(unpair(high, mz), mx - 1, -5, mx + 11)
    )
    mid_x[...] = mid
    low, high = before[11:20].astype(F32), after[11:20].astype(F32)
    coarse = (
        rows_at(coarse_own[...], -2, -6, cx + 13)
        + rows_at(unpair(low, cz), -6, -6, cx + 13)
        + rows_at(unpair(high, cz), cx - 2, -6, cx + 13)
    )
    coarse_x[...] = coarse
    buf[...] = jnp.zeros_like(buf)
    for out, fine_at, mid_at in ((up, cells_y - 4, my - 4), (down, 0, 0)):
        buf[:, 0:4, :] = fine_x[:, fine_at : fine_at + 4, :]
        buf[0 : mx + 11, 4:11, :] = pair_lanes(mid_x[:, mid_at : mid_at + 7, :])
        buf[mx + 11 : mx + cx + 24, 4:13, 0 : 2 * cz] = pair_lanes(coarse_x[:, 0:9, :])
        out[...] = buf[...].astype(BF16)


def join_y_kernel(
    fine_x, mid_x, coarse_x, before, after, fine_xy, mid_xy, coarse_xy, up, down, low, high, buf, side
):
    cells_y = fine_x.shape[1]
    my, cy = cells_y // 2, cells_y // 4
    rows_m, rows_c = mid_x.shape[0], coarse_x.shape[0]
    mz, cz = mid_x.shape[2], coarse_x.shape[2]
    low[...] = before[...].astype(F32)
    high[...] = after[...].astype(F32)
    fine_xy[:, 0:4, :] = low[:, 0:4, :]
    fine_xy[:, 4 : 4 + cells_y, :] = fine_x[...]
    fine_xy[:, 4 + cells_y : 8 + cells_y, :] = high[:, 0:4, :]
    mid_xy[...] = jnp.zeros_like(mid_xy)
    mid_xy[:, 4 : 7 + my, :] = mid_x[:, 0 : my + 3, :]
    mid_xy[:, 0:7, :] += unpair(low[0:rows_m, 4:11, :], mz)
    mid_xy[:, 4 + my : 11 + my, :] += unpair(high[0:rows_m, 4:11, :], mz)
    from_low = unpair(low[rows_m : rows_m + rows_c, 4:13, :], cz)
    from_high = unpair(high[rows_m : rows_m + rows_c, 4:13, :], cz)
    side[...] = jnp.zeros_like(side)
    side[:, 4 : 9 + cy, :] = coarse_x[:, 0 : cy + 5, :]
    coarse_xy[...] = side[...]
    coarse_xy[:, 0:9, :] += from_low
    half = up.shape[0]
    buf[...] = jnp.zeros_like(buf)

    def pack(rows, out):
        buf[:, 0:5, 0 : 2 * cz] = pair_lanes(rows[0:half])
        buf[0 : rows_c - half, 8:13, 0 : 2 * cz] = pair_lanes(rows[half:rows_c])
        out[...] = buf[...].astype(BF16)

    pack(coarse_xy[:, 4 + cy : 9 + cy, :], up)
    coarse_xy[:, 4 + cy : 13 + cy, :] += from_high
    side[:, 4 + cy : 13 + cy, :] += from_high
    pack(side[:, 4:9, :], down)


def base_plan(depth, groups):
    per = HALF // depth
    offsets = range(-1, 2 * groups)
    plan = np.full((len(offsets), 2, HALF), -1, np.int64)
    for i, offset in enumerate(offsets):
        for sign in (0, 1):
            for t in range(HALF):
                d = t - HALF * sign
                j = int(np.floor(d / depth + 0.5))
                e = d - depth * j
                tap = per * offset - j
                if abs(e) <= 4 and 0 <= tap <= 8 and abs(j) < per:
                    plan[i, sign, t] = tap * 9 + 4 - e
    return plan


def one_hot_of(plan):
    flat = plan.reshape(-1)
    return (np.arange(HALF)[:, None] == flat[None, :]).astype(jnp.bfloat16)


def bands_kernel(depth, groups, stencil, one_hot, out, bases):
    per = HALF // depth
    values = jnp.dot(stencil[...], one_hot[...], preferred_element_type=F32)
    for dx in range(9):
        bases[dx] = jnp.broadcast_to(values[dx : dx + 1], bases.shape[1:])
    row = lax.broadcasted_iota(jnp.int32, (HALF, HALF), 0)
    col = lax.broadcasted_iota(jnp.int32, (HALF, HALF), 1)
    apart = lax.rem(row, depth) - lax.rem(col, depth)
    band = (apart <= 4) & (apart >= -4)
    right = band & (col >= row)
    left = band & (col < row)

    def one_dx(dx, carry):
        def rolled(i, sign):
            at = (2 * i + sign) * HALF
            line = bases[dx, :, at : at + HALF]
            full = jnp.concatenate([line] * (HALF // 8), axis=0)
            return pltpu.roll(full, 0, 1, stride=1, stride_axis=0)

        for i in range(2 * groups + 1):
            offset = i - 1
            block = jnp.where(right, rolled(i, 0), jnp.where(left, rolled(i, 1), 0.0)).astype(BF16)
            for group in range(groups):
                for a in (0, 1):
                    b = 2 * group + a - offset
                    if b in (0, 1):
                        out[
                            dx,
                            group * WIDE + a * HALF : group * WIDE + (a + 1) * HALF,
                            b * HALF : (b + 1) * HALF,
                        ] = block
        return carry

    lax.fori_loop(0, 9, one_dx, 0)


def bands(stencil, depth, groups):
    one_hot = jnp.asarray(one_hot_of(base_plan(depth, groups)))
    flat = jnp.pad(stencil.reshape(9, 81), ((0, 7), (0, HALF - 81)))
    return pl.pallas_call(
        functools.partial(bands_kernel, depth, groups),
        out_shape=jax.ShapeDtypeStruct((9, groups * WIDE, WIDE), BF16),
        in_specs=[whole(), whole()],
        out_specs=whole(),
        scratch_shapes=[pltpu.VMEM((9, 8, one_hot.shape[1]), F32)],
        compiler_params=pltpu.CompilerParams(vmem_limit_bytes=VMEM_LIMIT),
        cost_estimate=pl.CostEstimate(flops=2 * 10**9, bytes_accessed=4 * 10**6, transcendentals=0),
    )(flat, one_hot)


def gather_rows(field, rows, per, groups, depth, lhs):
    for parity in (0, 1):
        count = rows - parity
        for group in range(groups):
            for a in range(per):
                lane = group * WIDE + a * depth
                part = field[parity:rows, pl.ds(a + per * group, 8, stride=per), :]
                lhs[parity, 0 : count * 8, lane : lane + depth] = part.reshape(count * 8, depth).astype(BF16)


def convolve(lhs, weights, out_rows, acc):
    n = out_rows * 8
    for dx in range(9):
        start = 16 * (dx // 2)
        part = jnp.dot(lhs[dx % 2, start : start + n, :], weights[dx], preferred_element_type=F32)
        acc[...] = part if dx == 0 else acc[...] + part


def conv_kernel(fine_xy, mid_xy, fine_w, mid_w, fine_acc, mid_acc, mid_pad, fine_lhs, mid_lhs):
    rows = fine_xy.shape[0]
    gather_rows(fine_xy, rows, 2, 5, fine_xy.shape[2], fine_lhs)
    convolve(fine_lhs, fine_w, rows - 8, fine_acc)
    mid_pad[...] = jnp.zeros_like(mid_pad)
    mid_pad[:, 0 : mid_xy.shape[1], :] = mid_xy[...]
    gather_rows(mid_pad, mid_pad.shape[0], 4, 3, mid_xy.shape[2], mid_lhs)
    convolve(mid_lhs, mid_w, mid_pad.shape[0] - 8, mid_acc)


def prolong_odd(a, b, c, d):
    return 0.5625 * (b + c) - 0.0625 * (a + d)


def finish_kernel(
    counts, coarse_xy, before, after, coarse_w, fine_acc, mid_acc, out,
    crs_pad, crs_lhs, crs_acc, msg, crs_pot, wide, mid_tot,
):
    gx, gy = lax.axis_index("gx"), lax.axis_index("gy")
    nx, ny = counts
    rows_c, _, cz = coarse_xy.shape
    cells_x, cells_y, cells_z = out.shape
    mx, my, mz = cells_x // 2, cells_y // 2, cells_z // 2
    cx, cy = cells_x // 4, cells_y // 4
    half = before.shape[0]
    crs_pad[...] = jnp.zeros_like(crs_pad)
    crs_pad[:, 0 : coarse_xy.shape[1], :] = coarse_xy[...]
    for source, at in ((before, 0), (after, cy + 8)):
        msg[...] = source[...].astype(F32)
        crs_pad[0:half, at : at + 5, :] += unpair(msg[:, 0:5, :], cz)
        crs_pad[half:rows_c, at : at + 5, :] += unpair(msg[0 : rows_c - half, 8:13, :], cz)
    gather_rows(crs_pad, rows_c, 8, 2, cz, crs_lhs)
    convolve(crs_lhs, coarse_w, rows_c - 8, crs_acc)
    rows = rows_c - 8
    pot = crs_acc[...].reshape(rows, 8, WIDE)
    for b in range(8):
        crs_pot[:, pl.ds(b, 2, stride=8), :] = pot[:, 0:2, b * cz : (b + 1) * cz]
    pot = crs_pot[...]
    keep = inside(pot.shape, 0, -2, cx, gx, nx) & inside(pot.shape, 1, -2, cy, gy, ny)
    pot = jnp.where(keep, pot, 0.0)
    n = cx + 2
    odd = prolong_odd(*(pot[s : s + n] for s in range(4)))
    even = jnp.concatenate([pot[2 : 1 + n], jnp.zeros_like(pot[:1])], axis=0) if n + 2 > rows else pot[2 : 2 + n]
    wide[:, 0] = odd
    wide[:, 1] = even
    wide_y = cy + 2
    v = wide[...].reshape((2 * n,) + pot.shape[1:])
    mid_tot[...] = jnp.zeros_like(mid_tot)
    odd = prolong_odd(*(v[:, s : s + wide_y] for s in range(4)))
    even = v[:, 2 : 1 + wide_y]
    matrix = transfer_matrix(mz, cz, True)
    mid_tot[:, pl.ds(0, wide_y, stride=2), 0:cz] = odd
    mid_tot[:, pl.ds(1, wide_y - 1, stride=2), 0:cz] = even
    total = dot_last(mid_tot[:, :, 0:cz], matrix)
    rows = mx + 3
    pot = mid_acc[...].reshape(rows, 8, WIDE)
    for b in range(4):
        mid_tot[0:rows, pl.ds(b, 3, stride=4), :] = pot[:, 0:3, b * mz : (b + 1) * mz]
    total = mid_tot[0:rows] + total[0:rows]
    keep = inside(total.shape, 0, -1, mx, gx, nx) & inside(total.shape, 1, -1, my, gy, ny)
    mid_tot[0:rows] = jnp.where(keep, total, 0.0)
    matrix = transfer_matrix(cells_z, mz, True)
    pot = fine_acc[...].reshape(cells_x, 8, WIDE)
    for a in (0, 1):
        if a == 0:
            u = mid_tot[0:rows, 1 : 1 + my, :]
        else:
            u = prolong_odd(*(mid_tot[0:rows, s : s + my, :] for s in range(4)))
        u = dot_last(u, matrix)
        odd = prolong_odd(*(u[s : s + mx] for s in range(4)))
        both = jnp.stack([u[1 : 1 + mx], odd], axis=1).reshape(cells_x, my, cells_z)
        out[:, pl.ds(a, my, stride=2), :] = pot[:, :, a * HALF : a * HALF + cells_z] + both


def whole():
    return pl.BlockSpec(memory_space=pltpu.VMEM)


def call(kernel, outs, ins, scratch, flops=10**8):
    return pl.pallas_call(
        kernel,
        out_shape=[jax.ShapeDtypeStruct(s, d) for s, d in outs],
        in_specs=[whole()] * len(ins),
        out_specs=[whole()] * len(outs),
        scratch_shapes=[pltpu.VMEM(s, d) for s, d in scratch],
        compiler_params=pltpu.CompilerParams(vmem_limit_bytes=VMEM_LIMIT),
        cost_estimate=pl.CostEstimate(flops=flops, bytes_accessed=10**6, transcendentals=0),
    )(*ins)


def exchange(up, down, axis, step, size):
    forward = [(i, i + step) for i in range(size - step)]
    backward = [(j, i) for i, j in forward]
    return lax.ppermute(up, axis, forward), lax.ppermute(down, axis, backward)


def local(counts, charges, kernel_fine, kernel_mid, kernel_coarse):
    nx, ny = counts
    cells_x, cells_y, cells_z = charges.shape
    mx, mz, cx, cz = cells_x // 2, cells_z // 2, cells_x // 4, cells_z // 4
    frame = cells_y
    fine_w = bands(kernel_fine, cells_z, 5)
    mid_w = bands(kernel_mid, mz, 3)
    coarse_w = bands(kernel_coarse, cz, 2)
    message = ((20, frame, cells_z), BF16)
    up, down, mid_own, coarse_own = call(
        functools.partial(spread_kernel, counts),
        [message, message, ((mx + 3, frame, mz), F32), ((cx + 5, frame, cz), F32)],
        [charges],
        [((mx + 3, frame + 24, mz), F32), ((mx + 3, frame + 24, mz), F32), ((cx + 5, frame, mz), F32)],
    )
    before, after = exchange(up, down, "gx", 1, nx)
    message = ((cells_x + 8, frame, cells_z), BF16)
    fine_x, mid_x, coarse_x, up, down = call(
        join_x_kernel,
        [
            ((cells_x + 8, cells_y, cells_z), F32),
            ((mx + 11, frame, mz), F32),
            ((cx + 13, frame, cz), F32),
            message,
            message,
        ],
        [charges, mid_own, coarse_own, before, after],
        [((cells_x + 8, frame, cells_z), F32)],
    )
    before, after = exchange(up, down, "gy", 1, ny)
    half = (cx + 14) // 2
    message = ((half, frame, cells_z), BF16)
    fine_xy, mid_xy, coarse_xy, up, down = call(
        join_y_kernel,
        [
            ((cells_x + 8, cells_y + 8, cells_z), F32),
            ((mx + 11, frame + 8, mz), F32),
            ((cx + 13, frame + 8, cz), F32),
            message,
            message,
        ],
        [fine_x, mid_x, coarse_x, before, after],
        [
            ((cells_x + 8, frame, cells_z), F32),
            ((cells_x + 8, frame, cells_z), F32),
            ((half, frame, cells_z), F32),
            ((cx + 13, frame + 8, cz), F32),
        ],
    )
    before, after = exchange(up, down, "gy", 2, ny)
    fine_acc, mid_acc = call(
        conv_kernel,
        [((cells_x * 8, WIDE), F32), (((mx + 3) * 8, WIDE), F32)],
        [fine_xy, mid_xy, fine_w, mid_w],
        [
            ((mx + 11, frame + 32, mz), F32),
            ((2, (cells_x + 8) * 8, 5 * WIDE), BF16),
            ((2, (mx + 12) * 8, 3 * WIDE), BF16),
        ],
        flops=10**10,
    )
    (out,) = call(
        functools.partial(finish_kernel, counts),
        [(charges.shape, F32)],
        [coarse_xy, before, after, coarse_w, fine_acc, mid_acc],
        [
            ((cx + 13, 80, cz), F32),
            ((2, (cx + 14) * 8, 2 * WIDE), BF16),
            (((cx + 5) * 8, WIDE), F32),
            ((half, frame, cells_z), F32),
            ((cx + 5, 16, cz), F32),
            ((cx + 2, 2, 16, cz), F32),
            ((mx + 4, 16, mz), F32),
        ],
    )
    return out


def solution(mesh):
    counts = (mesh.shape["gx"], mesh.shape["gy"])
    placed = (P("gx", "gy", None), P(), P(), P())
    return jax.shard_map(
        functools.partial(local, counts),
        mesh=mesh,
        in_specs=placed,
        out_specs=P("gx", "gy", None),
        check_vma=False,
    )
```

profile of v0, /device:TPU:20, one launch (start us, length us, event | category | flops | bytes accessed | tf_op | source)
XLA Modules:
  0.0 60.8 jit_solution(11805755542033407605)
XLA Ops:
  0.0 2.7 %shard_map.73 = (bf16[20,16,128]{2,1,0:T(8,128)(2,1)}, bf16[20,16,128]{2,1,0:T(8,128)(2,1)}, f32[35,16,64]{2,1,0:T(8,128)}, f32[21,16,32]{2,1,0:T(8,128)}) custom-call(f32[64,16,128]{2,1,0:T(8,128)} %charges.3), custom_call_target="tpu_custom_call" | custom-call | flops 100000000 | bytes 1000000 | tf_op jit(solution)/shard_map/pallas_call | solution.py:365
  2.7 3.4 %collective-permute-start = (bf16[20,16,128]{2,1,0:T(8,128)(2,1)}, bf16[20,16,128]{2,1,0:T(8,128)(2,1)S(1)}, u32[]{:S(2)}, u32[]{:S(2)}) collective-permute-start(bf16[20,16,128]{2,1,0:T(8,128)(2,1)} %get-tuple-element.23), channel_id=1, source_target_pairs={{0,8},{8,16},{16,24},{1,9},{9,17},{17,25},{2,10},{10,18},{18,26},{... | collective-permute-start | bytes 245768 | tf_op jit(solution)/shard_map/ppermute | solution.py:379
  6.1 3.3 %collective-permute-start.1 = (bf16[20,16,128]{2,1,0:T(8,128)(2,1)}, bf16[20,16,128]{2,1,0:T(8,128)(2,1)S(1)}, u32[]{:S(2)}, u32[]{:S(2)}) collective-permute-start(bf16[20,16,128]{2,1,0:T(8,128)(2,1)} %get-tuple-element.24), channel_id=1, source_target_pairs={{8,0},{16,8},{24,16},{9,1},{17,9},{25,17},{10,2},{18,10},{26,18},{... | collective-permute-start | bytes 245768 | tf_op jit(solution)/shard_map/ppermute | solution.py:379
  9.4 0.9 %reshape.10 = bf16[9,81]{1,0:T(8,128)(2,1)S(1)} reshape(bf16[9,9,9]{2,1,0:T(8,128)(2,1)} %param.8) | data formatting | bytes 2916 | tf_op jit(solution)/shard_map/reshape | solution.py:256
  10.3 0.6 pad.11.stencil
  10.9 0.0 copy-start.6
  10.9 0.0 copy-start.7
  10.9 6.2 %shard_map.77.fine_w = bf16[9,1280,256]{2,1,0:T(8,128)(2,1)} custom-call(bf16[16,128]{1,0:T(8,128)(2,1)} %pad.11.stencil, bf16[128,2816]{1,0:T(8,128)(2,1)} %constant.9.clone.one_hot), custom_call_target="tpu_custom_call" | custom-call | flops 2000000000 | bytes 4000000 | tf_op jit(solution)/shard_map/pallas_call | solution.py:257
  17.1 0.0 copy-done.6
  17.1 0.1 reshape.11
  17.2 0.6 pad.12.stencil
  17.8 0.0 copy-done.7
  17.8 0.1 reshape.9
  17.9 0.6 pad.10.stencil
  18.5 0.0 collective-permute-done.before
  18.5 0.0 copy-start.2
  18.5 0.0 collective-permute-done.1.after
  18.5 0.0 copy-start.3
  18.5 0.6 %copy-done.2 = bf16[20,16,128]{2,1,0:T(8,128)(2,1)} copy-done((bf16[20,16,128]{2,1,0:T(8,128)(2,1)}, bf16[20,16,128]{2,1,0:T(8,128)(2,1)S(1)}, u32[]{:S(2)}) %copy-start.2) | copy-done | bytes 81944
  19.1 0.0 copy-done.3
  19.2 2.6 %shard_map.74 = (f32[72,16,128]{2,1,0:T(8,128)}, f32[43,16,64]{2,1,0:T(8,128)}, f32[29,16,32]{2,1,0:T(8,128)}, bf16[72,16,128]{2,1,0:T(8,128)(2,1)}, bf16[72,16,128]{2,1,0:T(8,128)(2,1)}) custom-call(f32[64,16,128]{2,1,0:T(8,128)} %charges.3, f32[35,16,64]{2,1,0:T(8,128)} %get-tuple-element.21.mid_own, f32[21,16,32]{2,1,0:T(8,128)} %get-tuple-element.22.coarse_own, ...), custom_call_target="tpu_custom_call" | custom-call | flops 100000000 | bytes 1000000 | tf_op jit(solution)/shard_map/pallas_call | solution.py:365
  21.8 1.9 %collective-permute-start.2 = (bf16[72,16,128]{2,1,0:T(8,128)(2,1)}, bf16[72,16,128]{2,1,0:T(8,128)(2,1)S(1)}, u32[]{:S(2)}, u32[]{:S(2)}) collective-permute-start(bf16[72,16,128]{2,1,0:T(8,128)(2,1)} %get-tuple-element.28), channel_id=1, source_target_pairs={{0,1},{1,2},{2,3},{3,4},{4,5},{5,6},{6,7},{8,9},{9,10},{10,11},{11... | collective-permute-start | bytes 884744 | tf_op jit(solution)/shard_map/ppermute | solution.py:379
  23.7 3.6 %collective-permute-start.3 = (bf16[72,16,128]{2,1,0:T(8,128)(2,1)}, bf16[72,16,128]{2,1,0:T(8,128)(2,1)S(1)}, u32[]{:S(2)}, u32[]{:S(2)}) collective-permute-start(bf16[72,16,128]{2,1,0:T(8,128)(2,1)} %get-tuple-element.29), channel_id=1, source_target_pairs={{1,0},{2,1},{3,2},{4,3},{5,4},{6,5},{7,6},{9,8},{10,9},{11,10},{12... | collective-permute-start | bytes 884744 | tf_op jit(solution)/shard_map/ppermute | solution.py:379
  27.4 4.8 %shard_map.78.mid_w = bf16[9,768,256]{2,1,0:T(8,128)(2,1)} custom-call(bf16[16,128]{1,0:T(8,128)(2,1)} %pad.12.stencil, bf16[128,1792]{1,0:T(8,128)(2,1)} %constant.10.clone.one_hot), custom_call_target="tpu_custom_call" | custom-call | flops 2000000000 | bytes 4000000 | tf_op jit(solution)/shard_map/pallas_call | solution.py:257
  32.1 4.0 %shard_map.76.coarse_w = bf16[9,512,256]{2,1,0:T(8,128)(2,1)} custom-call(bf16[16,128]{1,0:T(8,128)(2,1)} %pad.10.stencil, bf16[128,1280]{1,0:T(8,128)(2,1)} %constant.11.clone.one_hot), custom_call_target="tpu_custom_call" | custom-call | flops 2000000000 | bytes 4000000 | tf_op jit(solution)/shard_map/pallas_call | solution.py:257
  36.1 0.0 collective-permute-done.2.before
  36.1 0.0 copy-start
  36.1 0.0 collective-permute-done.3.after
  36.1 0.0 copy-start.1
  36.1 0.7 %copy-done = bf16[72,16,128]{2,1,0:T(8,128)(2,1)} copy-done((bf16[72,16,128]{2,1,0:T(8,128)(2,1)}, bf16[72,16,128]{2,1,0:T(8,128)(2,1)S(1)}, u32[]{:S(2)}) %copy-start) | copy-done | bytes 294936
  36.8 0.1 copy-done.1
  36.9 3.0 %shard_map.75 = (f32[72,24,128]{2,1,0:T(8,128)}, f32[43,24,64]{2,1,0:T(8,128)}, f32[29,24,32]{2,1,0:T(8,128)}, bf16[15,16,128]{2,1,0:T(8,128)(2,1)}, bf16[15,16,128]{2,1,0:T(8,128)(2,1)}) custom-call(f32[72,16,128]{2,1,0:T(8,128)} %get-tuple-element.25.fine_x, f32[43,16,64]{2,1,0:T(8,128)} %get-tuple-element.26.mid_x, ...), custom_call_target="tpu_custom_call" | custom-call | flops 100000000 | bytes 1000000 | tf_op jit(solution)/shard_map/pallas_call | solution.py:365
  39.9 3.5 %collective-permute-start.4 = (bf16[15,16,128]{2,1,0:T(8,128)(2,1)}, bf16[15,16,128]{2,1,0:T(8,128)(2,1)S(1)}, u32[]{:S(2)}, u32[]{:S(2)}) collective-permute-start(bf16[15,16,128]{2,1,0:T(8,128)(2,1)} %get-tuple-element.31), channel_id=1, source_target_pairs={{0,2},{1,3},{2,4},{3,5},{4,6},{5,7},{8,10},{9,11},{10,12},{11,13},... | collective-permute-start | bytes 184328 | tf_op jit(solution)/shard_map/ppermute | solution.py:379
  43.4 2.4 %collective-permute-start.5 = (bf16[15,16,128]{2,1,0:T(8,128)(2,1)}, bf16[15,16,128]{2,1,0:T(8,128)(2,1)S(1)}, u32[]{:S(2)}, u32[]{:S(2)}) collective-permute-start(bf16[15,16,128]{2,1,0:T(8,128)(2,1)} %get-tuple-element.32), channel_id=1, source_target_pairs={{2,0},{3,1},{4,2},{5,3},{6,4},{7,5},{10,8},{11,9},{12,10},{13,11},... | collective-permute-start | bytes 184328 | tf_op jit(solution)/shard_map/ppermute | solution.py:379
  45.8 9.4 %shard_map.79 = (f32[512,256]{1,0:T(8,128)}, f32[280,256]{1,0:T(8,128)}) custom-call(f32[72,24,128]{2,1,0:T(8,128)} %get-tuple-element.33.fine_xy, f32[43,24,64]{2,1,0:T(8,128)} %get-tuple-element.34.mid_xy, bf16[9,1280,256]{2,1,0:T(8,128)(2,1)} %shard_map.77.fine_w, bf16[9,768,256]{2,1,0:T(8,128)(2,1)} %shard_map.78.mid_w), custom_call_target="tpu_custom_call" | custom-call | flops 10000000000 | bytes 1000000 | tf_op jit(solution)/shard_map/pallas_call | solution.py:365
  55.1 0.0 collective-permute-done.4.before
  55.1 0.0 copy-start.4
  55.2 0.0 collective-permute-done.5.after
  55.2 0.0 copy-start.5
  55.2 0.6 copy-done.4
  55.8 0.0 copy-done.5
  55.8 5.0 %shard_map.80 = f32[64,16,128]{2,1,0:T(8,128)} custom-call(f32[29,24,32]{2,1,0:T(8,128)} %get-tuple-element.30.coarse_xy, bf16[15,16,128]{2,1,0:T(8,128)(2,1)} %copy-done.4, bf16[15,16,128]{2,1,0:T(8,128)(2,1)} %copy-done.5, bf16[9,512,256]{2,1,0:T(8,128)(2,1)} %shard_map.76.coarse_w, f32[512,256]{1,0:T(8,128)} %get-tuple-element.35.fine_acc, ...), custom_call_target="tpu_custom_call" | custom-call | flops 100000000 | bytes 1000000 | tf_op jit(solution)/shard_map/pallas_call | solution.py:365
Async XLA Ops:
  2.7 15.8 %collective-permute-start = (bf16[20,16,128]{2,1,0:T(8,128)(2,1)}, bf16[20,16,128]{2,1,0:T(8,128)(2,1)S(1)}, u32[]{:S(2)}, u32[]{:S(2)}) collective-permute-start(bf16[20,16,128]{2,1,0:T(8,128)(2,1)} %get-tuple-element.23), channel_id=1, source_target_pairs={{0,8},{8,16},{16,24},{1,9},{9,17},{17,25},{2,10},{10,18},{18,26},{... | collective-permute-start | bytes 245768 | tf_op jit(solution)/shard_map/ppermute | solution.py:379
  6.1 12.4 %collective-permute-start.1 = (bf16[20,16,128]{2,1,0:T(8,128)(2,1)}, bf16[20,16,128]{2,1,0:T(8,128)(2,1)S(1)}, u32[]{:S(2)}, u32[]{:S(2)}) collective-permute-start(bf16[20,16,128]{2,1,0:T(8,128)(2,1)} %get-tuple-element.24), channel_id=1, source_target_pairs={{8,0},{16,8},{24,16},{9,1},{17,9},{25,17},{10,2},{18,10},{26,18},{... | collective-permute-start | bytes 245768 | tf_op jit(solution)/shard_map/ppermute | solution.py:379
  10.9 6.2 %copy-start.6 = (bf16[9,9,9]{2,1,0:T(8,128)(2,1)S(1)}, bf16[9,9,9]{2,1,0:T(8,128)(2,1)}, u32[]{:S(2)}) copy-start(bf16[9,9,9]{2,1,0:T(8,128)(2,1)} %param.9) | copy-start | bytes 4378
  10.9 6.9 %copy-start.7 = (bf16[9,9,9]{2,1,0:T(8,128)(2,1)S(1)}, bf16[9,9,9]{2,1,0:T(8,128)(2,1)}, u32[]{:S(2)}) copy-start(bf16[9,9,9]{2,1,0:T(8,128)(2,1)} %param.10) | copy-start | bytes 4378
  18.5 0.6 %copy-start.2 = (bf16[20,16,128]{2,1,0:T(8,128)(2,1)}, bf16[20,16,128]{2,1,0:T(8,128)(2,1)S(1)}, u32[]{:S(2)}) copy-start(bf16[20,16,128]{2,1,0:T(8,128)(2,1)S(1)} %collective-permute-done.before) | copy-start | bytes 245764
  18.5 0.7 %copy-start.3 = (bf16[20,16,128]{2,1,0:T(8,128)(2,1)}, bf16[20,16,128]{2,1,0:T(8,128)(2,1)S(1)}, u32[]{:S(2)}) copy-start(bf16[20,16,128]{2,1,0:T(8,128)(2,1)S(1)} %collective-permute-done.1.after) | copy-start | bytes 245764
  21.8 14.3 %collective-permute-start.2 = (bf16[72,16,128]{2,1,0:T(8,128)(2,1)}, bf16[72,16,128]{2,1,0:T(8,128)(2,1)S(1)}, u32[]{:S(2)}, u32[]{:S(2)}) collective-permute-start(bf16[72,16,128]{2,1,0:T(8,128)(2,1)} %get-tuple-element.28), channel_id=1, source_target_pairs={{0,1},{1,2},{2,3},{3,4},{4,5},{5,6},{6,7},{8,9},{9,10},{10,11},{11... | collective-permute-start | bytes 884744 | tf_op jit(solution)/shard_map/ppermute | solution.py:379
  23.7 12.4 %collective-permute-start.3 = (bf16[72,16,128]{2,1,0:T(8,128)(2,1)}, bf16[72,16,128]{2,1,0:T(8,128)(2,1)S(1)}, u32[]{:S(2)}, u32[]{:S(2)}) collective-permute-start(bf16[72,16,128]{2,1,0:T(8,128)(2,1)} %get-tuple-element.29), channel_id=1, source_target_pairs={{1,0},{2,1},{3,2},{4,3},{5,4},{6,5},{7,6},{9,8},{10,9},{11,10},{12... | collective-permute-start | bytes 884744 | tf_op jit(solution)/shard_map/ppermute | solution.py:379
  36.1 0.7 %copy-start = (bf16[72,16,128]{2,1,0:T(8,128)(2,1)}, bf16[72,16,128]{2,1,0:T(8,128)(2,1)S(1)}, u32[]{:S(2)}) copy-start(bf16[72,16,128]{2,1,0:T(8,128)(2,1)S(1)} %collective-permute-done.2.before) | copy-start | bytes 884740
  36.1 0.8 %copy-start.1 = (bf16[72,16,128]{2,1,0:T(8,128)(2,1)}, bf16[72,16,128]{2,1,0:T(8,128)(2,1)S(1)}, u32[]{:S(2)}) copy-start(bf16[72,16,128]{2,1,0:T(8,128)(2,1)S(1)} %collective-permute-done.3.after) | copy-start | bytes 884740
  39.9 15.2 %collective-permute-start.4 = (bf16[15,16,128]{2,1,0:T(8,128)(2,1)}, bf16[15,16,128]{2,1,0:T(8,128)(2,1)S(1)}, u32[]{:S(2)}, u32[]{:S(2)}) collective-permute-start(bf16[15,16,128]{2,1,0:T(8,128)(2,1)} %get-tuple-element.31), channel_id=1, source_target_pairs={{0,2},{1,3},{2,4},{3,5},{4,6},{5,7},{8,10},{9,11},{10,12},{11,13},... | collective-permute-start | bytes 184328 | tf_op jit(solution)/shard_map/ppermute | solution.py:379
  43.4 11.8 %collective-permute-start.5 = (bf16[15,16,128]{2,1,0:T(8,128)(2,1)}, bf16[15,16,128]{2,1,0:T(8,128)(2,1)S(1)}, u32[]{:S(2)}, u32[]{:S(2)}) collective-permute-start(bf16[15,16,128]{2,1,0:T(8,128)(2,1)} %get-tuple-element.32), channel_id=1, source_target_pairs={{2,0},{3,1},{4,2},{5,3},{6,4},{7,5},{10,8},{11,9},{12,10},{13,11},... | collective-permute-start | bytes 184328 | tf_op jit(solution)/shard_map/ppermute | solution.py:379
  55.1 0.6 %copy-start.4 = (bf16[15,16,128]{2,1,0:T(8,128)(2,1)}, bf16[15,16,128]{2,1,0:T(8,128)(2,1)S(1)}, u32[]{:S(2)}) copy-start(bf16[15,16,128]{2,1,0:T(8,128)(2,1)S(1)} %collective-permute-done.4.before) | copy-start | bytes 184324
  55.2 0.6 %copy-start.5 = (bf16[15,16,128]{2,1,0:T(8,128)(2,1)}, bf16[15,16,128]{2,1,0:T(8,128)(2,1)S(1)}, u32[]{:S(2)}) copy-start(bf16[15,16,128]{2,1,0:T(8,128)(2,1)S(1)} %collective-permute-done.5.after) | copy-start | bytes 184324
where the time goes:
time: 61.3 us; the launch traced here: 60.8 us
  Pallas kernels  37.6 us (61%)
  starting transfers between devices  18.1 us (30%)
  local copies, waits for them, and re-layouts  4.98 us (8%)
    pallas_call x5, Pallas kernels, call(): pl.pallas_call(kernel, out_shape=[jax.ShapeDtypeStruct(s, d) for s, d in...  22.7 us
    ppermute x6, starting transfers between devices, exchange(): return (lax.ppermute(up, axis, forward), lax.ppermute(down, axis, backward))  18.1 us
    pallas_call x3, Pallas kernels, bands(): pl.pallas_call(functools.partial(bands_kernel, depth, groups), out_shape=...  14.9 us
    unnamed x16, local copies, waits for them, and re-layouts  2.11 us
    pad x3, local copies, waits for them, and re-layouts, bands(): flat = jnp.pad(stencil.reshape(9, 81), ((0, 7), (0, HALF - 81)))  1.81 us
  transfers between devices with their start and end apart: 6, of which 0 were waited for; matrix products, arithmetic and copies ran while one was open for 5% of the time, Pallas kernels for 40%

commit v1 on v0

--- a/solution.py
+++ b/solution.py
@@ -2,7 +2,6 @@
 
 import jax
 import jax.numpy as jnp
-import numpy as np
 from jax import lax
 from jax.experimental import pallas as pl
 from jax.experimental.pallas import tpu as pltpu
@@ -12,7 +11,7 @@
 BF16 = jnp.bfloat16
 WIDE = 256
 HALF = 128
-VMEM_LIMIT = 56 * 1024 * 1024
+VMEM_LIMIT = 14 * 1024 * 1024
 
 
 def split_pair(v):
@@ -81,7 +80,20 @@
     return ((at >= 0) | (index > 0)) & ((at < cells) | (index < count - 1))
 
 
-def spread_kernel(counts, charges, up, down, mid_own, coarse_own, even_pad, odd_pad, crs):
+def spread_kernel(counts, *refs):
+    outside, (up, down, mid_own, coarse_own) = refs[0:4], refs[4:8]
+    lines, (even_pad, odd_pad, crs, charges), raws, sems = refs[8:11], refs[11:15], refs[15:18], refs[18]
+    copies = [
+        pltpu.make_async_copy(source, target, sems.at[i])
+        for i, (source, target) in enumerate(zip(outside, (charges,) + raws))
+    ]
+    for copy in copies:
+        copy.start()
+    even_pad[...] = jnp.zeros_like(even_pad)
+    odd_pad[...] = jnp.zeros_like(odd_pad)
+    for line in lines:
+        line[...] = jnp.zeros_like(line)
+    copies[0].wait()
     gx, gy = lax.axis_index("gx"), lax.axis_index("gy")
     nx, ny = counts
     cells_x, cells_y, cells_z = charges.shape
@@ -91,8 +103,6 @@
     even, odd = pairs_of_rows(charges[...])
     mid = restrict_rows(even, 0, odd, 0, -1, mx + 3)
     mid = dot_last(mid, transfer_matrix(cells_z, mz, False))
-    even_pad[...] = jnp.zeros_like(even_pad)
-    odd_pad[...] = jnp.zeros_like(odd_pad)
     mid_own[...] = mid
     even_pad[:, 8 : 8 + my] = mid_own[:, pl.ds(0, my, stride=2), :]
     odd_pad[:, 8 : 8 + my] = mid_own[:, pl.ds(1, my, stride=2), :]
@@ -118,14 +128,39 @@
     coarse_own[...] = coarse
     for out, fine_at, mid_at, coarse_at in ((up, cells_x - 4, mx - 4, cx - 4), (down, 0, 0, 0)):
         out[0:4] = charges[fine_at : fine_at + 4].astype(BF16)
-        out[4:11] = pair_lanes(mid[mid_at : mid_at + 7]).astype(BF16)
-        packed = pair_lanes(coarse[coarse_at : coarse_at + 9])
-        blank = jnp.zeros(packed.shape[:-1] + (out.shape[2] - packed.shape[2],), F32)
-        out[11:20] = jnp.concatenate([packed, blank], axis=-1).astype(BF16)
+        out[4:8] = two_halves(mid[mid_at : mid_at + 7]).astype(BF16)
+        out[8:13] = two_halves(pair_lanes(coarse[coarse_at : coarse_at + 9])).astype(BF16)
+    for copy, line, raw in zip(copies[1:], lines, raws):
+        copy.wait()
+        line[:, 0:9, 0:9] = raw[...].astype(F32)
+
+
+def two_halves(v):
+    half = (v.shape[0] + 1) // 2
+    return jnp.concatenate([v[:half], rows_at(v, 0, half, half)], axis=-1)
 
 
 def unpair(v, width):
     return v[..., :width] + v[..., width : 2 * width]
+
+
+def from_halves(v, count):
+    lanes = v.shape[-1] // 2
+    return jnp.concatenate([v[..., :lanes], v[: count - v.shape[0], :, lanes:]], axis=0)
+
+
+def fine_parts(rows):
+    q = rows // 4
+    return [(slice(0, q), q * r, q * r + q, 4 * r, 0) for r in range(4)]
+
+
+def quarters(rows, at, lanes):
+    q = -(-rows // 4)
+    parts = []
+    for r in range(4):
+        first, last = q * r, min(q * r + q, rows)
+        parts.append((slice(at, at + last - first), first, last, 8 * (r // 2), lanes * (r % 2)))
+    return parts
 
 
 def join_x_kernel(charges, mid_own, coarse_own, before, after, fine_x, mid_x, coarse_x, up, down, buf):
@@ -136,14 +171,14 @@
     fine_x[0:4] = before[0:4].astype(F32)
     fine_x[4 : 4 + cells_x] = charges[...].astype(BF16).astype(F32)
     fine_x[4 + cells_x : 8 + cells_x] = after[0:4].astype(F32)
-    low, high = before[4:11].astype(F32), after[4:11].astype(F32)
+    low, high = (from_halves(m[4:8].astype(F32), 7) for m in (before, after))
     mid = (
         rows_at(mid_own[...], -1, -5, mx + 11)
-        + rows_at(unpair(low, mz), -5, -5, mx + 11)
-        + rows_at(unpair(high, mz), mx - 1, -5, mx + 11)
+        + rows_at(low, -5, -5, mx + 11)
+        + rows_at(high, mx - 1, -5, mx + 11)
     )
     mid_x[...] = mid
-    low, high = before[11:20].astype(F32), after[11:20].astype(F32)
+    low, high = (from_halves(m[8:13].astype(F32), 9) for m in (before, after))
     coarse = (
         rows_at(coarse_own[...], -2, -6, cx + 13)
         + rows_at(unpair(low, cz), -6, -6, cx + 13)
@@ -152,9 +187,13 @@
     coarse_x[...] = coarse
     buf[...] = jnp.zeros_like(buf)
     for out, fine_at, mid_at in ((up, cells_y - 4, my - 4), (down, 0, 0)):
-        buf[:, 0:4, :] = fine_x[:, fine_at : fine_at + 4, :]
-        buf[0 : mx + 11, 4:11, :] = pair_lanes(mid_x[:, mid_at : mid_at + 7, :])
-        buf[mx + 11 : mx + cx + 24, 4:13, 0 : 2 * cz] = pair_lanes(coarse_x[:, 0:9, :])
+        for part, first, last, top, left in fine_parts(cells_x + 8):
+            buf[part, top : top + 4, left:] = fine_x[first:last, fine_at : fine_at + 4, :]
+        at = (cells_x + 8) // 4
+        for part, first, last, top, left in quarters(mx + 11, at, mz):
+            buf[part, top : top + 7, left : left + mz] = mid_x[first:last, mid_at : mid_at + 7, :]
+        at += -(-(mx + 11) // 4)
+        buf[at:, 0:9, :] = two_halves(pair_lanes(coarse_x[:, 0:9, :]))
         out[...] = buf[...].astype(BF16)
 
 
@@ -167,25 +206,29 @@
     mz, cz = mid_x.shape[2], coarse_x.shape[2]
     low[...] = before[...].astype(F32)
     high[...] = after[...].astype(F32)
-    fine_xy[:, 0:4, :] = low[:, 0:4, :]
     fine_xy[:, 4 : 4 + cells_y, :] = fine_x[...]
-    fine_xy[:, 4 + cells_y : 8 + cells_y, :] = high[:, 0:4, :]
+    for part, first, last, top, _ in fine_parts(fine_x.shape[0]):
+        fine_xy[first:last, 0:4, :] = low[part, top : top + 4, :]
+        fine_xy[first:last, 4 + cells_y : 8 + cells_y, :] = high[part, top : top + 4, :]
     mid_xy[...] = jnp.zeros_like(mid_xy)
     mid_xy[:, 4 : 7 + my, :] = mid_x[:, 0 : my + 3, :]
-    mid_xy[:, 0:7, :] += unpair(low[0:rows_m, 4:11, :], mz)
-    mid_xy[:, 4 + my : 11 + my, :] += unpair(high[0:rows_m, 4:11, :], mz)
-    from_low = unpair(low[rows_m : rows_m + rows_c, 4:13, :], cz)
-    from_high = unpair(high[rows_m : rows_m + rows_c, 4:13, :], cz)
+    at = fine_x.shape[0] // 4
+    for part, first, last, top, left in quarters(rows_m, at, mz):
+        mid_xy[first:last, 0:7, :] += low[part, top : top + 7, left : left + mz]
+        mid_xy[first:last, 4 + my : 11 + my, :] += high[part, top : top + 7, left : left + mz]
+    at += -(-rows_m // 4)
+    from_low = unpair(from_halves(low[at:, 0:9, :], rows_c), cz)
+    from_high = unpair(from_halves(high[at:, 0:9, :], rows_c), cz)
     side[...] = jnp.zeros_like(side)
     side[:, 4 : 9 + cy, :] = coarse_x[:, 0 : cy + 5, :]
     coarse_xy[...] = side[...]
     coarse_xy[:, 0:9, :] += from_low
-    half = up.shape[0]
     buf[...] = jnp.zeros_like(buf)
 
     def pack(rows, out):
-        buf[:, 0:5, 0 : 2 * cz] = pair_lanes(rows[0:half])
-        buf[0 : rows_c - half, 8:13, 0 : 2 * cz] = pair_lanes(rows[half:rows_c])
+        rows = pair_lanes(rows)
+        for part, first, last, top, left in quarters(rows_c, 0, 2 * cz):
+            buf[part, top : top + 5, left : left + 2 * cz] = rows[first:last]
         out[...] = buf[...].astype(BF16)
 
     pack(coarse_xy[:, 4 + cy : 9 + cy, :], up)
@@ -194,75 +237,73 @@
     pack(side[:, 4:9, :], down)
 
 
-def base_plan(depth, groups):
-    per = HALF // depth
-    offsets = range(-1, 2 * groups)
-    plan = np.full((len(offsets), 2, HALF), -1, np.int64)
-    for i, offset in enumerate(offsets):
-        for sign in (0, 1):
-            for t in range(HALF):
-                d = t - HALF * sign
-                j = int(np.floor(d / depth + 0.5))
-                e = d - depth * j
-                tap = per * offset - j
-                if abs(e) <= 4 and 0 <= tap <= 8 and abs(j) < per:
-                    plan[i, sign, t] = tap * 9 + 4 - e
-    return plan
-
-
-def one_hot_of(plan):
-    flat = plan.reshape(-1)
-    return (np.arange(HALF)[:, None] == flat[None, :]).astype(jnp.bfloat16)
-
-
-def bands_kernel(depth, groups, stencil, one_hot, out, bases):
-    per = HALF // depth
-    values = jnp.dot(stencil[...], one_hot[...], preferred_element_type=F32)
-    for dx in range(9):
-        bases[dx] = jnp.broadcast_to(values[dx : dx + 1], bases.shape[1:])
-    row = lax.broadcasted_iota(jnp.int32, (HALF, HALF), 0)
-    col = lax.broadcasted_iota(jnp.int32, (HALF, HALF), 1)
-    apart = lax.rem(row, depth) - lax.rem(col, depth)
-    band = (apart <= 4) & (apart >= -4)
-    right = band & (col >= row)
-    left = band & (col < row)
-
-    def one_dx(dx, carry):
-        def rolled(i, sign):
-            at = (2 * i + sign) * HALF
-            line = bases[dx, :, at : at + HALF]
-            full = jnp.concatenate([line] * (HALF // 8), axis=0)
-            return pltpu.roll(full, 0, 1, stride=1, stride_axis=0)
-
-        for i in range(2 * groups + 1):
-            offset = i - 1
-            block = jnp.where(right, rolled(i, 0), jnp.where(left, rolled(i, 1), 0.0)).astype(BF16)
-            for group in range(groups):
-                for a in (0, 1):
-                    b = 2 * group + a - offset
-                    if b in (0, 1):
-                        out[
-                            dx,
-                            group * WIDE + a * HALF : group * WIDE + (a + 1) * HALF,
-                            b * HALF : (b + 1) * HALF,
-                        ] = block
-        return carry
-
-    lax.fori_loop(0, 9, one_dx, 0)
-
-
-def bands(stencil, depth, groups):
-    one_hot = jnp.asarray(one_hot_of(base_plan(depth, groups)))
-    flat = jnp.pad(stencil.reshape(9, 81), ((0, 7), (0, HALF - 81)))
-    return pl.pallas_call(
-        functools.partial(bands_kernel, depth, groups),
-        out_shape=jax.ShapeDtypeStruct((9, groups * WIDE, WIDE), BF16),
-        in_specs=[whole(), whole()],
-        out_specs=whole(),
-        scratch_shapes=[pltpu.VMEM((9, 8, one_hot.shape[1]), F32)],
-        compiler_params=pltpu.CompilerParams(vmem_limit_bytes=VMEM_LIMIT),
-        cost_estimate=pl.CostEstimate(flops=2 * 10**9, bytes_accessed=4 * 10**6, transcendentals=0),
-    )(flat, one_hot)
+def bands_kernel(levels, *refs):
+    n = len(levels)
+    (turned,) = refs[2 * n :]
+    tap = lax.broadcasted_iota(jnp.int32, (HALF, HALF), 0)
+    place = lax.broadcasted_iota(jnp.int32, (HALF, HALF), 1)
+    reverse = ((tap <= 8) & (place == jnp.where(tap <= 4, 4 - tap, HALF + 4 - tap))).astype(F32).astype(BF16)
+    for (depth, groups), lines, out in zip(levels, refs[:n], refs[n : 2 * n]):
+        per = HALF // depth
+        flat = lines[...].reshape(9 * 16, HALF).astype(BF16)
+        values = jnp.dot(flat, reverse, preferred_element_type=F32)
+        if per == 1:
+            turned[0] = pltpu.roll(values.reshape(9, 16, HALF), 0, 2, stride=16, stride_axis=1)
+            turned[1, :, 0:8, :] = jnp.broadcast_to(jnp.sum(turned[0, :, 0:8, :], axis=1, keepdims=True), (9, 8, HALF))
+        else:
+            for j in range(per):
+                turned[j] = (pltpu.roll(values, j * depth, 1) if j else values).reshape(9, 16, HALF)
+        apart = lax.rem(tap, depth) - lax.rem(place, depth)
+        band = (apart <= 4) & (apart >= -4)
+
+        def one_dx(dx, carry, per=per, depth=depth, groups=groups, out=out, band=band):
+            def turn(line, by):
+                return pltpu.roll(jnp.broadcast_to(line, (8, HALF)), by, 1, stride=1, stride_axis=0)
+
+            def line_at(first):
+                parts = [turned[j, dx, first - j : first - j + 1, :] for j in range(per) if 0 <= first - j <= 8]
+                return functools.reduce(jnp.add, parts) if parts else None
+
+            if per == 1:
+                joint = [turn(turned[1, dx, 0:1, :], 8 * r) for r in range(16)]
+                last = [turn(turned[0, dx, 8:9, :], 8 * r) for r in range(16)]
+
+            def rows_of(offset):
+                for a in range(per):
+                    line = None if per == 1 else line_at(per * offset + a)
+                    for g in range(depth // 8):
+                        if per == 1:
+                            full = last[g] if offset == 8 else joint[(g - 2 * offset) % 16]
+                        else:
+                            full = jnp.zeros((8, HALF), F32) if line is None else turn(line, 8 * g)
+                        at = a * depth + 8 * g
+                        yield jnp.where(band[at : at + 8], full, 0.0)
+
+            zero = jnp.zeros((HALF, HALF), BF16)
+            for offset in range(-1, 2 * groups):
+                block = zero
+                if 0 <= per * offset <= 8:
+                    block = jnp.concatenate(list(rows_of(offset)), axis=0).astype(BF16)
+                for group in range(groups):
+                    for a in (0, 1):
+                        b = 2 * group + a - offset
+                        if b in (0, 1):
+                            at = group * WIDE + a * HALF
+                            out[dx, at : at + HALF, b * HALF : (b + 1) * HALF] = block
+            return carry
+
+        lax.fori_loop(0, 9, one_dx, 0)
+
+
+def bands(stencils, levels):
+    most = max([2] + [HALF // depth for depth, _ in levels])
+    return call(
+        functools.partial(bands_kernel, levels),
+        [((9, groups * WIDE, WIDE), BF16) for _, groups in levels],
+        list(stencils),
+        [((most, 9, 16, HALF), F32)],
+        flops=10**9,
+    )
 
 
 def gather_rows(field, rows, per, groups, depth, lhs):
@@ -275,6 +316,18 @@
                 lhs[parity, 0 : count * 8, lane : lane + depth] = part.reshape(count * 8, depth).astype(BF16)
 
 
+def gather_staged(field, rows, per, groups, depth, stage, lhs):
+    count = field.shape[1] // per
+    stage[...] = jnp.zeros_like(stage)
+    for a in range(per):
+        stage[:, 0:count, a * depth : (a + 1) * depth] = field[:, pl.ds(a, count, stride=per), :]
+    for parity in (0, 1):
+        n = (rows - parity) * 8
+        for group in range(groups):
+            part = stage[parity:rows, group : group + 8, :].reshape(n, WIDE)
+            lhs[parity, 0:n, group * WIDE : (group + 1) * WIDE] = part.astype(BF16)
+
+
 def convolve(lhs, weights, out_rows, acc):
     n = out_rows * 8
     for dx in range(9):
@@ -283,14 +336,13 @@
         acc[...] = part if dx == 0 else acc[...] + part
 
 
-def conv_kernel(fine_xy, mid_xy, fine_w, mid_w, fine_acc, mid_acc, mid_pad, fine_lhs, mid_lhs):
+def conv_kernel(fine_xy, mid_xy, fine_w, mid_w, fine_acc, mid_acc, stage, fine_lhs, mid_lhs):
     rows = fine_xy.shape[0]
     gather_rows(fine_xy, rows, 2, 5, fine_xy.shape[2], fine_lhs)
     convolve(fine_lhs, fine_w, rows - 8, fine_acc)
-    mid_pad[...] = jnp.zeros_like(mid_pad)
-    mid_pad[:, 0 : mid_xy.shape[1], :] = mid_xy[...]
-    gather_rows(mid_pad, mid_pad.shape[0], 4, 3, mid_xy.shape[2], mid_lhs)
-    convolve(mid_lhs, mid_w, mid_pad.shape[0] - 8, mid_acc)
+    rows = mid_xy.shape[0]
+    gather_staged(mid_xy, rows, 4, 3, mid_xy.shape[2], stage, mid_lhs)
+    convolve(mid_lhs, mid_w, rows - 8, mid_acc)
 
 
 def prolong_odd(a, b, c, d):
@@ -299,7 +351,7 @@
 
 def finish_kernel(
     counts, coarse_xy, before, after, coarse_w, fine_acc, mid_acc, out,
-    crs_pad, crs_lhs, crs_acc, msg, crs_pot, wide, mid_tot,
+    crs_pad, stage, crs_lhs, crs_acc, msg, crs_pot, wide, mid_tot,
 ):
     gx, gy = lax.axis_index("gx"), lax.axis_index("gy")
     nx, ny = counts
@@ -307,14 +359,12 @@
     cells_x, cells_y, cells_z = out.shape
     mx, my, mz = cells_x // 2, cells_y // 2, cells_z // 2
     cx, cy = cells_x // 4, cells_y // 4
-    half = before.shape[0]
-    crs_pad[...] = jnp.zeros_like(crs_pad)
-    crs_pad[:, 0 : coarse_xy.shape[1], :] = coarse_xy[...]
+    crs_pad[...] = coarse_xy[...]
     for source, at in ((before, 0), (after, cy + 8)):
         msg[...] = source[...].astype(F32)
-        crs_pad[0:half, at : at + 5, :] += unpair(msg[:, 0:5, :], cz)
-        crs_pad[half:rows_c, at : at + 5, :] += unpair(msg[0 : rows_c - half, 8:13, :], cz)
-    gather_rows(crs_pad, rows_c, 8, 2, cz, crs_lhs)
+        for part, first, last, top, left in quarters(rows_c, 0, 2 * cz):
+            crs_pad[first:last, at : at + 5, :] += unpair(msg[part, top : top + 5, left : left + 2 * cz], cz)
+    gather_staged(crs_pad, rows_c, 8, 2, cz, stage, crs_lhs)
     convolve(crs_lhs, coarse_w, rows_c - 8, crs_acc)
     rows = rows_c - 8
     pot = crs_acc[...].reshape(rows, 8, WIDE)
@@ -361,16 +411,21 @@
     return pl.BlockSpec(memory_space=pltpu.VMEM)
 
 
-def call(kernel, outs, ins, scratch, flops=10**8):
+def call(kernel, outs, ins, scratch, flops=10**8, vmem_out=True, after=(), space=pltpu.VMEM, sems=0, limit=VMEM_LIMIT):
+    n = len(ins)
+
+    def body(*refs):
+        kernel(*refs[:n], *refs[n + len(after) :])
+
     return pl.pallas_call(
-        kernel,
-        out_shape=[jax.ShapeDtypeStruct(s, d) for s, d in outs],
-        in_specs=[whole()] * len(ins),
+        body,
+        out_shape=[pltpu.VMEM(s, d) for s, d in outs] if vmem_out else [jax.ShapeDtypeStruct(s, d) for s, d in outs],
+        in_specs=[pl.BlockSpec(memory_space=space)] * n + [pl.BlockSpec(memory_space=pl.ANY)] * len(after),
         out_specs=[whole()] * len(outs),
-        scratch_shapes=[pltpu.VMEM(s, d) for s, d in scratch],
-        compiler_params=pltpu.CompilerParams(vmem_limit_bytes=VMEM_LIMIT),
+        scratch_shapes=[pltpu.VMEM(s, d) for s, d in scratch] + [pltpu.SemaphoreType.DMA((sems,))] * (sems > 0),
+        compiler_params=pltpu.CompilerParams(vmem_limit_bytes=limit),
         cost_estimate=pl.CostEstimate(flops=flops, bytes_accessed=10**6, transcendentals=0),
-    )(*ins)
+    )(*ins, *after)
 
 
 def exchange(up, down, axis, step, size):
@@ -384,18 +439,28 @@
     cells_x, cells_y, cells_z = charges.shape
     mx, mz, cx, cz = cells_x // 2, cells_z // 2, cells_x // 4, cells_z // 4
     frame = cells_y
-    fine_w = bands(kernel_fine, cells_z, 5)
-    mid_w = bands(kernel_mid, mz, 3)
-    coarse_w = bands(kernel_coarse, cz, 2)
-    message = ((20, frame, cells_z), BF16)
-    up, down, mid_own, coarse_own = call(
+    message = ((13, frame, cells_z), BF16)
+    line = ((9, 16, HALF), F32)
+    up, down, mid_own, coarse_own, *lines = call(
         functools.partial(spread_kernel, counts),
-        [message, message, ((mx + 3, frame, mz), F32), ((cx + 5, frame, cz), F32)],
-        [charges],
-        [((mx + 3, frame + 24, mz), F32), ((mx + 3, frame + 24, mz), F32), ((cx + 5, frame, mz), F32)],
+        [message, message, ((mx + 3, frame, mz), F32), ((cx + 5, frame, cz), F32), line, line, line],
+        [charges, kernel_fine, kernel_mid, kernel_coarse],
+        [
+            ((mx + 3, frame + 24, mz), F32),
+            ((mx + 3, frame + 24, mz), F32),
+            ((cx + 5, frame, mz), F32),
+            (charges.shape, F32),
+        ]
+        + [((9, 9, 9), BF16)] * 3,
+        space=pltpu.HBM,
+        sems=4,
+        limit=60 * 1024 * 1024,
     )
     before, after = exchange(up, down, "gx", 1, nx)
-    message = ((cells_x + 8, frame, cells_z), BF16)
+    levels = ((cells_z, 5), (mz, 3), (cz, 2))
+    fine_w, mid_w, coarse_w = bands(lines, levels)
+    rows = (cells_x + 8) // 4 + (mx + 14) // 4 + (cx + 14) // 2
+    message = ((rows, frame, cells_z), BF16)
     fine_x, mid_x, coarse_x, up, down = call(
         join_x_kernel,
         [
@@ -406,10 +471,11 @@
             message,
         ],
         [charges, mid_own, coarse_own, before, after],
-        [((cells_x + 8, frame, cells_z), F32)],
+        [((rows, frame, cells_z), F32)],
+        after=(fine_w,),
     )
     before, after = exchange(up, down, "gy", 1, ny)
-    half = (cx + 14) // 2
+    half = (cx + 16) // 4
     message = ((half, frame, cells_z), BF16)
     fine_xy, mid_xy, coarse_xy, up, down = call(
         join_y_kernel,
@@ -422,8 +488,8 @@
         ],
         [fine_x, mid_x, coarse_x, before, after],
         [
-            ((cells_x + 8, frame, cells_z), F32),
-            ((cells_x + 8, frame, cells_z), F32),
+            ((rows, frame, cells_z), F32),
+            ((rows, frame, cells_z), F32),
             ((half, frame, cells_z), F32),
             ((cx + 13, frame + 8, cz), F32),
         ],
@@ -434,7 +500,7 @@
         [((cells_x * 8, WIDE), F32), (((mx + 3) * 8, WIDE), F32)],
         [fine_xy, mid_xy, fine_w, mid_w],
         [
-            ((mx + 11, frame + 32, mz), F32),
+            ((mx + 11, 16, WIDE), F32),
             ((2, (cells_x + 8) * 8, 5 * WIDE), BF16),
             ((2, (mx + 12) * 8, 3 * WIDE), BF16),
         ],
@@ -445,7 +511,8 @@
         [(charges.shape, F32)],
         [coarse_xy, before, after, coarse_w, fine_acc, mid_acc],
         [
-            ((cx + 13, 80, cz), F32),
+            ((cx + 13, frame + 8, cz), F32),
+            ((cx + 13, 16, WIDE), F32),
             ((2, (cx + 14) * 8, 2 * WIDE), BF16),
             (((cx + 5) * 8, WIDE), F32),
             ((half, frame, cells_z), F32),
@@ -453,6 +520,7 @@
             ((cx + 2, 2, 16, cz), F32),
             ((mx + 4, 16, mz), F32),
         ],
+        vmem_out=False,
     )
     return out
 

time: 61.3 us -> 37.4 us (0.61)
  the two profiles are of different devices: /device:TPU:20 before, /device:TPU:21 now
where the time goes in v1:
time: 37.4 us; the launch traced here: 37.2 us
  starting transfers between devices  17.7 us (47%)
  Pallas kernels  14.4 us (39%)
  waiting for transfers between devices  4.9 us (13%)
    ppermute x6, starting transfers between devices, exchange(): return (lax.ppermute(up, axis, forward), lax.ppermute(down, axis, backward))  17.7 us
    pallas_call x6, Pallas kernels, call(): pl.pallas_call(body, out_shape=[pltpu.VMEM(s, d) for s, d in outs] if vme...  14.4 us
    ppermute x6, waiting for transfers between devices, exchange(): return (lax.ppermute(up, axis, forward), lax.ppermute(down, axis, backward))  4.9 us
  transfers between devices with their start and end apart: 6, of which 2 were waited for; matrix products, arithmetic and copies ran while one was open for 0% of the time, Pallas kernels for 23%

profile of v1, /device:TPU:21, one launch (start us, length us, event | category | flops | bytes accessed | tf_op | source)
XLA Modules:
  0.0 37.2 jit_solution(3840409566768327738)
XLA Ops:
  0.0 0.0 copy-start
  0.0 2.1 %shard_map.46 = (bf16[13,16,128]{2,1,0:T(8,128)(2,1)S(1)}, bf16[13,16,128]{2,1,0:T(8,128)(2,1)S(1)}, f32[35,16,64]{2,1,0:T(8,128)S(1)}, f32[21,16,32]{2,1,0:T(8,...) custom-call(f32[64,16,128]{2,1,0:T(8,128)} %refs_0_.3, ...), custom_call_target="tpu_custom_call" | custom-call | flops 100000000 | bytes 1000000 | tf_op jit(solution)/shard_map/pallas_call | solution.py:420
  2.1 3.1 %collective-permute-start = (bf16[13,16,128]{2,1,0:T(8,128)(2,1)S(1)}, bf16[13,16,128]{2,1,0:T(8,128)(2,1)S(1)}, u32[]{:S(2)}, u32[]{:S(2)}) collective-permute-start(bf16[13,16,128]{2,1,0:T(8,128)(2,1)S(1)} %get-tuple-element.29), channel_id=1, source_target_pairs={{0,8},{8,16},{16,24},{1,9},{9,17},{17,25},{2,10},{10,18},{18,26},{... | collective-permute-start | bytes 159752 | tf_op jit(solution)/shard_map/ppermute | solution.py:434
  5.2 3.1 %collective-permute-start.1 = (bf16[13,16,128]{2,1,0:T(8,128)(2,1)S(1)}, bf16[13,16,128]{2,1,0:T(8,128)(2,1)S(1)}, u32[]{:S(2)}, u32[]{:S(2)}) collective-permute-start(bf16[13,16,128]{2,1,0:T(8,128)(2,1)S(1)} %get-tuple-element.30), channel_id=1, source_target_pairs={{8,0},{16,8},{24,16},{9,1},{17,9},{25,17},{10,2},{18,10},{26,18},{... | collective-permute-start | bytes 159752 | tf_op jit(solution)/shard_map/ppermute | solution.py:434
  8.3 4.0 %shard_map.47 = (bf16[9,1280,256]{2,1,0:T(8,128)(2,1)S(1)}, bf16[9,768,256]{2,1,0:T(8,128)(2,1)S(1)}, bf16[9,512,256]{2,1,0:T(8,128)(2,1)S(1)}) custom-call(f32[9,16,128]{2,1,0:T(8,128)S(1)} %get-tuple-element.31.refs_0_, f32[9,16,128]{2,1,0:T(8,128)S(1)} %get-tuple-element.32.refs_1_, f32[9,16,128]{2,1,0:T(8,128)S(1)} %get-tuple-element.33.refs_2_), custom_call_target="tpu_custom_call" | custom-call | flops 1000000000 | bytes 1000000 | tf_op jit(solution)/shard_map/pallas_call | solution.py:420
  12.3 0.0 collective-permute-done.refs_3_
  12.3 0.0 collective-permute-done.1.refs_4_
  12.3 0.0 copy-done
  12.3 0.5 %shard_map.48 = (f32[72,16,128]{2,1,0:T(8,128)S(1)}, f32[43,16,64]{2,1,0:T(8,128)S(1)}, f32[29,16,32]{2,1,0:T(8,128)S(1)}, bf16[44,16,128]{2,1,0:T(8,128)(2,1)S(1)}, bf16[44,16,128]{2,1,0:T(8,128)(2,1)S(1)}) custom-call(f32[64,16,128]{2,1,0:T(8,128)S(1)} %copy-done, f32[35,16,64]{2,1,0:T(8,128)S(1)} %get-tuple-element.27.refs_1_, ...), custom_call_target="tpu_custom_call" | custom-call | flops 100000000 | bytes 1000000 | tf_op jit(solution)/shard_map/pallas_call | solution.py:420
  12.8 4.3 %collective-permute-start.2 = (bf16[44,16,128]{2,1,0:T(8,128)(2,1)S(1)}, bf16[44,16,128]{2,1,0:T(8,128)(2,1)S(1)}, u32[]{:S(2)}, u32[]{:S(2)}) collective-permute-start(bf16[44,16,128]{2,1,0:T(8,128)(2,1)S(1)} %get-tuple-element.38), channel_id=1, source_target_pairs={{0,1},{1,2},{2,3},{3,4},{4,5},{5,6},{6,7},{8,9},{9,10},{10,11},{11... | collective-permute-start | bytes 540680 | tf_op jit(solution)/shard_map/ppermute | solution.py:434
  17.1 1.9 %collective-permute-start.3 = (bf16[44,16,128]{2,1,0:T(8,128)(2,1)S(1)}, bf16[44,16,128]{2,1,0:T(8,128)(2,1)S(1)}, u32[]{:S(2)}, u32[]{:S(2)}) collective-permute-start(bf16[44,16,128]{2,1,0:T(8,128)(2,1)S(1)} %get-tuple-element.39), channel_id=1, source_target_pairs={{1,0},{2,1},{3,2},{4,3},{5,4},{6,5},{7,6},{9,8},{10,9},{11,10},{12... | collective-permute-start | bytes 540680 | tf_op jit(solution)/shard_map/ppermute | solution.py:434
  19.1 0.5 %collective-permute-done.2.refs_3_ = bf16[44,16,128]{2,1,0:T(8,128)(2,1)S(1)} collective-permute-done((bf16[44,16,128]{2,1,0:T(8,128)(2,1)S(1)}, bf16[44,16,128]{2,1,0:T(8,128)(2,1)S(1)}, u32[]{:S(2)}, u32[]{:S(2)}) %collective-permute-start.2) | collective-permute-done | bytes 180256 | tf_op jit(solution)/shard_map/ppermute | solution.py:434
  19.5 4.4 %collective-permute-done.3.refs_4_ = bf16[44,16,128]{2,1,0:T(8,128)(2,1)S(1)} collective-permute-done((bf16[44,16,128]{2,1,0:T(8,128)(2,1)S(1)}, bf16[44,16,128]{2,1,0:T(8,128)(2,1)S(1)}, u32[]{:S(2)}, u32[]{:S(2)}) %collective-permute-start.3) | collective-permute-done | bytes 180256 | tf_op jit(solution)/shard_map/ppermute | solution.py:434
  23.9 0.6 %shard_map.49 = (f32[72,24,128]{2,1,0:T(8,128)S(1)}, f32[43,24,64]{2,1,0:T(8,128)S(1)}, f32[29,24,32]{2,1,0:T(8,128)S(1)}, bf16[8,16,128]{2,1,0:T(8,128)(2,1)S(1)}, bf16[8,16,128]{2,1,0:T(8,128)(2,1)S(1)}) custom-call(f32[72,16,128]{2,1,0:T(8,128)S(1)} %get-tuple-element.35.refs_0_, f32[43,16,64]{2,1,0:T(8,128)S(1)} %get-tuple-element.36.refs_1_, ...), custom_call_target="tpu_custom_call" | custom-call | flops 100000000 | bytes 1000000 | tf_op jit(solution)/shard_map/pallas_call | solution.py:420
  24.5 1.9 %collective-permute-start.4 = (bf16[8,16,128]{2,1,0:T(8,128)(2,1)S(1)}, bf16[8,16,128]{2,1,0:T(8,128)(2,1)S(1)}, u32[]{:S(2)}, u32[]{:S(2)}) collective-permute-start(bf16[8,16,128]{2,1,0:T(8,128)(2,1)S(1)} %get-tuple-element.41), channel_id=1, source_target_pairs={{0,2},{1,3},{2,4},{3,5},{4,6},{5,7},{8,10},{9,11},{10,12},{11,13},... | collective-permute-start | bytes 98312 | tf_op jit(solution)/shard_map/ppermute | solution.py:434
  26.5 3.4 %collective-permute-start.5 = (bf16[8,16,128]{2,1,0:T(8,128)(2,1)S(1)}, bf16[8,16,128]{2,1,0:T(8,128)(2,1)S(1)}, u32[]{:S(2)}, u32[]{:S(2)}) collective-permute-start(bf16[8,16,128]{2,1,0:T(8,128)(2,1)S(1)} %get-tuple-element.42), channel_id=1, source_target_pairs={{2,0},{3,1},{4,2},{5,3},{6,4},{7,5},{10,8},{11,9},{12,10},{13,11},... | collective-permute-start | bytes 98312 | tf_op jit(solution)/shard_map/ppermute | solution.py:434
  29.8 4.4 %shard_map.50 = (f32[512,256]{1,0:T(8,128)S(1)}, f32[280,256]{1,0:T(8,128)S(1)}) custom-call(f32[72,24,128]{2,1,0:T(8,128)S(1)} %get-tuple-element.44.refs_0_, f32[43,24,64]{2,1,0:T(8,128)S(1)} %get-tuple-element.45.refs_1_, bf16[9,1280,256]{2,1,0:T(8,128)(2,1)S(1)} %get-tuple-element.34.refs_5_.refs_2_, bf16[9,768,256]{2,1,0:T(8,128)(2,1)S(1)} %get-tuple-element.46.refs_3_), custom_call_target="tpu_custom_call" | custom-call | flops 10000000000 | bytes 1000000 | tf_op jit(solution)/shard_map/pallas_call | solution.py:420
  34.3 0.0 collective-permute-done.4.refs_1_
  34.3 0.0 collective-permute-done.5.refs_2_
  34.3 2.8 %shard_map.51 = f32[64,16,128]{2,1,0:T(8,128)} custom-call(f32[29,24,32]{2,1,0:T(8,128)S(1)} %get-tuple-element.40.refs_0_, bf16[8,16,128]{2,1,0:T(8,128)(2,1)S(1)} %collective-permute-done.4.refs_1_, bf16[8,16,128]{2,1,0:T(8,128)(2,1)S(1)} %collective-permute-done.5.refs_2_, bf16[9,512,256]{2,1,0:T(8,128)(2,1)S(1)} %get-tuple-element.43.refs_3_, ...), custom_call_target="tpu_custom_call" | custom-call | flops 100000000 | bytes 1000000 | tf_op jit(solution)/shard_map/pallas_call | solution.py:420
Async XLA Ops:
  0.0 12.3 %copy-start = (f32[64,16,128]{2,1,0:T(8,128)S(1)}, f32[64,16,128]{2,1,0:T(8,128)}, u32[]{:S(2)}) copy-start(f32[64,16,128]{2,1,0:T(8,128)} %refs_0_.3) | copy-start | bytes 1572868
  2.1 10.2 %collective-permute-start = (bf16[13,16,128]{2,1,0:T(8,128)(2,1)S(1)}, bf16[13,16,128]{2,1,0:T(8,128)(2,1)S(1)}, u32[]{:S(2)}, u32[]{:S(2)}) collective-permute-start(bf16[13,16,128]{2,1,0:T(8,128)(2,1)S(1)} %get-tuple-element.29), channel_id=1, source_target_pairs={{0,8},{8,16},{16,24},{1,9},{9,17},{17,25},{2,10},{10,18},{18,26},{... | collective-permute-start | bytes 159752 | tf_op jit(solution)/shard_map/ppermute | solution.py:434
  5.2 7.1 %collective-permute-start.1 = (bf16[13,16,128]{2,1,0:T(8,128)(2,1)S(1)}, bf16[13,16,128]{2,1,0:T(8,128)(2,1)S(1)}, u32[]{:S(2)}, u32[]{:S(2)}) collective-permute-start(bf16[13,16,128]{2,1,0:T(8,128)(2,1)S(1)} %get-tuple-element.30), channel_id=1, source_target_pairs={{8,0},{16,8},{24,16},{9,1},{17,9},{25,17},{10,2},{18,10},{26,18},{... | collective-permute-start | bytes 159752 | tf_op jit(solution)/shard_map/ppermute | solution.py:434
  12.8 6.8 %collective-permute-start.2 = (bf16[44,16,128]{2,1,0:T(8,128)(2,1)S(1)}, bf16[44,16,128]{2,1,0:T(8,128)(2,1)S(1)}, u32[]{:S(2)}, u32[]{:S(2)}) collective-permute-start(bf16[44,16,128]{2,1,0:T(8,128)(2,1)S(1)} %get-tuple-element.38), channel_id=1, source_target_pairs={{0,1},{1,2},{2,3},{3,4},{4,5},{5,6},{6,7},{8,9},{9,10},{10,11},{11... | collective-permute-start | bytes 540680 | tf_op jit(solution)/shard_map/ppermute | solution.py:434
  17.1 6.8 %collective-permute-start.3 = (bf16[44,16,128]{2,1,0:T(8,128)(2,1)S(1)}, bf16[44,16,128]{2,1,0:T(8,128)(2,1)S(1)}, u32[]{:S(2)}, u32[]{:S(2)}) collective-permute-start(bf16[44,16,128]{2,1,0:T(8,128)(2,1)S(1)} %get-tuple-element.39), channel_id=1, source_target_pairs={{1,0},{2,1},{3,2},{4,3},{5,4},{6,5},{7,6},{9,8},{10,9},{11,10},{12... | collective-permute-start | bytes 540680 | tf_op jit(solution)/shard_map/ppermute | solution.py:434
  24.5 9.7 %collective-permute-start.4 = (bf16[8,16,128]{2,1,0:T(8,128)(2,1)S(1)}, bf16[8,16,128]{2,1,0:T(8,128)(2,1)S(1)}, u32[]{:S(2)}, u32[]{:S(2)}) collective-permute-start(bf16[8,16,128]{2,1,0:T(8,128)(2,1)S(1)} %get-tuple-element.41), channel_id=1, source_target_pairs={{0,2},{1,3},{2,4},{3,5},{4,6},{5,7},{8,10},{9,11},{10,12},{11,13},... | collective-permute-start | bytes 98312 | tf_op jit(solution)/shard_map/ppermute | solution.py:434
  26.5 7.8 %collective-permute-start.5 = (bf16[8,16,128]{2,1,0:T(8,128)(2,1)S(1)}, bf16[8,16,128]{2,1,0:T(8,128)(2,1)S(1)}, u32[]{:S(2)}, u32[]{:S(2)}) collective-permute-start(bf16[8,16,128]{2,1,0:T(8,128)(2,1)S(1)} %get-tuple-element.42), channel_id=1, source_target_pairs={{2,0},{3,1},{4,2},{5,3},{6,4},{7,5},{10,8},{11,9},{12,10},{13,11},... | collective-permute-start | bytes 98312 | tf_op jit(solution)/shard_map/ppermute | solution.py:434

commit v2 on v1

--- a/solution.py
+++ b/solution.py
@@ -81,8 +81,8 @@
 
 
 def spread_kernel(counts, *refs):
-    outside, (up, down, mid_own, coarse_own) = refs[0:4], refs[4:8]
-    lines, (even_pad, odd_pad, crs, charges), raws, sems = refs[8:11], refs[11:15], refs[15:18], refs[18]
+    outside, (message, fine_own, mid_own, coarse_own, lines) = refs[0:4], refs[4:9]
+    (even_pad, odd_pad, crs, charges), raws, sems = refs[9:13], refs[13:16], refs[16]
     copies = [
         pltpu.make_async_copy(source, target, sems.at[i])
         for i, (source, target) in enumerate(zip(outside, (charges,) + raws))
@@ -91,9 +91,9 @@
         copy.start()
     even_pad[...] = jnp.zeros_like(even_pad)
     odd_pad[...] = jnp.zeros_like(odd_pad)
-    for line in lines:
-        line[...] = jnp.zeros_like(line)
+    lines[...] = jnp.zeros_like(lines)
     copies[0].wait()
+    fine_own[...] = charges[...].astype(BF16)
     gx, gy = lax.axis_index("gx"), lax.axis_index("gy")
     nx, ny = counts
     cells_x, cells_y, cells_z = charges.shape
@@ -126,13 +126,15 @@
     keep = inside(coarse.shape, 0, -2, cx, gx, nx) & inside(coarse.shape, 1, -2, cy, gy, ny)
     coarse = jnp.where(keep, coarse, 0.0)
     coarse_own[...] = coarse
-    for out, fine_at, mid_at, coarse_at in ((up, cells_x - 4, mx - 4, cx - 4), (down, 0, 0, 0)):
+    after, before = jnp.minimum(gx + 1, nx - 1), jnp.maximum(gx - 1, 0)
+    for slot, fine_at, mid_at, coarse_at in ((after, cells_x - 4, mx - 4, cx - 4), (before, 0, 0, 0)):
+        out = message.at[slot]
         out[0:4] = charges[fine_at : fine_at + 4].astype(BF16)
         out[4:8] = two_halves(mid[mid_at : mid_at + 7]).astype(BF16)
         out[8:13] = two_halves(pair_lanes(coarse[coarse_at : coarse_at + 9])).astype(BF16)
-    for copy, line, raw in zip(copies[1:], lines, raws):
-        copy.wait()
-        line[:, 0:9, 0:9] = raw[...].astype(F32)
+    for i, raw in enumerate(raws):
+        copies[i + 1].wait()
+        lines[9 * i : 9 * i + 9, 0:9, 0:9] = raw[...].astype(F32)
 
 
 def two_halves(v):
@@ -163,22 +165,30 @@
     return parts
 
 
-def join_x_kernel(charges, mid_own, coarse_own, before, after, fine_x, mid_x, coarse_x, up, down, buf):
+def join_x_kernel(nx, charges, mid_own, coarse_own, lines, message, fine_x, mid_x, coarse_x, lines_x, first_out, second_out, buf):
+    gx = lax.axis_index("gx")
+    lines_x[...] = lines[...]
+    before = jnp.where(gx > 0, message[jnp.maximum(gx - 1, 0)].astype(F32), 0.0)
+    after = jnp.where(gx < nx - 1, message[jnp.minimum(gx + 1, nx - 1)].astype(F32), 0.0)
     cells_x, cells_y, _ = charges.shape
     mx, cx = cells_x // 2, cells_x // 4
     mz, cz = mid_own.shape[2], coarse_own.shape[2]
     my = cells_y // 2
-    fine_x[0:4] = before[0:4].astype(F32)
-    fine_x[4 : 4 + cells_x] = charges[...].astype(BF16).astype(F32)
-    fine_x[4 + cells_x : 8 + cells_x] = after[0:4].astype(F32)
-    low, high = (from_halves(m[4:8].astype(F32), 7) for m in (before, after))
+    rows_x = cells_x + 8
+    own = slice(4, 4 + cells_y)
+    for edge in (0, 4 + cells_y):
+        fine_x[:, edge : edge + 4, :] = jnp.zeros((rows_x, 4, charges.shape[2]), F32)
+    fine_x[0:4, own, :] = before[0:4]
+    fine_x[4 : 4 + cells_x, own, :] = charges[...].astype(F32)
+    fine_x[4 + cells_x : rows_x, own, :] = after[0:4]
+    low, high = (from_halves(m[4:8], 7) for m in (before, after))
     mid = (
         rows_at(mid_own[...], -1, -5, mx + 11)
         + rows_at(low, -5, -5, mx + 11)
         + rows_at(high, mx - 1, -5, mx + 11)
     )
     mid_x[...] = mid
-    low, high = (from_halves(m[8:13].astype(F32), 9) for m in (before, after))
+    low, high = (from_halves(m[8:13], 9) for m in (before, after))
     coarse = (
         rows_at(coarse_own[...], -2, -6, cx + 13)
         + rows_at(unpair(low, cz), -6, -6, cx + 13)
@@ -186,7 +196,8 @@
     )
     coarse_x[...] = coarse
     buf[...] = jnp.zeros_like(buf)
-    for out, fine_at, mid_at in ((up, cells_y - 4, my - 4), (down, 0, 0)):
+
+    def pack(out, fine_at, mid_at):
         for part, first, last, top, left in fine_parts(cells_x + 8):
             buf[part, top : top + 4, left:] = fine_x[first:last, fine_at : fine_at + 4, :]
         at = (cells_x + 8) // 4
@@ -196,23 +207,26 @@
         buf[at:, 0:9, :] = two_halves(pair_lanes(coarse_x[:, 0:9, :]))
         out[...] = buf[...].astype(BF16)
 
-
-def join_y_kernel(
-    fine_x, mid_x, coarse_x, before, after, fine_xy, mid_xy, coarse_xy, up, down, low, high, buf, side
-):
-    cells_y = fine_x.shape[1]
-    my, cy = cells_y // 2, cells_y // 4
+    flag = up_first(1, 1)
+
+    @pl.when(flag)
+    def _():
+        pack(first_out, cells_y, my - 4)
+        pack(second_out, 4, 0)
+
+    @pl.when(jnp.logical_not(flag))
+    def _():
+        pack(first_out, 4, 0)
+        pack(second_out, cells_y, my - 4)
+
+
+def join_y_kernel(at, mid_x, coarse_x, first_in, second_in, mid_xy, coarse_xy, first_out, second_out, low, high, buf, side):
+    my, cy = mid_x.shape[1] // 2, mid_x.shape[1] // 4
     rows_m, rows_c = mid_x.shape[0], coarse_x.shape[0]
     mz, cz = mid_x.shape[2], coarse_x.shape[2]
-    low[...] = before[...].astype(F32)
-    high[...] = after[...].astype(F32)
-    fine_xy[:, 4 : 4 + cells_y, :] = fine_x[...]
-    for part, first, last, top, _ in fine_parts(fine_x.shape[0]):
-        fine_xy[first:last, 0:4, :] = low[part, top : top + 4, :]
-        fine_xy[first:last, 4 + cells_y : 8 + cells_y, :] = high[part, top : top + 4, :]
+    low[...], high[...] = by_order(up_first(1, 1), first_in[...].astype(F32), second_in[...].astype(F32))
     mid_xy[...] = jnp.zeros_like(mid_xy)
     mid_xy[:, 4 : 7 + my, :] = mid_x[:, 0 : my + 3, :]
-    at = fine_x.shape[0] // 4
     for part, first, last, top, left in quarters(rows_m, at, mz):
         mid_xy[first:last, 0:7, :] += low[part, top : top + 7, left : left + mz]
         mid_xy[first:last, 4 + my : 11 + my, :] += high[part, top : top + 7, left : left + mz]
@@ -231,79 +245,78 @@
             buf[part, top : top + 5, left : left + 2 * cz] = rows[first:last]
         out[...] = buf[...].astype(BF16)
 
-    pack(coarse_xy[:, 4 + cy : 9 + cy, :], up)
+    up = coarse_xy[:, 4 + cy : 9 + cy, :]
     coarse_xy[:, 4 + cy : 13 + cy, :] += from_high
     side[:, 4 + cy : 13 + cy, :] += from_high
-    pack(side[:, 4:9, :], down)
-
-
-def bands_kernel(levels, *refs):
-    n = len(levels)
-    (turned,) = refs[2 * n :]
+    down = side[:, 4:9, :]
+    flag = up_first(2, 0)
+    pack(jnp.where(flag, up, down), first_out)
+    pack(jnp.where(flag, down, up), second_out)
+
+
+def bands_kernel(begin, levels, lines, *refs):
+    outs, joint, last, turned = refs[:-3], refs[-3], refs[-2], refs[-1]
     tap = lax.broadcasted_iota(jnp.int32, (HALF, HALF), 0)
     place = lax.broadcasted_iota(jnp.int32, (HALF, HALF), 1)
     reverse = ((tap <= 8) & (place == jnp.where(tap <= 4, 4 - tap, HALF + 4 - tap))).astype(F32).astype(BF16)
-    for (depth, groups), lines, out in zip(levels, refs[:n], refs[n : 2 * n]):
-        per = HALF // depth
-        flat = lines[...].reshape(9 * 16, HALF).astype(BF16)
-        values = jnp.dot(flat, reverse, preferred_element_type=F32)
-        if per == 1:
-            turned[0] = pltpu.roll(values.reshape(9, 16, HALF), 0, 2, stride=16, stride_axis=1)
-            turned[1, :, 0:8, :] = jnp.broadcast_to(jnp.sum(turned[0, :, 0:8, :], axis=1, keepdims=True), (9, 8, HALF))
-        else:
-            for j in range(per):
-                turned[j] = (pltpu.roll(values, j * depth, 1) if j else values).reshape(9, 16, HALF)
-        apart = lax.rem(tap, depth) - lax.rem(place, depth)
-        band = (apart <= 4) & (apart >= -4)
-
-        def one_dx(dx, carry, per=per, depth=depth, groups=groups, out=out, band=band):
-            def turn(line, by):
-                return pltpu.roll(jnp.broadcast_to(line, (8, HALF)), by, 1, stride=1, stride_axis=0)
-
-            def line_at(first):
-                parts = [turned[j, dx, first - j : first - j + 1, :] for j in range(per) if 0 <= first - j <= 8]
-                return functools.reduce(jnp.add, parts) if parts else None
-
-            if per == 1:
-                joint = [turn(turned[1, dx, 0:1, :], 8 * r) for r in range(16)]
-                last = [turn(turned[0, dx, 8:9, :], 8 * r) for r in range(16)]
-
-            def rows_of(offset):
+    n = len(levels)
+    flat = lines[9 * begin : 9 * (begin + n)].reshape(n * 9 * 16, HALF).astype(BF16)
+    values = jnp.dot(flat, reverse, preferred_element_type=F32).reshape(n * 9, 16, HALF)
+    turned[...] = pltpu.roll(values, 0, 2, stride=16, stride_axis=1)
+    joint[...] = jnp.broadcast_to(jnp.sum(turned[:, 0:8, :], axis=1, keepdims=True), joint.shape)
+    ninth = [turned[9 * i : 9 * i + 9, 8:9, :] for i in range(n)]
+    ninth = functools.reduce(jnp.add, [pltpu.roll(v, 16 * i, 2) if i else v for i, v in enumerate(ninth)])
+    last[...] = jnp.broadcast_to(ninth, last.shape)
+    lane = lax.broadcasted_iota(jnp.int32, (8, HALF), 1)
+
+    def one_dx(dx, carry):
+        def turns(line):
+            return [pltpu.roll(line, 8 * r, 1, stride=1, stride_axis=0) for r in range(16)]
+
+        ninths = turns(last[dx])
+        for level, ((depth, groups), out) in enumerate(zip(levels, outs)):
+            per, steps = HALF // depth, depth // 8
+            eights = turns(joint[9 * level + dx])
+            for offset in range(2 * groups - 1):
+                rows = []
                 for a in range(per):
-                    line = None if per == 1 else line_at(per * offset + a)
-                    for g in range(depth // 8):
-                        if per == 1:
-                            full = last[g] if offset == 8 else joint[(g - 2 * offset) % 16]
-                        else:
-                            full = jnp.zeros((8, HALF), F32) if line is None else turn(line, 8 * g)
-                        at = a * depth + 8 * g
-                        yield jnp.where(band[at : at + 8], full, 0.0)
-
-            zero = jnp.zeros((HALF, HALF), BF16)
-            for offset in range(-1, 2 * groups):
-                block = zero
-                if 0 <= per * offset <= 8:
-                    block = jnp.concatenate(list(rows_of(offset)), axis=0).astype(BF16)
-                for group in range(groups):
-                    for a in (0, 1):
-                        b = 2 * group + a - offset
-                        if b in (0, 1):
-                            at = group * WIDE + a * HALF
-                            out[dx, at : at + HALF, b * HALF : (b + 1) * HALF] = block
-            return carry
-
-        lax.fori_loop(0, 9, one_dx, 0)
-
-
-def bands(stencils, levels):
-    most = max([2] + [HALF // depth for depth, _ in levels])
+                    for g in range(steps):
+                        full = jnp.zeros((8, HALF), F32)
+                        for b in range(per):
+                            line = per * offset + a - b
+                            at = steps * b + g
+                            if 0 <= line <= 8:
+                                part = ninths[(at - 2 * level) % 16] if line == 8 else eights[(at - 2 * line) % 16]
+                                full = part if per == 1 else jnp.where(lane // depth == b, part, full)
+                        apart = lax.rem(lane, depth) - 8 * g - lax.broadcasted_iota(jnp.int32, (8, HALF), 0)
+                        rows.append(jnp.where((apart <= 4) & (apart >= -4), full, 0.0))
+                out[dx, offset] = jnp.concatenate(rows, axis=0).astype(BF16)
+        return carry
+
+    lax.fori_loop(0, 9, one_dx, 0)
+
+
+def bands(lines, begin, levels, after=()):
+    n = len(levels) * 9
     return call(
-        functools.partial(bands_kernel, levels),
-        [((9, groups * WIDE, WIDE), BF16) for _, groups in levels],
-        list(stencils),
-        [((most, 9, 16, HALF), F32)],
+        functools.partial(bands_kernel, begin, levels),
+        [((9, 2 * groups - 1, HALF, HALF), BF16) for _, groups in levels],
+        [lines],
+        [((n, 8, HALF), F32), ((9, 8, HALF), F32), ((n, 16, HALF), F32)],
         flops=10**9,
-    )
+        after=after,
+    )
+
+
+def weights_of(blocks, dx):
+    count = blocks.shape[1]
+    zero = jnp.zeros((HALF, HALF), BF16)
+
+    def block(offset):
+        return blocks[dx, offset] if 0 <= offset < count else zero
+
+    halves = range(count + 1)
+    return jnp.concatenate([jnp.concatenate([block(h), block(h - 1)], axis=1) for h in halves], axis=0)
 
 
 def gather_rows(field, rows, per, groups, depth, lhs):
@@ -332,17 +345,57 @@
     n = out_rows * 8
     for dx in range(9):
         start = 16 * (dx // 2)
-        part = jnp.dot(lhs[dx % 2, start : start + n, :], weights[dx], preferred_element_type=F32)
+        part = jnp.dot(lhs[dx % 2, start : start + n, :], weights_of(weights, dx), preferred_element_type=F32)
         acc[...] = part if dx == 0 else acc[...] + part
 
 
-def conv_kernel(fine_xy, mid_xy, fine_w, mid_w, fine_acc, mid_acc, stage, fine_lhs, mid_lhs):
-    rows = fine_xy.shape[0]
-    gather_rows(fine_xy, rows, 2, 5, fine_xy.shape[2], fine_lhs)
-    convolve(fine_lhs, fine_w, rows - 8, fine_acc)
+def own_kernel(fine_x, weights, acc, lhs):
+    rows = fine_x.shape[0]
+    gather_rows(fine_x, rows, 2, 5, fine_x.shape[2], lhs)
+    convolve(lhs, weights, rows - 8, acc)
+
+
+def group_weights(blocks, dx, group):
+    return weights_of(blocks, dx)[group * WIDE : (group + 1) * WIDE]
+
+
+def rim_kernel(first_in, second_in, mid_xy, own, fine_w, mid_w, fine_acc, mid_acc, rim, stage_f, lhs_f, stage, mid_lhs, sums):
+    cells_x = own.shape[0] // 8
+    quarter = cells_x // 4
+    tiles = rim.shape[1]
+    rim[0], rim[1] = by_order(up_first(1, 1), *(v[0:tiles].astype(F32) for v in (first_in, second_in)))
+    for side in (0, 1):
+        for q in range(4):
+            for r in range(4):
+                first, last = max(quarter * q, tiles * r), min(quarter * q + quarter + 8, tiles * r + tiles)
+                if first < last:
+                    to = slice(first - quarter * q, last - quarter * q)
+                    source_rows = slice(first - tiles * r, last - tiles * r)
+                    for a in (0, 1):
+                        part = rim[side, source_rows, pl.ds(4 * r + a, 2, stride=2), :]
+                        stage_f[side, to, 2 * q : 2 * q + 2, a * HALF : (a + 1) * HALF] = part
+        for parity in (0, 1):
+            n = quarter + 8 - parity
+            lhs_f[side, parity, 0 : 8 * n, :] = stage_f[side, parity : parity + n].reshape(8 * n, WIDE).astype(BF16)
+    n = quarter * 8
+    for dx in range(9):
+        start = 16 * (dx // 2)
+        for i, (side, group) in enumerate(((0, 0), (0, 1), (1, 3), (1, 4))):
+            rows = lhs_f[side, dx % 2, start : start + n, :]
+            part = jnp.dot(rows, group_weights(fine_w, dx, group), preferred_element_type=F32)
+            sums[i] = part if dx == 0 else sums[i] + part
     rows = mid_xy.shape[0]
     gather_staged(mid_xy, rows, 4, 3, mid_xy.shape[2], stage, mid_lhs)
     convolve(mid_lhs, mid_w, rows - 8, mid_acc)
+    fine_acc[...] = own[...].reshape(fine_acc.shape)
+    near, far, far_right, near_right = (sums[i].reshape(quarter, 8, WIDE) for i in range(4))
+    odd = lax.rem(lax.broadcasted_iota(jnp.int32, near.shape, 1), 2) == 1
+    stage_f[0, 0:quarter] = near + jnp.where(odd, 0.0, pltpu.roll(far, 7, 1))
+    stage_f[1, 0:quarter] = near_right + jnp.where(odd, pltpu.roll(far_right, 1, 1), 0.0)
+    for q in range(4):
+        at = slice(quarter * q, quarter * q + quarter)
+        fine_acc[at, 0:2, :] += stage_f[0, 0:quarter, 2 * q : 2 * q + 2, :]
+        fine_acc[at, 6:8, :] += stage_f[1, 0:quarter, 2 * q : 2 * q + 2, :]
 
 
 def prolong_odd(a, b, c, d):
@@ -350,7 +403,7 @@
 
 
 def finish_kernel(
-    counts, coarse_xy, before, after, coarse_w, fine_acc, mid_acc, out,
+    counts, coarse_xy, first_in, second_in, coarse_w, fine_acc, mid_acc, out,
     crs_pad, stage, crs_lhs, crs_acc, msg, crs_pot, wide, mid_tot,
 ):
     gx, gy = lax.axis_index("gx"), lax.axis_index("gy")
@@ -360,8 +413,9 @@
     mx, my, mz = cells_x // 2, cells_y // 2, cells_z // 2
     cx, cy = cells_x // 4, cells_y // 4
     crs_pad[...] = coarse_xy[...]
-    for source, at in ((before, 0), (after, cy + 8)):
-        msg[...] = source[...].astype(F32)
+    received = by_order(up_first(2, 0), *(v[...].astype(F32) for v in (first_in, second_in)))
+    for source, at in zip(received, (0, cy + 8)):
+        msg[...] = source
         for part, first, last, top, left in quarters(rows_c, 0, 2 * cz):
             crs_pad[first:last, at : at + 5, :] += unpair(msg[part, top : top + 5, left : left + 2 * cz], cz)
     gather_staged(crs_pad, rows_c, 8, 2, cz, stage, crs_lhs)
@@ -395,7 +449,7 @@
     keep = inside(total.shape, 0, -1, mx, gx, nx) & inside(total.shape, 1, -1, my, gy, ny)
     mid_tot[0:rows] = jnp.where(keep, total, 0.0)
     matrix = transfer_matrix(cells_z, mz, True)
-    pot = fine_acc[...].reshape(cells_x, 8, WIDE)
+    pot = fine_acc[...]
     for a in (0, 1):
         if a == 0:
             u = mid_tot[0:rows, 1 : 1 + my, :]
@@ -428,10 +482,21 @@
     )(*ins, *after)
 
 
-def exchange(up, down, axis, step, size):
-    forward = [(i, i + step) for i in range(size - step)]
-    backward = [(j, i) for i, j in forward]
-    return lax.ppermute(up, axis, forward), lax.ppermute(down, axis, backward)
+def swap(first, second, axis, step, size, start):
+    received = []
+    for message, group in ((first, start), (second, 1 - start)):
+        lower = [i for i in range(size - step) if (i // step) % 2 == group]
+        pairs = [(i, i + step) for i in lower] + [(i + step, i) for i in lower]
+        received.append(lax.ppermute(message, axis, pairs))
+    return received
+
+
+def up_first(step, start):
+    return lax.rem(lax.axis_index("gy") // step, 2) == start
+
+
+def by_order(flag, first, second):
+    return jnp.where(flag, second, first), jnp.where(flag, first, second)
 
 
 def local(counts, charges, kernel_fine, kernel_mid, kernel_coarse):
@@ -439,11 +504,10 @@
     cells_x, cells_y, cells_z = charges.shape
     mx, mz, cx, cz = cells_x // 2, cells_z // 2, cells_x // 4, cells_z // 4
     frame = cells_y
-    message = ((13, frame, cells_z), BF16)
-    line = ((9, 16, HALF), F32)
-    up, down, mid_own, coarse_own, *lines = call(
+    lines = ((27, 16, HALF), F32)
+    message, fine_own, mid_own, coarse_own, lines = call(
         functools.partial(spread_kernel, counts),
-        [message, message, ((mx + 3, frame, mz), F32), ((cx + 5, frame, cz), F32), line, line, line],
+        [((nx, 13, frame, cells_z), BF16), (charges.shape, BF16), ((mx + 3, frame, mz), F32), ((cx + 5, frame, cz), F32), lines],
         [charges, kernel_fine, kernel_mid, kernel_coarse],
         [
             ((mx + 3, frame + 24, mz), F32),
@@ -456,60 +520,71 @@
         sems=4,
         limit=60 * 1024 * 1024,
     )
-    before, after = exchange(up, down, "gx", 1, nx)
-    levels = ((cells_z, 5), (mz, 3), (cz, 2))
-    fine_w, mid_w, coarse_w = bands(lines, levels)
+    message = lax.all_to_all(message, "gx", 0, 0)
     rows = (cells_x + 8) // 4 + (mx + 14) // 4 + (cx + 14) // 2
-    message = ((rows, frame, cells_z), BF16)
-    fine_x, mid_x, coarse_x, up, down = call(
-        join_x_kernel,
+    packed = ((rows, frame, cells_z), BF16)
+    fine_x, mid_x, coarse_x, lines, first, second = call(
+        functools.partial(join_x_kernel, nx),
         [
-            ((cells_x + 8, cells_y, cells_z), F32),
+            ((cells_x + 8, cells_y + 8, cells_z), F32),
             ((mx + 11, frame, mz), F32),
             ((cx + 13, frame, cz), F32),
-            message,
-            message,
+            (lines.shape, F32),
+            packed,
+            packed,
         ],
-        [charges, mid_own, coarse_own, before, after],
+        [fine_own, mid_own, coarse_own, lines, message],
         [((rows, frame, cells_z), F32)],
-        after=(fine_w,),
-    )
-    before, after = exchange(up, down, "gy", 1, ny)
+    )
+    first, second = swap(first, second, "gy", 1, ny, 1)
+    (fine_w,) = bands(lines, 0, ((cells_z, 5),))
+    (own_acc,) = call(
+        own_kernel,
+        [((cells_x * 8, WIDE), F32)],
+        [fine_x, fine_w],
+        [((2, (cells_x + 8) * 8, 5 * WIDE), BF16)],
+        flops=10**9,
+    )
     half = (cx + 16) // 4
     message = ((half, frame, cells_z), BF16)
-    fine_xy, mid_xy, coarse_xy, up, down = call(
-        join_y_kernel,
+    mid_xy, coarse_xy, last_first, last_second = call(
+        functools.partial(join_y_kernel, (cells_x + 8) // 4),
         [
-            ((cells_x + 8, cells_y + 8, cells_z), F32),
             ((mx + 11, frame + 8, mz), F32),
             ((cx + 13, frame + 8, cz), F32),
             message,
             message,
         ],
-        [fine_x, mid_x, coarse_x, before, after],
+        [mid_x, coarse_x, first, second],
         [
             ((rows, frame, cells_z), F32),
             ((rows, frame, cells_z), F32),
             ((half, frame, cells_z), F32),
             ((cx + 13, frame + 8, cz), F32),
         ],
-    )
-    before, after = exchange(up, down, "gy", 2, ny)
+        after=(own_acc,),
+    )
+    last_first, last_second = swap(last_first, last_second, "gy", 2, ny, 0)
+    quarter = cells_x // 4
+    mid_w, coarse_w = bands(lines, 1, ((mz, 3), (cz, 2)), (mid_xy,))
     fine_acc, mid_acc = call(
-        conv_kernel,
-        [((cells_x * 8, WIDE), F32), (((mx + 3) * 8, WIDE), F32)],
-        [fine_xy, mid_xy, fine_w, mid_w],
+        rim_kernel,
+        [((cells_x, 8, WIDE), F32), (((mx + 3) * 8, WIDE), F32)],
+        [first, second, mid_xy, own_acc, fine_w, mid_w],
         [
+            ((2, (cells_x + 8) // 4, frame, cells_z), F32),
+            ((2, quarter + 8, 8, WIDE), F32),
+            ((2, 2, (quarter + 8) * 8, WIDE), BF16),
             ((mx + 11, 16, WIDE), F32),
-            ((2, (cells_x + 8) * 8, 5 * WIDE), BF16),
             ((2, (mx + 12) * 8, 3 * WIDE), BF16),
+            ((4, quarter * 8, WIDE), F32),
         ],
-        flops=10**10,
+        flops=10**9,
     )
     (out,) = call(
         functools.partial(finish_kernel, counts),
         [(charges.shape, F32)],
-        [coarse_xy, before, after, coarse_w, fine_acc, mid_acc],
+        [coarse_xy, last_first, last_second, coarse_w, fine_acc, mid_acc],
         [
             ((cx + 13, frame + 8, cz), F32),
             ((cx + 13, 16, WIDE), F32),

time: 37.4 us -> 31.1 us (0.83)
  the two profiles are of different devices: /device:TPU:21 before, /device:TPU:0 now
where the time goes in v2:
time: 31.1 us; the launch traced here: 30.9 us
  Pallas kernels  14.2 us (46%)
  blocking collectives  10.6 us (34%)
  starting transfers between devices  5.95 us (19%)
    pallas_call x8, Pallas kernels, call(): pl.pallas_call(body, out_shape=[pltpu.VMEM(s, d) for s, d in outs] if vme...  14.2 us
    all_to_all x1, blocking collectives, local(): message = lax.all_to_all(message, 'gx', 0, 0)  10.6 us
    ppermute x4, starting transfers between devices, swap(): received.append(lax.ppermute(message, axis, pairs))  5.95 us
  transfers between devices with their start and end apart: 4, of which 0 were waited for; matrix products, arithmetic and copies ran while one was open for 0% of the time, Pallas kernels for 27%

profile of v2, /device:TPU:0, one launch (start us, length us, event | category | flops | bytes accessed | tf_op | source)
XLA Modules:
  0.0 30.9 jit_solution(4056076597931375357)
XLA Ops:
  0.0 2.0 %shard_map.46 = (bf16[4,13,16,128]{3,2,1,0:T(8,128)(2,1)S(1)}, bf16[64,16,128]{2,1,0:T(8,128)(2,1)S(1)}, f32[35,16,64]{2,1,0:T(8,128)S(1)}, f32[21,16,32]{2,1,0:T(8,128)S(1)}, f32[27,16,128]{2,1,0:T(8,128)S(1)}) custom-call(f32[64,16,128]{2,1,0:T(8,128)} %refs_0_.1, bf16[9,9,9]{2,1,0:T(8,128)(2,1)} %refs_1_.1, bf16[9,9,9]{2,1,0:T(8,128)(2,1)} %refs_2_.1, ...), custom_call_target="tpu_custom_call" | custom-call | flops 100000000 | bytes 1000000 | tf_op jit(solution)/shard_map/pallas_call | solution.py:474
  2.0 10.6 %all_to_all.5.refs_4_ = bf16[4,13,16,128]{3,2,1,0:T(8,128)(2,1)S(1)} all-to-all(bf16[4,13,16,128]{3,2,1,0:T(8,128)(2,1)S(1)} %get-tuple-element.28), channel_id=1, replica_groups=mesh['gx'=4,'gy'=8] {'gx'}, dimensions={0} | all-to-all | bytes 425984 | tf_op jit(solution)/shard_map/all_to_all | solution.py:523
  12.6 0.6 %shard_map.47 = (f32[72,24,128]{2,1,0:T(8,128)S(1)}, f32[43,16,64]{2,1,0:T(8,128)S(1)}, f32[29,16,32]{2,1,0:T(8,128)S(1)}, f32[27,16,128]{2,1,0:T(8,128)S(1)}, b...) custom-call(bf16[64,16,128]{2,1,0:T(8,128)(2,1)S(1)} %get-tuple-element.24.refs_0_, ...), custom_call_target="tpu_custom_call" | custom-call | flops 100000000 | bytes 1000000 | tf_op jit(solution)/shard_map/pallas_call | solution.py:474
  13.2 0.7 %collective-permute-start = (bf16[44,16,128]{2,1,0:T(8,128)(2,1)S(1)}, bf16[44,16,128]{2,1,0:T(8,128)(2,1)S(1)}, u32[]{:S(2)}, u32[]{:S(2)}) collective-permute-start(bf16[44,16,128]{2,1,0:T(8,128)(2,1)S(1)} %get-tuple-element.31), channel_id=1, source_target_pairs={{1,2},{3,4},{5,6},{2,1},{4,3},{6,5},{9,10},{11,12},{13,14},{10,9},... | collective-permute-start | bytes 540680 | tf_op jit(solution)/shard_map/ppermute | solution.py:490
  13.9 3.0 %collective-permute-start.1 = (bf16[44,16,128]{2,1,0:T(8,128)(2,1)S(1)}, bf16[44,16,128]{2,1,0:T(8,128)(2,1)S(1)}, u32[]{:S(2)}, u32[]{:S(2)}) collective-permute-start(bf16[44,16,128]{2,1,0:T(8,128)(2,1)S(1)} %get-tuple-element.32), channel_id=1, source_target_pairs={{0,1},{2,3},{4,5},{6,7},{1,0},{3,2},{5,4},{7,6},{8,9},{10,11},{12,... | collective-permute-start | bytes 540680 | tf_op jit(solution)/shard_map/ppermute | solution.py:490
  16.8 1.2 %shard_map.48.refs_1_.refs_4_ = bf16[9,9,128,128]{3,2,1,0:T(8,128)(2,1)S(1)} custom-call(f32[27,16,128]{2,1,0:T(8,128)S(1)} %get-tuple-element.34.refs_0_), custom_call_target="tpu_custom_call" | custom-call | flops 1000000000 | bytes 1000000 | tf_op jit(solution)/shard_map/pallas_call | solution.py:474
  18.1 3.3 %shard_map.49.refs_4_.refs_3_ = f32[512,256]{1,0:T(8,128)S(1)} custom-call(f32[72,24,128]{2,1,0:T(8,128)S(1)} %get-tuple-element.33.refs_0_, bf16[9,9,128,128]{3,2,1,0:T(8,128)(2,1)S(1)} %shard_map.48.refs_1_.refs_4_), custom_call_target="tpu_custom_call" | custom-call | flops 1000000000 | bytes 1000000 | tf_op jit(solution)/shard_map/pallas_call | solution.py:474
  21.4 0.0 collective-permute-done.refs_2_.refs_0_
  21.4 0.0 collective-permute-done.1.refs_3_.refs_1_
  21.4 0.5 %shard_map.50 = (f32[43,24,64]{2,1,0:T(8,128)S(1)}, f32[29,24,32]{2,1,0:T(8,128)S(1)}, bf16[8,16,128]{2,1,0:T(8,128)(2,1)S(1)}, bf16[8,16,128]{2,1,0:T(8,128)(2,1)S(1)}) custom-call(f32[43,16,64]{2,1,0:T(8,128)S(1)} %get-tuple-element.29.refs_0_, f32[29,16,32]{2,1,0:T(8,128)S(1)} %get-tuple-element.30.refs_1_, ...), custom_call_target="tpu_custom_call" | custom-call | flops 100000000 | bytes 1000000 | tf_op jit(solution)/shard_map/pallas_call | solution.py:474
  21.9 1.6 %collective-permute-start.2 = (bf16[8,16,128]{2,1,0:T(8,128)(2,1)S(1)}, bf16[8,16,128]{2,1,0:T(8,128)(2,1)S(1)}, u32[]{:S(2)}, u32[]{:S(2)}) collective-permute-start(bf16[8,16,128]{2,1,0:T(8,128)(2,1)S(1)} %get-tuple-element.36), channel_id=1, source_target_pairs={{0,2},{1,3},{4,6},{5,7},{2,0},{3,1},{6,4},{7,5},{8,10},{9,11},{12,... | collective-permute-start | bytes 98312 | tf_op jit(solution)/shard_map/ppermute | solution.py:490
  23.6 0.7 %collective-permute-start.3 = (bf16[8,16,128]{2,1,0:T(8,128)(2,1)S(1)}, bf16[8,16,128]{2,1,0:T(8,128)(2,1)S(1)}, u32[]{:S(2)}, u32[]{:S(2)}) collective-permute-start(bf16[8,16,128]{2,1,0:T(8,128)(2,1)S(1)} %get-tuple-element.37), channel_id=1, source_target_pairs={{2,4},{3,5},{4,2},{5,3},{10,12},{11,13},{12,10},{13,11},{18,20},{1... | collective-permute-start | bytes 98312 | tf_op jit(solution)/shard_map/ppermute | solution.py:490
  24.2 1.5 %shard_map.51 = (bf16[9,5,128,128]{3,2,1,0:T(8,128)(2,1)S(1)}, bf16[9,3,128,128]{3,2,1,0:T(8,128)(2,1)S(1)}) custom-call(f32[27,16,128]{2,1,0:T(8,128)S(1)} %get-tuple-element.34.refs_0_, f32[43,24,64]{2,1,0:T(8,128)S(1)} %get-tuple-element.38.refs_1_.refs_2_), custom_call_target="tpu_custom_call" | custom-call | flops 1000000000 | bytes 1000000 | tf_op jit(solution)/shard_map/pallas_call | solution.py:474
  25.7 2.2 %shard_map.52 = (f32[64,8,256]{2,1,0:T(8,128)S(1)}, f32[280,256]{1,0:T(8,128)S(1)}) custom-call(bf16[44,16,128]{2,1,0:T(8,128)(2,1)S(1)} %collective-permute-done.refs_2_.refs_0_, bf16[44,16,128]{2,1,0:T(8,128)(2,1)S(1)} %collective-permute-done.1.refs_3_.refs_1_, f32[43,24,64]{2,1,0:T(8,128)S(1)} %get-tuple-element.38.refs_1_.refs_2_, ...), custom_call_target="tpu_custom_call" | custom-call | flops 1000000000 | bytes 1000000 | tf_op jit(solution)/shard_map/pallas_call | solution.py:474
  28.0 0.0 collective-permute-done.2.refs_1_
  28.0 0.0 collective-permute-done.3.refs_2_
  28.0 2.9 %shard_map.53 = f32[64,16,128]{2,1,0:T(8,128)} custom-call(f32[29,24,32]{2,1,0:T(8,128)S(1)} %get-tuple-element.35.refs_0_, bf16[8,16,128]{2,1,0:T(8,128)(2,1)S(1)} %collective-permute-done.2.refs_1_, bf16[8,16,128]{2,1,0:T(8,128)(2,1)S(1)} %collective-permute-done.3.refs_2_, bf16[9,3,128,128]{3,2,1,0:T(8,128)(2,1)S(1)} %get-tuple-element.39.refs_3_, ...), custom_call_target="tpu_custom_call" | custom-call | flops 100000000 | bytes 1000000 | tf_op jit(solution)/shard_map/pallas_call | solution.py:474
Async XLA Ops:
  13.2 8.2 %collective-permute-start = (bf16[44,16,128]{2,1,0:T(8,128)(2,1)S(1)}, bf16[44,16,128]{2,1,0:T(8,128)(2,1)S(1)}, u32[]{:S(2)}, u32[]{:S(2)}) collective-permute-start(bf16[44,16,128]{2,1,0:T(8,128)(2,1)S(1)} %get-tuple-element.31), channel_id=1, source_target_pairs={{1,2},{3,4},{5,6},{2,1},{4,3},{6,5},{9,10},{11,12},{13,14},{10,9},... | collective-permute-start | bytes 540680 | tf_op jit(solution)/shard_map/ppermute | solution.py:490
  13.9 7.6 %collective-permute-start.1 = (bf16[44,16,128]{2,1,0:T(8,128)(2,1)S(1)}, bf16[44,16,128]{2,1,0:T(8,128)(2,1)S(1)}, u32[]{:S(2)}, u32[]{:S(2)}) collective-permute-start(bf16[44,16,128]{2,1,0:T(8,128)(2,1)S(1)} %get-tuple-element.32), channel_id=1, source_target_pairs={{0,1},{2,3},{4,5},{6,7},{1,0},{3,2},{5,4},{7,6},{8,9},{10,11},{12,... | collective-permute-start | bytes 540680 | tf_op jit(solution)/shard_map/ppermute | solution.py:490
  21.9 6.0 %collective-permute-start.2 = (bf16[8,16,128]{2,1,0:T(8,128)(2,1)S(1)}, bf16[8,16,128]{2,1,0:T(8,128)(2,1)S(1)}, u32[]{:S(2)}, u32[]{:S(2)}) collective-permute-start(bf16[8,16,128]{2,1,0:T(8,128)(2,1)S(1)} %get-tuple-element.36), channel_id=1, source_target_pairs={{0,2},{1,3},{4,6},{5,7},{2,0},{3,1},{6,4},{7,5},{8,10},{9,11},{12,... | collective-permute-start | bytes 98312 | tf_op jit(solution)/shard_map/ppermute | solution.py:490
  23.6 4.4 %collective-permute-start.3 = (bf16[8,16,128]{2,1,0:T(8,128)(2,1)S(1)}, bf16[8,16,128]{2,1,0:T(8,128)(2,1)S(1)}, u32[]{:S(2)}, u32[]{:S(2)}) collective-permute-start(bf16[8,16,128]{2,1,0:T(8,128)(2,1)S(1)} %get-tuple-element.37), channel_id=1, source_target_pairs={{2,4},{3,5},{4,2},{5,3},{10,12},{11,13},{12,10},{13,11},{18,20},{1... | collective-permute-start | bytes 98312 | tf_op jit(solution)/shard_map/ppermute | solution.py:490

commit v3 on v2

--- a/solution.py
+++ b/solution.py
@@ -81,8 +81,8 @@
 
 
 def spread_kernel(counts, *refs):
-    outside, (message, fine_own, mid_own, coarse_own, lines) = refs[0:4], refs[4:9]
-    (even_pad, odd_pad, crs, charges), raws, sems = refs[9:13], refs[13:16], refs[16]
+    outside, (first_out, second_out, fine_own, mid_own, coarse_own, lines) = refs[0:4], refs[4:10]
+    (even_pad, odd_pad, crs, charges), raws, sems = refs[10:14], refs[14:17], refs[17]
     copies = [
         pltpu.make_async_copy(source, target, sems.at[i])
         for i, (source, target) in enumerate(zip(outside, (charges,) + raws))
@@ -126,12 +126,23 @@
     keep = inside(coarse.shape, 0, -2, cx, gx, nx) & inside(coarse.shape, 1, -2, cy, gy, ny)
     coarse = jnp.where(keep, coarse, 0.0)
     coarse_own[...] = coarse
-    after, before = jnp.minimum(gx + 1, nx - 1), jnp.maximum(gx - 1, 0)
-    for slot, fine_at, mid_at, coarse_at in ((after, cells_x - 4, mx - 4, cx - 4), (before, 0, 0, 0)):
-        out = message.at[slot]
+    def pack(out, fine_at, mid_at, coarse_at):
         out[0:4] = charges[fine_at : fine_at + 4].astype(BF16)
-        out[4:8] = two_halves(mid[mid_at : mid_at + 7]).astype(BF16)
-        out[8:13] = two_halves(pair_lanes(coarse[coarse_at : coarse_at + 9])).astype(BF16)
+        out[4:8] = two_halves(mid_own[mid_at : mid_at + 7]).astype(BF16)
+        out[8:13] = two_halves(pair_lanes(coarse_own[coarse_at : coarse_at + 9])).astype(BF16)
+
+    flag = up_first("gx", 1, 1)
+
+    @pl.when(flag)
+    def _():
+        pack(first_out, cells_x - 4, mx - 4, cx - 4)
+        pack(second_out, 0, 0, 0)
+
+    @pl.when(jnp.logical_not(flag))
+    def _():
+        pack(first_out, 0, 0, 0)
+        pack(second_out, cells_x - 4, mx - 4, cx - 4)
+
     for i, raw in enumerate(raws):
         copies[i + 1].wait()
         lines[9 * i : 9 * i + 9, 0:9, 0:9] = raw[...].astype(F32)
@@ -165,11 +176,8 @@
     return parts
 
 
-def join_x_kernel(nx, charges, mid_own, coarse_own, lines, message, fine_x, mid_x, coarse_x, lines_x, first_out, second_out, buf):
-    gx = lax.axis_index("gx")
-    lines_x[...] = lines[...]
-    before = jnp.where(gx > 0, message[jnp.maximum(gx - 1, 0)].astype(F32), 0.0)
-    after = jnp.where(gx < nx - 1, message[jnp.minimum(gx + 1, nx - 1)].astype(F32), 0.0)
+def join_x_kernel(charges, mid_own, coarse_own, first_in, second_in, fine_x, mid_x, coarse_x, first_out, second_out, buf):
+    before, after = by_order(up_first("gx", 1, 1), *(v[...].astype(F32) for v in (first_in, second_in)))
     cells_x, cells_y, _ = charges.shape
     mx, cx = cells_x // 2, cells_x // 4
     mz, cz = mid_own.shape[2], coarse_own.shape[2]
@@ -207,7 +215,7 @@
         buf[at:, 0:9, :] = two_halves(pair_lanes(coarse_x[:, 0:9, :]))
         out[...] = buf[...].astype(BF16)
 
-    flag = up_first(1, 1)
+    flag = up_first("gy", 1, 1)
 
     @pl.when(flag)
     def _():
@@ -224,7 +232,7 @@
     my, cy = mid_x.shape[1] // 2, mid_x.shape[1] // 4
     rows_m, rows_c = mid_x.shape[0], coarse_x.shape[0]
     mz, cz = mid_x.shape[2], coarse_x.shape[2]
-    low[...], high[...] = by_order(up_first(1, 1), first_in[...].astype(F32), second_in[...].astype(F32))
+    low[...], high[...] = by_order(up_first("gy", 1, 1), first_in[...].astype(F32), second_in[...].astype(F32))
     mid_xy[...] = jnp.zeros_like(mid_xy)
     mid_xy[:, 4 : 7 + my, :] = mid_x[:, 0 : my + 3, :]
     for part, first, last, top, left in quarters(rows_m, at, mz):
@@ -249,7 +257,7 @@
     coarse_xy[:, 4 + cy : 13 + cy, :] += from_high
     side[:, 4 + cy : 13 + cy, :] += from_high
     down = side[:, 4:9, :]
-    flag = up_first(2, 0)
+    flag = up_first("gy", 2, 0)
     pack(jnp.where(flag, up, down), first_out)
     pack(jnp.where(flag, down, up), second_out)
 
@@ -363,7 +371,7 @@
     cells_x = own.shape[0] // 8
     quarter = cells_x // 4
     tiles = rim.shape[1]
-    rim[0], rim[1] = by_order(up_first(1, 1), *(v[0:tiles].astype(F32) for v in (first_in, second_in)))
+    rim[0], rim[1] = by_order(up_first("gy", 1, 1), *(v[0:tiles].astype(F32) for v in (first_in, second_in)))
     for side in (0, 1):
         for q in range(4):
             for r in range(4):
@@ -413,7 +421,7 @@
     mx, my, mz = cells_x // 2, cells_y // 2, cells_z // 2
     cx, cy = cells_x // 4, cells_y // 4
     crs_pad[...] = coarse_xy[...]
-    received = by_order(up_first(2, 0), *(v[...].astype(F32) for v in (first_in, second_in)))
+    received = by_order(up_first("gy", 2, 0), *(v[...].astype(F32) for v in (first_in, second_in)))
     for source, at in zip(received, (0, cy + 8)):
         msg[...] = source
         for part, first, last, top, left in quarters(rows_c, 0, 2 * cz):
@@ -491,8 +499,8 @@
     return received
 
 
-def up_first(step, start):
-    return lax.rem(lax.axis_index("gy") // step, 2) == start
+def up_first(axis, step, start):
+    return lax.rem(lax.axis_index(axis) // step, 2) == start
 
 
 def by_order(flag, first, second):
@@ -505,9 +513,10 @@
     mx, mz, cx, cz = cells_x // 2, cells_z // 2, cells_x // 4, cells_z // 4
     frame = cells_y
     lines = ((27, 16, HALF), F32)
-    message, fine_own, mid_own, coarse_own, lines = call(
+    message = ((13, frame, cells_z), BF16)
+    first, second, fine_own, mid_own, coarse_own, lines = call(
         functools.partial(spread_kernel, counts),
-        [((nx, 13, frame, cells_z), BF16), (charges.shape, BF16), ((mx + 3, frame, mz), F32), ((cx + 5, frame, cz), F32), lines],
+        [message, message, (charges.shape, BF16), ((mx + 3, frame, mz), F32), ((cx + 5, frame, cz), F32), lines],
         [charges, kernel_fine, kernel_mid, kernel_coarse],
         [
             ((mx + 3, frame + 24, mz), F32),
@@ -520,24 +529,24 @@
         sems=4,
         limit=60 * 1024 * 1024,
     )
-    message = lax.all_to_all(message, "gx", 0, 0)
+    first, second = swap(first, second, "gx", 1, nx, 1)
+    fine_w, mid_w, coarse_w = bands(lines, 0, ((cells_z, 5), (mz, 3), (cz, 2)))
     rows = (cells_x + 8) // 4 + (mx + 14) // 4 + (cx + 14) // 2
     packed = ((rows, frame, cells_z), BF16)
-    fine_x, mid_x, coarse_x, lines, first, second = call(
-        functools.partial(join_x_kernel, nx),
+    fine_x, mid_x, coarse_x, first, second = call(
+        join_x_kernel,
         [
             ((cells_x + 8, cells_y + 8, cells_z), F32),
             ((mx + 11, frame, mz), F32),
             ((cx + 13, frame, cz), F32),
-            (lines.shape, F32),
             packed,
             packed,
         ],
-        [fine_own, mid_own, coarse_own, lines, message],
+        [fine_own, mid_own, coarse_own, first, second],
         [((rows, frame, cells_z), F32)],
+        after=(fine_w,),
     )
     first, second = swap(first, second, "gy", 1, ny, 1)
-    (fine_w,) = bands(lines, 0, ((cells_z, 5),))
     (own_acc,) = call(
         own_kernel,
         [((cells_x * 8, WIDE), F32)],
@@ -566,7 +575,6 @@
     )
     last_first, last_second = swap(last_first, last_second, "gy", 2, ny, 0)
     quarter = cells_x // 4
-    mid_w, coarse_w = bands(lines, 1, ((mz, 3), (cz, 2)), (mid_xy,))
     fine_acc, mid_acc = call(
         rim_kernel,
         [((cells_x, 8, WIDE), F32), (((mx + 3) * 8, WIDE), F32)],

time: 31.1 us -> 28 us (0.900)
  the two profiles are of different devices: /device:TPU:0 before, /device:TPU:20 now
where the time goes in v3:
time: 28 us; the launch traced here: 27.8 us
  Pallas kernels  13.5 us (48%)
  starting transfers between devices  10.4 us (37%)
  waiting for transfers between devices  3.78 us (14%)
    pallas_call x7, Pallas kernels, call(): pl.pallas_call(body, out_shape=[pltpu.VMEM(s, d) for s, d in outs] if vme...  13.5 us
    ppermute x6, starting transfers between devices, swap(): received.append(lax.ppermute(message, axis, pairs))  10.4 us
    ppermute x6, waiting for transfers between devices, swap(): received.append(lax.ppermute(message, axis, pairs))  3.78 us
  transfers between devices with their start and end apart: 6, of which 3 were waited for; matrix products, arithmetic and copies ran while one was open for 0% of the time, Pallas kernels for 27%

profile of v3, /device:TPU:20, one launch (start us, length us, event | category | flops | bytes accessed | tf_op | source)
XLA Modules:
  0.0 27.8 jit_solution(4944720424059215235)
XLA Ops:
  0.0 2.0 %shard_map.46 = (bf16[13,16,128]{2,1,0:T(8,128)(2,1)S(1)}, bf16[13,16,128]{2,1,0:T(8,128)(2,1)S(1)}, bf16[64,16,128]{2,1,0:T(8,128)(2,1)S(1)}, f32[35,16,64]{2,1...) custom-call(f32[64,16,128]{2,1,0:T(8,128)} %refs_0_.1, bf16[9,9,9]{2,1,0:T(8,128)(2,1)} %refs_1_.1, ...), custom_call_target="tpu_custom_call" | custom-call | flops 100000000 | bytes 1000000 | tf_op jit(solution)/shard_map/pallas_call | solution.py:482
  2.0 3.3 %collective-permute-start = (bf16[13,16,128]{2,1,0:T(8,128)(2,1)S(1)}, bf16[13,16,128]{2,1,0:T(8,128)(2,1)S(1)}, u32[]{:S(2)}, u32[]{:S(2)}) collective-permute-start(bf16[13,16,128]{2,1,0:T(8,128)(2,1)S(1)} %get-tuple-element.28), channel_id=1, source_target_pairs={{8,16},{16,8},{9,17},{17,9},{10,18},{18,10},{11,19},{19,11},{12,20... | collective-permute-start | bytes 159752 | tf_op jit(solution)/shard_map/ppermute | solution.py:498
  5.4 0.1 collective-permute-start.1
  5.5 2.0 %shard_map.47 = (bf16[9,9,128,128]{3,2,1,0:T(8,128)(2,1)S(1)}, bf16[9,5,128,128]{3,2,1,0:T(8,128)(2,1)S(1)}, bf16[9,3,128,128]{3,2,1,0:T(8,128)(2,1)S(1)}) custom-call(f32[27,16,128]{2,1,0:T(8,128)S(1)} %get-tuple-element.30.refs_0_), custom_call_target="tpu_custom_call" | custom-call | flops 1000000000 | bytes 1000000 | tf_op jit(solution)/shard_map/pallas_call | solution.py:482
  7.4 1.5 %collective-permute-done.refs_3_ = bf16[13,16,128]{2,1,0:T(8,128)(2,1)S(1)} collective-permute-done((bf16[13,16,128]{2,1,0:T(8,128)(2,1)S(1)}, bf16[13,16,128]{2,1,0:T(8,128)(2,1)S(1)}, u32[]{:S(2)}, u32[]{:S(2)}) %collective-permute-start) | collective-permute-done | bytes 53280 | tf_op jit(solution)/shard_map/ppermute | solution.py:498
  9.0 0.6 %collective-permute-done.1.refs_4_ = bf16[13,16,128]{2,1,0:T(8,128)(2,1)S(1)} collective-permute-done((bf16[13,16,128]{2,1,0:T(8,128)(2,1)S(1)}, bf16[13,16,128]{2,1,0:T(8,128)(2,1)S(1)}, u32[]{:S(2)}, u32[]{:S(2)}) %collective-permute-start.1) | collective-permute-done | bytes 53280 | tf_op jit(solution)/shard_map/ppermute | solution.py:498
  9.6 0.6 %shard_map.48 = (f32[72,24,128]{2,1,0:T(8,128)S(1)}, f32[43,16,64]{2,1,0:T(8,128)S(1)}, f32[29,16,32]{2,1,0:T(8,128)S(1)}, bf16[44,16,128]{2,1,0:T(8,128)(2,1)S(1)}, bf16[44,16,128]{2,1,0:T(8,128)(2,1)S(1)}) custom-call(bf16[64,16,128]{2,1,0:T(8,128)(2,1)S(1)} %get-tuple-element.25.refs_0_, f32[35,16,64]{2,1,0:T(8,128)S(1)} %get-tuple-element.26.refs_1_, ...), custom_call_target="tpu_custom_call" | custom-call | flops 100000000 | bytes 1000000 | tf_op jit(solution)/shard_map/pallas_call | solution.py:482
  10.2 1.9 %collective-permute-start.2 = (bf16[44,16,128]{2,1,0:T(8,128)(2,1)S(1)}, bf16[44,16,128]{2,1,0:T(8,128)(2,1)S(1)}, u32[]{:S(2)}, u32[]{:S(2)}) collective-permute-start(bf16[44,16,128]{2,1,0:T(8,128)(2,1)S(1)} %get-tuple-element.34), channel_id=1, source_target_pairs={{1,2},{3,4},{5,6},{2,1},{4,3},{6,5},{9,10},{11,12},{13,14},{10,9},... | collective-permute-start | bytes 540680 | tf_op jit(solution)/shard_map/ppermute | solution.py:498
  12.1 1.7 %collective-permute-start.3 = (bf16[44,16,128]{2,1,0:T(8,128)(2,1)S(1)}, bf16[44,16,128]{2,1,0:T(8,128)(2,1)S(1)}, u32[]{:S(2)}, u32[]{:S(2)}) collective-permute-start(bf16[44,16,128]{2,1,0:T(8,128)(2,1)S(1)} %get-tuple-element.35), channel_id=1, source_target_pairs={{0,1},{2,3},{4,5},{6,7},{1,0},{3,2},{5,4},{7,6},{8,9},{10,11},{12,... | collective-permute-start | bytes 540680 | tf_op jit(solution)/shard_map/ppermute | solution.py:498
  13.8 3.3 %shard_map.49.refs_4_.refs_3_ = f32[512,256]{1,0:T(8,128)S(1)} custom-call(f32[72,24,128]{2,1,0:T(8,128)S(1)} %get-tuple-element.36.refs_0_, bf16[9,9,128,128]{3,2,1,0:T(8,128)(2,1)S(1)} %get-tuple-element.31.refs_5_.refs_1_.refs_4_), custom_call_target="tpu_custom_call" | custom-call | flops 1000000000 | bytes 1000000 | tf_op jit(solution)/shard_map/pallas_call | solution.py:482
  17.2 0.0 collective-permute-done.2.refs_2_.refs_0_
  17.2 0.0 collective-permute-done.3.refs_3_.refs_1_
  17.2 0.5 %shard_map.50 = (f32[43,24,64]{2,1,0:T(8,128)S(1)}, f32[29,24,32]{2,1,0:T(8,128)S(1)}, bf16[8,16,128]{2,1,0:T(8,128)(2,1)S(1)}, bf16[8,16,128]{2,1,0:T(8,128)(2,1)S(1)}) custom-call(f32[43,16,64]{2,1,0:T(8,128)S(1)} %get-tuple-element.32.refs_0_, f32[29,16,32]{2,1,0:T(8,128)S(1)} %get-tuple-element.33.refs_1_, ...), custom_call_target="tpu_custom_call" | custom-call | flops 100000000 | bytes 1000000 | tf_op jit(solution)/shard_map/pallas_call | solution.py:482
  17.7 1.4 %collective-permute-start.4 = (bf16[8,16,128]{2,1,0:T(8,128)(2,1)S(1)}, bf16[8,16,128]{2,1,0:T(8,128)(2,1)S(1)}, u32[]{:S(2)}, u32[]{:S(2)}) collective-permute-start(bf16[8,16,128]{2,1,0:T(8,128)(2,1)S(1)} %get-tuple-element.38), channel_id=1, source_target_pairs={{0,2},{1,3},{4,6},{5,7},{2,0},{3,1},{6,4},{7,5},{8,10},{9,11},{12,... | collective-permute-start | bytes 98312 | tf_op jit(solution)/shard_map/ppermute | solution.py:498
  19.1 1.9 %collective-permute-start.5 = (bf16[8,16,128]{2,1,0:T(8,128)(2,1)S(1)}, bf16[8,16,128]{2,1,0:T(8,128)(2,1)S(1)}, u32[]{:S(2)}, u32[]{:S(2)}) collective-permute-start(bf16[8,16,128]{2,1,0:T(8,128)(2,1)S(1)} %get-tuple-element.39), channel_id=1, source_target_pairs={{2,4},{3,5},{4,2},{5,3},{10,12},{11,13},{12,10},{13,11},{18,20},{1... | collective-permute-start | bytes 98312 | tf_op jit(solution)/shard_map/ppermute | solution.py:498
  21.1 2.2 %shard_map.51 = (f32[64,8,256]{2,1,0:T(8,128)S(1)}, f32[280,256]{1,0:T(8,128)S(1)}) custom-call(bf16[44,16,128]{2,1,0:T(8,128)(2,1)S(1)} %collective-permute-done.2.refs_2_.refs_0_, bf16[44,16,128]{2,1,0:T(8,128)(2,1)S(1)} %collective-permute-done.3.refs_3_.refs_1_, f32[43,24,64]{2,1,0:T(8,128)S(1)} %get-tuple-element.41.refs_2_, ...), custom_call_target="tpu_custom_call" | custom-call | flops 1000000000 | bytes 1000000 | tf_op jit(solution)/shard_map/pallas_call | solution.py:482
  23.3 0.0 collective-permute-done.4.refs_1_
  23.3 1.6 %collective-permute-done.5.refs_2_ = bf16[8,16,128]{2,1,0:T(8,128)(2,1)S(1)} collective-permute-done((bf16[8,16,128]{2,1,0:T(8,128)(2,1)S(1)}, bf16[8,16,128]{2,1,0:T(8,128)(2,1)S(1)}, u32[]{:S(2)}, u32[]{:S(2)}) %collective-permute-start.5) | collective-permute-done | bytes 32800 | tf_op jit(solution)/shard_map/ppermute | solution.py:498
  24.9 2.9 %shard_map.52 = f32[64,16,128]{2,1,0:T(8,128)} custom-call(f32[29,24,32]{2,1,0:T(8,128)S(1)} %get-tuple-element.37.refs_0_, bf16[8,16,128]{2,1,0:T(8,128)(2,1)S(1)} %collective-permute-done.4.refs_1_, bf16[8,16,128]{2,1,0:T(8,128)(2,1)S(1)} %collective-permute-done.5.refs_2_, bf16[9,3,128,128]{3,2,1,0:T(8,128)(2,1)S(1)} %get-tuple-element.40.refs_3_, ...), custom_call_target="tpu_custom_call" | custom-call | flops 100000000 | bytes 1000000 | tf_op jit(solution)/shard_map/pallas_call | solution.py:482
Async XLA Ops:
  2.0 6.9 %collective-permute-start = (bf16[13,16,128]{2,1,0:T(8,128)(2,1)S(1)}, bf16[13,16,128]{2,1,0:T(8,128)(2,1)S(1)}, u32[]{:S(2)}, u32[]{:S(2)}) collective-permute-start(bf16[13,16,128]{2,1,0:T(8,128)(2,1)S(1)} %get-tuple-element.28), channel_id=1, source_target_pairs={{8,16},{16,8},{9,17},{17,9},{10,18},{18,10},{11,19},{19,11},{12,20... | collective-permute-start | bytes 159752 | tf_op jit(solution)/shard_map/ppermute | solution.py:498
  5.4 4.2 %collective-permute-start.1 = (bf16[13,16,128]{2,1,0:T(8,128)(2,1)S(1)}, bf16[13,16,128]{2,1,0:T(8,128)(2,1)S(1)}, u32[]{:S(2)}, u32[]{:S(2)}) collective-permute-start(bf16[13,16,128]{2,1,0:T(8,128)(2,1)S(1)} %get-tuple-element.29), channel_id=1, source_target_pairs={{0,8},{16,24},{8,0},{24,16},{1,9},{17,25},{9,1},{25,17},{2,10},{18... | collective-permute-start | bytes 159752 | tf_op jit(solution)/shard_map/ppermute | solution.py:498
  10.2 7.0 %collective-permute-start.2 = (bf16[44,16,128]{2,1,0:T(8,128)(2,1)S(1)}, bf16[44,16,128]{2,1,0:T(8,128)(2,1)S(1)}, u32[]{:S(2)}, u32[]{:S(2)}) collective-permute-start(bf16[44,16,128]{2,1,0:T(8,128)(2,1)S(1)} %get-tuple-element.34), channel_id=1, source_target_pairs={{1,2},{3,4},{5,6},{2,1},{4,3},{6,5},{9,10},{11,12},{13,14},{10,9},... | collective-permute-start | bytes 540680 | tf_op jit(solution)/shard_map/ppermute | solution.py:498
  12.1 5.1 %collective-permute-start.3 = (bf16[44,16,128]{2,1,0:T(8,128)(2,1)S(1)}, bf16[44,16,128]{2,1,0:T(8,128)(2,1)S(1)}, u32[]{:S(2)}, u32[]{:S(2)}) collective-permute-start(bf16[44,16,128]{2,1,0:T(8,128)(2,1)S(1)} %get-tuple-element.35), channel_id=1, source_target_pairs={{0,1},{2,3},{4,5},{6,7},{1,0},{3,2},{5,4},{7,6},{8,9},{10,11},{12,... | collective-permute-start | bytes 540680 | tf_op jit(solution)/shard_map/ppermute | solution.py:498
  17.7 5.6 %collective-permute-start.4 = (bf16[8,16,128]{2,1,0:T(8,128)(2,1)S(1)}, bf16[8,16,128]{2,1,0:T(8,128)(2,1)S(1)}, u32[]{:S(2)}, u32[]{:S(2)}) collective-permute-start(bf16[8,16,128]{2,1,0:T(8,128)(2,1)S(1)} %get-tuple-element.38), channel_id=1, source_target_pairs={{0,2},{1,3},{4,6},{5,7},{2,0},{3,1},{6,4},{7,5},{8,10},{9,11},{12,... | collective-permute-start | bytes 98312 | tf_op jit(solution)/shard_map/ppermute | solution.py:498
  19.1 5.8 %collective-permute-start.5 = (bf16[8,16,128]{2,1,0:T(8,128)(2,1)S(1)}, bf16[8,16,128]{2,1,0:T(8,128)(2,1)S(1)}, u32[]{:S(2)}, u32[]{:S(2)}) collective-permute-start(bf16[8,16,128]{2,1,0:T(8,128)(2,1)S(1)} %get-tuple-element.39), channel_id=1, source_target_pairs={{2,4},{3,5},{4,2},{5,3},{10,12},{11,13},{12,10},{13,11},{18,20},{1... | collective-permute-start | bytes 98312 | tf_op jit(solution)/shard_map/ppermute | solution.py:498

commit v4 on v3

--- a/solution.py
+++ b/solution.py
@@ -412,7 +412,7 @@
 
 def finish_kernel(
     counts, coarse_xy, first_in, second_in, coarse_w, fine_acc, mid_acc, out,
-    crs_pad, stage, crs_lhs, crs_acc, msg, crs_pot, wide, mid_tot,
+    crs_pad, stage, packed, crs_lhs, msg, crs_pot, wide, mid_tot,
 ):
     gx, gy = lax.axis_index("gx"), lax.axis_index("gy")
     nx, ny = counts
@@ -426,13 +426,26 @@
         msg[...] = source
         for part, first, last, top, left in quarters(rows_c, 0, 2 * cz):
             crs_pad[first:last, at : at + 5, :] += unpair(msg[part, top : top + 5, left : left + 2 * cz], cz)
-    gather_staged(crs_pad, rows_c, 8, 2, cz, stage, crs_lhs)
-    convolve(crs_lhs, coarse_w, rows_c - 8, crs_acc)
     rows = rows_c - 8
-    pot = crs_acc[...].reshape(rows, 8, WIDE)
-    for b in range(8):
-        crs_pot[:, pl.ds(b, 2, stride=8), :] = pot[:, 0:2, b * cz : (b + 1) * cz]
-    pot = crs_pot[...]
+    part = crs_lhs.shape[0] // 8
+    per = HALF // cz
+    stage[...] = jnp.zeros_like(stage)
+    for a in range(per):
+        stage[0:rows_c, 0:5, a * cz : (a + 1) * cz] = crs_pad[:, pl.ds(a, 5, stride=per), :]
+    for q in range(2):
+        for group in range(3):
+            moved = stage[part * q : part * q + part + 8, group : group + 4, :]
+            packed[:, 4 * q : 4 * q + 4, group * HALF : (group + 1) * HALF] = moved
+    for dx in range(9):
+        lhs = packed[dx : dx + part].reshape(part * 8, 3 * HALF)
+        crs_lhs[:, dx * 3 * HALF : (dx + 1) * 3 * HALF] = lhs.astype(BF16)
+    weights = coarse_w[...].reshape(9 * 3 * HALF, HALF)
+    pot = jnp.dot(crs_lhs[...], weights, preferred_element_type=F32).reshape(part, 8, HALF)
+    for q in range(2):
+        for b in range(per):
+            moved = pot[:, 4 * q : 4 * q + 3, b * cz : (b + 1) * cz]
+            crs_pot[part * q : part * q + part, pl.ds(b, 3, stride=per), :] = moved
+    pot = crs_pot[0:rows]
     keep = inside(pot.shape, 0, -2, cx, gx, nx) & inside(pot.shape, 1, -2, cy, gy, ny)
     pot = jnp.where(keep, pot, 0.0)
     n = cx + 2
@@ -589,17 +602,18 @@
         ],
         flops=10**9,
     )
+    part = (cx + 6) // 2
     (out,) = call(
         functools.partial(finish_kernel, counts),
         [(charges.shape, F32)],
         [coarse_xy, last_first, last_second, coarse_w, fine_acc, mid_acc],
         [
             ((cx + 13, frame + 8, cz), F32),
-            ((cx + 13, 16, WIDE), F32),
-            ((2, (cx + 14) * 8, 2 * WIDE), BF16),
-            (((cx + 5) * 8, WIDE), F32),
+            ((2 * part + 8, 8, HALF), F32),
+            ((part + 8, 8, 3 * HALF), F32),
+            ((part * 8, 9 * 3 * HALF), BF16),
             ((half, frame, cells_z), F32),
-            ((cx + 5, 16, cz), F32),
+            ((2 * part, 16, cz), F32),
             ((cx + 2, 2, 16, cz), F32),
             ((mx + 4, 16, mz), F32),
         ],

time: 28 us -> 27.5 us (0.982)
  Pallas kernels: 13.5 us -> 13 us
    pallas_call x7, Pallas kernels: 13.5 us -> 13 us  [call(): pl.pallas_call(body, out_shape=[pltpu.VMEM(s, d) for s, d in outs] if vme...]
  transfers between devices with their start and end apart: 6 -> 6, of which waited for: 3 -> 3; matrix products, arithmetic and copies ran while one was open for 0% -> 0% of each run, Pallas kernels for 27% -> 28%
where the time goes in v4:
time: 27.5 us; the launch traced here: 27.2 us
  Pallas kernels  13 us (47%)
  starting transfers between devices  10.4 us (38%)
  waiting for transfers between devices  3.78 us (14%)
    pallas_call x7, Pallas kernels, call(): pl.pallas_call(body, out_shape=[pltpu.VMEM(s, d) for s, d in outs] if vme...  13 us
    ppermute x6, starting transfers between devices, swap(): received.append(lax.ppermute(message, axis, pairs))  10.4 us
    ppermute x6, waiting for transfers between devices, swap(): received.append(lax.ppermute(message, axis, pairs))  3.78 us
  transfers between devices with their start and end apart: 6, of which 3 were waited for; matrix products, arithmetic and copies ran while one was open for 0% of the time, Pallas kernels for 28%

profile of v4, /device:TPU:20, one launch (start us, length us, event | category | flops | bytes accessed | tf_op | source)
XLA Modules:
  0.0 27.2 jit_solution(130294983638804520)
XLA Ops:
  0.0 2.0 %shard_map.46 = (bf16[13,16,128]{2,1,0:T(8,128)(2,1)S(1)}, bf16[13,16,128]{2,1,0:T(8,128)(2,1)S(1)}, bf16[64,16,128]{2,1,0:T(8,128)(2,1)S(1)}, f32[35,16,64]{2,1...) custom-call(f32[64,16,128]{2,1,0:T(8,128)} %refs_0_.1, bf16[9,9,9]{2,1,0:T(8,128)(2,1)} %refs_1_.1, ...), custom_call_target="tpu_custom_call" | custom-call | flops 100000000 | bytes 1000000 | tf_op jit(solution)/shard_map/pallas_call | solution.py:495
  2.0 3.3 %collective-permute-start = (bf16[13,16,128]{2,1,0:T(8,128)(2,1)S(1)}, bf16[13,16,128]{2,1,0:T(8,128)(2,1)S(1)}, u32[]{:S(2)}, u32[]{:S(2)}) collective-permute-start(bf16[13,16,128]{2,1,0:T(8,128)(2,1)S(1)} %get-tuple-element.28), channel_id=1, source_target_pairs={{8,16},{16,8},{9,17},{17,9},{10,18},{18,10},{11,19},{19,11},{12,20... | collective-permute-start | bytes 159752 | tf_op jit(solution)/shard_map/ppermute | solution.py:511
  5.4 0.1 collective-permute-start.1
  5.5 2.0 %shard_map.47 = (bf16[9,9,128,128]{3,2,1,0:T(8,128)(2,1)S(1)}, bf16[9,5,128,128]{3,2,1,0:T(8,128)(2,1)S(1)}, bf16[9,3,128,128]{3,2,1,0:T(8,128)(2,1)S(1)}) custom-call(f32[27,16,128]{2,1,0:T(8,128)S(1)} %get-tuple-element.30.refs_0_), custom_call_target="tpu_custom_call" | custom-call | flops 1000000000 | bytes 1000000 | tf_op jit(solution)/shard_map/pallas_call | solution.py:495
  7.4 1.5 %collective-permute-done.refs_3_ = bf16[13,16,128]{2,1,0:T(8,128)(2,1)S(1)} collective-permute-done((bf16[13,16,128]{2,1,0:T(8,128)(2,1)S(1)}, bf16[13,16,128]{2,1,0:T(8,128)(2,1)S(1)}, u32[]{:S(2)}, u32[]{:S(2)}) %collective-permute-start) | collective-permute-done | bytes 53280 | tf_op jit(solution)/shard_map/ppermute | solution.py:511
  9.0 0.6 %collective-permute-done.1.refs_4_ = bf16[13,16,128]{2,1,0:T(8,128)(2,1)S(1)} collective-permute-done((bf16[13,16,128]{2,1,0:T(8,128)(2,1)S(1)}, bf16[13,16,128]{2,1,0:T(8,128)(2,1)S(1)}, u32[]{:S(2)}, u32[]{:S(2)}) %collective-permute-start.1) | collective-permute-done | bytes 53280 | tf_op jit(solution)/shard_map/ppermute | solution.py:511
  9.6 0.6 %shard_map.48 = (f32[72,24,128]{2,1,0:T(8,128)S(1)}, f32[43,16,64]{2,1,0:T(8,128)S(1)}, f32[29,16,32]{2,1,0:T(8,128)S(1)}, bf16[44,16,128]{2,1,0:T(8,128)(2,1)S(1)}, bf16[44,16,128]{2,1,0:T(8,128)(2,1)S(1)}) custom-call(bf16[64,16,128]{2,1,0:T(8,128)(2,1)S(1)} %get-tuple-element.25.refs_0_, f32[35,16,64]{2,1,0:T(8,128)S(1)} %get-tuple-element.26.refs_1_, ...), custom_call_target="tpu_custom_call" | custom-call | flops 100000000 | bytes 1000000 | tf_op jit(solution)/shard_map/pallas_call | solution.py:495
  10.2 1.9 %collective-permute-start.2 = (bf16[44,16,128]{2,1,0:T(8,128)(2,1)S(1)}, bf16[44,16,128]{2,1,0:T(8,128)(2,1)S(1)}, u32[]{:S(2)}, u32[]{:S(2)}) collective-permute-start(bf16[44,16,128]{2,1,0:T(8,128)(2,1)S(1)} %get-tuple-element.34), channel_id=1, source_target_pairs={{1,2},{3,4},{5,6},{2,1},{4,3},{6,5},{9,10},{11,12},{13,14},{10,9},... | collective-permute-start | bytes 540680 | tf_op jit(solution)/shard_map/ppermute | solution.py:511
  12.1 1.7 %collective-permute-start.3 = (bf16[44,16,128]{2,1,0:T(8,128)(2,1)S(1)}, bf16[44,16,128]{2,1,0:T(8,128)(2,1)S(1)}, u32[]{:S(2)}, u32[]{:S(2)}) collective-permute-start(bf16[44,16,128]{2,1,0:T(8,128)(2,1)S(1)} %get-tuple-element.35), channel_id=1, source_target_pairs={{0,1},{2,3},{4,5},{6,7},{1,0},{3,2},{5,4},{7,6},{8,9},{10,11},{12,... | collective-permute-start | bytes 540680 | tf_op jit(solution)/shard_map/ppermute | solution.py:511
  13.8 3.3 %shard_map.49.refs_4_.refs_3_ = f32[512,256]{1,0:T(8,128)S(1)} custom-call(f32[72,24,128]{2,1,0:T(8,128)S(1)} %get-tuple-element.36.refs_0_, bf16[9,9,128,128]{3,2,1,0:T(8,128)(2,1)S(1)} %get-tuple-element.31.refs_5_.refs_1_.refs_4_), custom_call_target="tpu_custom_call" | custom-call | flops 1000000000 | bytes 1000000 | tf_op jit(solution)/shard_map/pallas_call | solution.py:495
  17.2 0.0 collective-permute-done.2.refs_2_.refs_0_
  17.2 0.0 collective-permute-done.3.refs_3_.refs_1_
  17.2 0.5 %shard_map.50 = (f32[43,24,64]{2,1,0:T(8,128)S(1)}, f32[29,24,32]{2,1,0:T(8,128)S(1)}, bf16[8,16,128]{2,1,0:T(8,128)(2,1)S(1)}, bf16[8,16,128]{2,1,0:T(8,128)(2,1)S(1)}) custom-call(f32[43,16,64]{2,1,0:T(8,128)S(1)} %get-tuple-element.32.refs_0_, f32[29,16,32]{2,1,0:T(8,128)S(1)} %get-tuple-element.33.refs_1_, ...), custom_call_target="tpu_custom_call" | custom-call | flops 100000000 | bytes 1000000 | tf_op jit(solution)/shard_map/pallas_call | solution.py:495
  17.7 1.4 %collective-permute-start.4 = (bf16[8,16,128]{2,1,0:T(8,128)(2,1)S(1)}, bf16[8,16,128]{2,1,0:T(8,128)(2,1)S(1)}, u32[]{:S(2)}, u32[]{:S(2)}) collective-permute-start(bf16[8,16,128]{2,1,0:T(8,128)(2,1)S(1)} %get-tuple-element.38), channel_id=1, source_target_pairs={{0,2},{1,3},{4,6},{5,7},{2,0},{3,1},{6,4},{7,5},{8,10},{9,11},{12,... | collective-permute-start | bytes 98312 | tf_op jit(solution)/shard_map/ppermute | solution.py:511
  19.1 1.9 %collective-permute-start.5 = (bf16[8,16,128]{2,1,0:T(8,128)(2,1)S(1)}, bf16[8,16,128]{2,1,0:T(8,128)(2,1)S(1)}, u32[]{:S(2)}, u32[]{:S(2)}) collective-permute-start(bf16[8,16,128]{2,1,0:T(8,128)(2,1)S(1)} %get-tuple-element.39), channel_id=1, source_target_pairs={{2,4},{3,5},{4,2},{5,3},{10,12},{11,13},{12,10},{13,11},{18,20},{1... | collective-permute-start | bytes 98312 | tf_op jit(solution)/shard_map/ppermute | solution.py:511
  21.1 2.2 %shard_map.51 = (f32[64,8,256]{2,1,0:T(8,128)S(1)}, f32[280,256]{1,0:T(8,128)S(1)}) custom-call(bf16[44,16,128]{2,1,0:T(8,128)(2,1)S(1)} %collective-permute-done.2.refs_2_.refs_0_, bf16[44,16,128]{2,1,0:T(8,128)(2,1)S(1)} %collective-permute-done.3.refs_3_.refs_1_, f32[43,24,64]{2,1,0:T(8,128)S(1)} %get-tuple-element.41.refs_2_, ...), custom_call_target="tpu_custom_call" | custom-call | flops 1000000000 | bytes 1000000 | tf_op jit(solution)/shard_map/pallas_call | solution.py:495
  23.3 0.0 collective-permute-done.4.refs_1_
  23.3 1.6 %collective-permute-done.5.refs_2_ = bf16[8,16,128]{2,1,0:T(8,128)(2,1)S(1)} collective-permute-done((bf16[8,16,128]{2,1,0:T(8,128)(2,1)S(1)}, bf16[8,16,128]{2,1,0:T(8,128)(2,1)S(1)}, u32[]{:S(2)}, u32[]{:S(2)}) %collective-permute-start.5) | collective-permute-done | bytes 32800 | tf_op jit(solution)/shard_map/ppermute | solution.py:511
  24.9 2.3 %shard_map.52 = f32[64,16,128]{2,1,0:T(8,128)} custom-call(f32[29,24,32]{2,1,0:T(8,128)S(1)} %get-tuple-element.37.refs_0_, bf16[8,16,128]{2,1,0:T(8,128)(2,1)S(1)} %collective-permute-done.4.refs_1_, bf16[8,16,128]{2,1,0:T(8,128)(2,1)S(1)} %collective-permute-done.5.refs_2_, bf16[9,3,128,128]{3,2,1,0:T(8,128)(2,1)S(1)} %get-tuple-element.40.refs_3_, ...), custom_call_target="tpu_custom_call" | custom-call | flops 100000000 | bytes 1000000 | tf_op jit(solution)/shard_map/pallas_call | solution.py:495
Async XLA Ops:
  2.0 6.9 %collective-permute-start = (bf16[13,16,128]{2,1,0:T(8,128)(2,1)S(1)}, bf16[13,16,128]{2,1,0:T(8,128)(2,1)S(1)}, u32[]{:S(2)}, u32[]{:S(2)}) collective-permute-start(bf16[13,16,128]{2,1,0:T(8,128)(2,1)S(1)} %get-tuple-element.28), channel_id=1, source_target_pairs={{8,16},{16,8},{9,17},{17,9},{10,18},{18,10},{11,19},{19,11},{12,20... | collective-permute-start | bytes 159752 | tf_op jit(solution)/shard_map/ppermute | solution.py:511
  5.4 4.2 %collective-permute-start.1 = (bf16[13,16,128]{2,1,0:T(8,128)(2,1)S(1)}, bf16[13,16,128]{2,1,0:T(8,128)(2,1)S(1)}, u32[]{:S(2)}, u32[]{:S(2)}) collective-permute-start(bf16[13,16,128]{2,1,0:T(8,128)(2,1)S(1)} %get-tuple-element.29), channel_id=1, source_target_pairs={{0,8},{16,24},{8,0},{24,16},{1,9},{17,25},{9,1},{25,17},{2,10},{18... | collective-permute-start | bytes 159752 | tf_op jit(solution)/shard_map/ppermute | solution.py:511
  10.2 7.0 %collective-permute-start.2 = (bf16[44,16,128]{2,1,0:T(8,128)(2,1)S(1)}, bf16[44,16,128]{2,1,0:T(8,128)(2,1)S(1)}, u32[]{:S(2)}, u32[]{:S(2)}) collective-permute-start(bf16[44,16,128]{2,1,0:T(8,128)(2,1)S(1)} %get-tuple-element.34), channel_id=1, source_target_pairs={{1,2},{3,4},{5,6},{2,1},{4,3},{6,5},{9,10},{11,12},{13,14},{10,9},... | collective-permute-start | bytes 540680 | tf_op jit(solution)/shard_map/ppermute | solution.py:511
  12.1 5.1 %collective-permute-start.3 = (bf16[44,16,128]{2,1,0:T(8,128)(2,1)S(1)}, bf16[44,16,128]{2,1,0:T(8,128)(2,1)S(1)}, u32[]{:S(2)}, u32[]{:S(2)}) collective-permute-start(bf16[44,16,128]{2,1,0:T(8,128)(2,1)S(1)} %get-tuple-element.35), channel_id=1, source_target_pairs={{0,1},{2,3},{4,5},{6,7},{1,0},{3,2},{5,4},{7,6},{8,9},{10,11},{12,... | collective-permute-start | bytes 540680 | tf_op jit(solution)/shard_map/ppermute | solution.py:511
  17.7 5.6 %collective-permute-start.4 = (bf16[8,16,128]{2,1,0:T(8,128)(2,1)S(1)}, bf16[8,16,128]{2,1,0:T(8,128)(2,1)S(1)}, u32[]{:S(2)}, u32[]{:S(2)}) collective-permute-start(bf16[8,16,128]{2,1,0:T(8,128)(2,1)S(1)} %get-tuple-element.38), channel_id=1, source_target_pairs={{0,2},{1,3},{4,6},{5,7},{2,0},{3,1},{6,4},{7,5},{8,10},{9,11},{12,... | collective-permute-start | bytes 98312 | tf_op jit(solution)/shard_map/ppermute | solution.py:511
  19.1 5.8 %collective-permute-start.5 = (bf16[8,16,128]{2,1,0:T(8,128)(2,1)S(1)}, bf16[8,16,128]{2,1,0:T(8,128)(2,1)S(1)}, u32[]{:S(2)}, u32[]{:S(2)}) collective-permute-start(bf16[8,16,128]{2,1,0:T(8,128)(2,1)S(1)} %get-tuple-element.39), channel_id=1, source_target_pairs={{2,4},{3,5},{4,2},{5,3},{10,12},{11,13},{12,10},{13,11},{18,20},{1... | collective-permute-start | bytes 98312 | tf_op jit(solution)/shard_map/ppermute | solution.py:511

commit v5 on v4

--- a/solution.py
+++ b/solution.py
@@ -80,9 +80,30 @@
     return ((at >= 0) | (index > 0)) & ((at < cells) | (index < count - 1))
 
 
+def x_slots(count, rows):
+    half = (count + 1) // 2
+    y = slice(0, rows)
+    return [
+        (slice(0, half), rows, 0, slice(0, half), 0, y),
+        (slice(half, count), rows, HALF // 2, slice(0, count - half), 0, y),
+    ]
+
+
+def x_pair_slots(used, rows, frame):
+    top, rest = frame - used, rows - (frame - used)
+    slots = [(slice(8, 9), rows, HALF // 2, slice(3, 4), 0, slice(0, rows))]
+    for half in (0, 1):
+        left = half * HALF // 2
+        slots.append((slice(4 * half, 4 * half + 4), top, left, slice(0, 4), used, slice(0, top)))
+        for g in range(4):
+            x = 4 * half + g
+            slots.append((slice(x, x + 1), rest, left, slice(4, 5), rest * g, slice(top, rows)))
+    return slots
+
+
 def spread_kernel(counts, *refs):
     outside, (first_out, second_out, fine_own, mid_own, coarse_own, lines) = refs[0:4], refs[4:10]
-    (even_pad, odd_pad, crs, charges), raws, sems = refs[10:14], refs[14:17], refs[17]
+    (even_pad, odd_pad, crs, charges, msg), raws, sems = refs[10:15], refs[15:18], refs[18]
     copies = [
         pltpu.make_async_copy(source, target, sems.at[i])
         for i, (source, target) in enumerate(zip(outside, (charges,) + raws))
@@ -92,6 +113,7 @@
     even_pad[...] = jnp.zeros_like(even_pad)
     odd_pad[...] = jnp.zeros_like(odd_pad)
     lines[...] = jnp.zeros_like(lines)
+    msg[...] = jnp.zeros_like(msg)
     copies[0].wait()
     fine_own[...] = charges[...].astype(BF16)
     gx, gy = lax.axis_index("gx"), lax.axis_index("gy")
@@ -128,8 +150,13 @@
     coarse_own[...] = coarse
     def pack(out, fine_at, mid_at, coarse_at):
         out[0:4] = charges[fine_at : fine_at + 4].astype(BF16)
-        out[4:8] = two_halves(mid_own[mid_at : mid_at + 7]).astype(BF16)
-        out[8:13] = two_halves(pair_lanes(coarse_own[coarse_at : coarse_at + 9])).astype(BF16)
+        for part, rows, left, tile, top, y in x_slots(7, my + 3):
+            value = mid_own[mid_at + part.start : mid_at + part.stop, y, :]
+            msg[tile, top : top + rows, left : left + mz] = value
+        for part, rows, left, tile, top, y in x_pair_slots(my + 3, cy + 5, frame):
+            value = coarse_own[coarse_at + part.start : coarse_at + part.stop, y, :]
+            msg[tile, top : top + rows, left : left + 2 * cz] = pair_lanes(value)
+        out[4:9] = msg[...].astype(BF16)
 
     flag = up_first("gx", 1, 1)
 
@@ -176,7 +203,16 @@
     return parts
 
 
-def join_x_kernel(charges, mid_own, coarse_own, first_in, second_in, fine_x, mid_x, coarse_x, first_out, second_out, buf):
+def ninth_rows(rows, count, at, lanes):
+    parts = []
+    for part, first, last, top, left in quarters(rows, at, lanes):
+        last = min(last, count)
+        if first < last:
+            parts.append((slice(part.start, part.start + last - first), first, last, top + 7, left))
+    return parts
+
+
+def join_x_kernel(charges, mid_own, coarse_own, first_in, second_in, fine_x, mid_x, coarse_x, first_out, second_out, buf, got):
     before, after = by_order(up_first("gx", 1, 1), *(v[...].astype(F32) for v in (first_in, second_in)))
     cells_x, cells_y, _ = charges.shape
     mx, cx = cells_x // 2, cells_x // 4
@@ -189,20 +225,16 @@
     fine_x[0:4, own, :] = before[0:4]
     fine_x[4 : 4 + cells_x, own, :] = charges[...].astype(F32)
     fine_x[4 + cells_x : rows_x, own, :] = after[0:4]
-    low, high = (from_halves(m[4:8], 7) for m in (before, after))
-    mid = (
-        rows_at(mid_own[...], -1, -5, mx + 11)
-        + rows_at(low, -5, -5, mx + 11)
-        + rows_at(high, mx - 1, -5, mx + 11)
-    )
-    mid_x[...] = mid
-    low, high = (from_halves(m[8:13], 9) for m in (before, after))
-    coarse = (
-        rows_at(coarse_own[...], -2, -6, cx + 13)
-        + rows_at(unpair(low, cz), -6, -6, cx + 13)
-        + rows_at(unpair(high, cz), cx - 2, -6, cx + 13)
-    )
-    coarse_x[...] = coarse
+    got[0], got[1] = before[4:9], after[4:9]
+    mid_x[...] = rows_at(mid_own[...], -1, -5, mx + 11)
+    coarse_x[...] = rows_at(coarse_own[...], -2, -6, cx + 13)
+    for side, mid_at, coarse_at in ((0, 0, 0), (1, mx + 4, cx + 4)):
+        for part, rows, left, tile, top, y in x_slots(7, my + 3):
+            at = slice(mid_at + part.start, mid_at + part.stop)
+            mid_x[at, y, :] += got[side, tile, top : top + rows, left : left + mz]
+        for part, rows, left, tile, top, y in x_pair_slots(my + 3, cells_y // 4 + 5, cells_y):
+            at = slice(coarse_at + part.start, coarse_at + part.stop)
+            coarse_x[at, y, :] += unpair(got[side, tile, top : top + rows, left : left + 2 * cz], cz)
     buf[...] = jnp.zeros_like(buf)
 
     def pack(out, fine_at, mid_at):
@@ -211,8 +243,12 @@
         at = (cells_x + 8) // 4
         for part, first, last, top, left in quarters(mx + 11, at, mz):
             buf[part, top : top + 7, left : left + mz] = mid_x[first:last, mid_at : mid_at + 7, :]
+        packed = pair_lanes(coarse_x[:, 0:9, :])
+        for part, first, last, top, left in ninth_rows(mx + 11, cx + 13, at, 2 * cz):
+            buf[part, top : top + 1, left : left + 2 * cz] = packed[first:last, 8:9, :]
         at += -(-(mx + 11) // 4)
-        buf[at:, 0:9, :] = two_halves(pair_lanes(coarse_x[:, 0:9, :]))
+        for part, first, last, top, left in quarters(cx + 13, at, 2 * cz):
+            buf[part, top : top + 8, left : left + 2 * cz] = packed[first:last, 0:8, :]
         out[...] = buf[...].astype(BF16)
 
     flag = up_first("gy", 1, 1)
@@ -228,7 +264,7 @@
         pack(second_out, cells_y, my - 4)
 
 
-def join_y_kernel(at, mid_x, coarse_x, first_in, second_in, mid_xy, coarse_xy, first_out, second_out, low, high, buf, side):
+def join_y_kernel(at, mid_x, coarse_x, first_in, second_in, mid_xy, coarse_xy, first_out, second_out, low, high, buf, side, from_low, from_high):
     my, cy = mid_x.shape[1] // 2, mid_x.shape[1] // 4
     rows_m, rows_c = mid_x.shape[0], coarse_x.shape[0]
     mz, cz = mid_x.shape[2], coarse_x.shape[2]
@@ -238,13 +274,17 @@
     for part, first, last, top, left in quarters(rows_m, at, mz):
         mid_xy[first:last, 0:7, :] += low[part, top : top + 7, left : left + mz]
         mid_xy[first:last, 4 + my : 11 + my, :] += high[part, top : top + 7, left : left + mz]
+    ninths = ninth_rows(rows_m, rows_c, at, 2 * cz)
     at += -(-rows_m // 4)
-    from_low = unpair(from_halves(low[at:, 0:9, :], rows_c), cz)
-    from_high = unpair(from_halves(high[at:, 0:9, :], rows_c), cz)
+    for source, target in ((low, from_low), (high, from_high)):
+        for part, first, last, top, left in ninths:
+            target[first:last, 8:9, :] = unpair(source[part, top : top + 1, left : left + 2 * cz], cz)
+        for part, first, last, top, left in quarters(rows_c, at, 2 * cz):
+            target[first:last, 0:8, :] = unpair(source[part, top : top + 8, left : left + 2 * cz], cz)
     side[...] = jnp.zeros_like(side)
     side[:, 4 : 9 + cy, :] = coarse_x[:, 0 : cy + 5, :]
     coarse_xy[...] = side[...]
-    coarse_xy[:, 0:9, :] += from_low
+    coarse_xy[:, 0:9, :] += from_low[:, 0:9, :]
     buf[...] = jnp.zeros_like(buf)
 
     def pack(rows, out):
@@ -254,8 +294,8 @@
         out[...] = buf[...].astype(BF16)
 
     up = coarse_xy[:, 4 + cy : 9 + cy, :]
-    coarse_xy[:, 4 + cy : 13 + cy, :] += from_high
-    side[:, 4 + cy : 13 + cy, :] += from_high
+    coarse_xy[:, 4 + cy : 13 + cy, :] += from_high[:, 0:9, :]
+    side[:, 4 + cy : 13 + cy, :] += from_high[:, 0:9, :]
     down = side[:, 4:9, :]
     flag = up_first("gy", 2, 0)
     pack(jnp.where(flag, up, down), first_out)
@@ -526,7 +566,7 @@
     mx, mz, cx, cz = cells_x // 2, cells_z // 2, cells_x // 4, cells_z // 4
     frame = cells_y
     lines = ((27, 16, HALF), F32)
-    message = ((13, frame, cells_z), BF16)
+    message = ((9, frame, cells_z), BF16)
     first, second, fine_own, mid_own, coarse_own, lines = call(
         functools.partial(spread_kernel, counts),
         [message, message, (charges.shape, BF16), ((mx + 3, frame, mz), F32), ((cx + 5, frame, cz), F32), lines],
@@ -536,6 +576,7 @@
             ((mx + 3, frame + 24, mz), F32),
             ((cx + 5, frame, mz), F32),
             (charges.shape, F32),
+            ((5, frame, cells_z), F32),
         ]
         + [((9, 9, 9), BF16)] * 3,
         space=pltpu.HBM,
@@ -544,7 +585,7 @@
     )
     first, second = swap(first, second, "gx", 1, nx, 1)
     fine_w, mid_w, coarse_w = bands(lines, 0, ((cells_z, 5), (mz, 3), (cz, 2)))
-    rows = (cells_x + 8) // 4 + (mx + 14) // 4 + (cx + 14) // 2
+    rows = (cells_x + 8) // 4 + (mx + 14) // 4 + (cx + 16) // 4
     packed = ((rows, frame, cells_z), BF16)
     fine_x, mid_x, coarse_x, first, second = call(
         join_x_kernel,
@@ -556,7 +597,7 @@
             packed,
         ],
         [fine_own, mid_own, coarse_own, first, second],
-        [((rows, frame, cells_z), F32)],
+        [((rows, frame, cells_z), F32), ((2, 5, frame, cells_z), F32)],
         after=(fine_w,),
     )
     first, second = swap(first, second, "gy", 1, ny, 1)
@@ -583,6 +624,8 @@
             ((rows, frame, cells_z), F32),
             ((half, frame, cells_z), F32),
             ((cx + 13, frame + 8, cz), F32),
+            ((cx + 13, frame, cz), F32),
+            ((cx + 13, frame, cz), F32),
         ],
         after=(own_acc,),
     )

time: 27.5 us -> 27.1 us (0.985)
  starting transfers between devices: 10.4 us -> 10.1 us
    ppermute x6, starting transfers between devices: 10.4 us -> 10.1 us  [swap(): received.append(lax.ppermute(message, axis, pairs))]
where the time goes in v5:
time: 27.1 us; the launch traced here: 26.9 us
  Pallas kernels  13.1 us (48%)
  starting transfers between devices  10.1 us (37%)
  waiting for transfers between devices  3.6 us (13%)
    pallas_call x7, Pallas kernels, call(): pl.pallas_call(body, out_shape=[pltpu.VMEM(s, d) for s, d in outs] if vme...  13.1 us
    ppermute x6, starting transfers between devices, swap(): received.append(lax.ppermute(message, axis, pairs))  10.1 us
    ppermute x6, waiting for transfers between devices, swap(): received.append(lax.ppermute(message, axis, pairs))  3.6 us
  transfers between devices with their start and end apart: 6, of which 3 were waited for; matrix products, arithmetic and copies ran while one was open for 0% of the time, Pallas kernels for 28%

profile of v5, /device:TPU:20, one launch (start us, length us, event | category | flops | bytes accessed | tf_op | source)
XLA Modules:
  0.0 26.9 jit_solution(1293609206528080060)
XLA Ops:
  0.0 2.0 %shard_map.46 = (bf16[9,16,128]{2,1,0:T(8,128)(2,1)S(1)}, bf16[9,16,128]{2,1,0:T(8,128)(2,1)S(1)}, bf16[64,16,128]{2,1,0:T(8,128)(2,1)S(1)}, f32[35,16,64]{2,1,0...) custom-call(f32[64,16,128]{2,1,0:T(8,128)} %refs_0_.1, bf16[9,9,9]{2,1,0:T(8,128)(2,1)} %refs_1_.1, ...), custom_call_target="tpu_custom_call" | custom-call | flops 100000000 | bytes 1000000 | tf_op jit(solution)/shard_map/pallas_call | solution.py:535
  2.0 3.4 %collective-permute-start = (bf16[9,16,128]{2,1,0:T(8,128)(2,1)S(1)}, bf16[9,16,128]{2,1,0:T(8,128)(2,1)S(1)}, u32[]{:S(2)}, u32[]{:S(2)}) collective-permute-start(bf16[9,16,128]{2,1,0:T(8,128)(2,1)S(1)} %get-tuple-element.28), channel_id=1, source_target_pairs={{8,16},{16,8},{9,17},{17,9},{10,18},{18,10},{11,19},{19,11},{12,20... | collective-permute-start | bytes 110600 | tf_op jit(solution)/shard_map/ppermute | solution.py:551
  5.4 0.1 collective-permute-start.1
  5.5 2.0 %shard_map.47 = (bf16[9,9,128,128]{3,2,1,0:T(8,128)(2,1)S(1)}, bf16[9,5,128,128]{3,2,1,0:T(8,128)(2,1)S(1)}, bf16[9,3,128,128]{3,2,1,0:T(8,128)(2,1)S(1)}) custom-call(f32[27,16,128]{2,1,0:T(8,128)S(1)} %get-tuple-element.30.refs_0_), custom_call_target="tpu_custom_call" | custom-call | flops 1000000000 | bytes 1000000 | tf_op jit(solution)/shard_map/pallas_call | solution.py:535
  7.5 1.3 %collective-permute-done.refs_3_ = bf16[9,16,128]{2,1,0:T(8,128)(2,1)S(1)} collective-permute-done((bf16[9,16,128]{2,1,0:T(8,128)(2,1)S(1)}, bf16[9,16,128]{2,1,0:T(8,128)(2,1)S(1)}, u32[]{:S(2)}, u32[]{:S(2)}) %collective-permute-start) | collective-permute-done | bytes 36896 | tf_op jit(solution)/shard_map/ppermute | solution.py:551
  8.8 0.6 %collective-permute-done.1.refs_4_ = bf16[9,16,128]{2,1,0:T(8,128)(2,1)S(1)} collective-permute-done((bf16[9,16,128]{2,1,0:T(8,128)(2,1)S(1)}, bf16[9,16,128]{2,1,0:T(8,128)(2,1)S(1)}, u32[]{:S(2)}, u32[]{:S(2)}) %collective-permute-start.1) | collective-permute-done | bytes 36896 | tf_op jit(solution)/shard_map/ppermute | solution.py:551
  9.4 0.6 %shard_map.48 = (f32[72,24,128]{2,1,0:T(8,128)S(1)}, f32[43,16,64]{2,1,0:T(8,128)S(1)}, f32[29,16,32]{2,1,0:T(8,128)S(1)}, bf16[37,16,128]{2,1,0:T(8,128)(2,1)S(1)}, bf16[37,16,128]{2,1,0:T(8,128)(2,1)S(1)}) custom-call(bf16[64,16,128]{2,1,0:T(8,128)(2,1)S(1)} %get-tuple-element.25.refs_0_, f32[35,16,64]{2,1,0:T(8,128)S(1)} %get-tuple-element.26.refs_1_, ...), custom_call_target="tpu_custom_call" | custom-call | flops 100000000 | bytes 1000000 | tf_op jit(solution)/shard_map/pallas_call | solution.py:535
  10.0 1.9 %collective-permute-start.2 = (bf16[37,16,128]{2,1,0:T(8,128)(2,1)S(1)}, bf16[37,16,128]{2,1,0:T(8,128)(2,1)S(1)}, u32[]{:S(2)}, u32[]{:S(2)}) collective-permute-start(bf16[37,16,128]{2,1,0:T(8,128)(2,1)S(1)} %get-tuple-element.34), channel_id=1, source_target_pairs={{1,2},{3,4},{5,6},{2,1},{4,3},{6,5},{9,10},{11,12},{13,14},{10,9},... | collective-permute-start | bytes 454664 | tf_op jit(solution)/shard_map/ppermute | solution.py:551
  12.0 1.7 %collective-permute-start.3 = (bf16[37,16,128]{2,1,0:T(8,128)(2,1)S(1)}, bf16[37,16,128]{2,1,0:T(8,128)(2,1)S(1)}, u32[]{:S(2)}, u32[]{:S(2)}) collective-permute-start(bf16[37,16,128]{2,1,0:T(8,128)(2,1)S(1)} %get-tuple-element.35), channel_id=1, source_target_pairs={{0,1},{2,3},{4,5},{6,7},{1,0},{3,2},{5,4},{7,6},{8,9},{10,11},{12,... | collective-permute-start | bytes 454664 | tf_op jit(solution)/shard_map/ppermute | solution.py:551
  13.7 3.3 %shard_map.49.refs_4_.refs_3_ = f32[512,256]{1,0:T(8,128)S(1)} custom-call(f32[72,24,128]{2,1,0:T(8,128)S(1)} %get-tuple-element.36.refs_0_, bf16[9,9,128,128]{3,2,1,0:T(8,128)(2,1)S(1)} %get-tuple-element.31.refs_5_.refs_1_.refs_4_), custom_call_target="tpu_custom_call" | custom-call | flops 1000000000 | bytes 1000000 | tf_op jit(solution)/shard_map/pallas_call | solution.py:535
  17.0 0.0 collective-permute-done.2.refs_2_.refs_0_
  17.1 0.0 collective-permute-done.3.refs_3_.refs_1_
  17.1 0.6 %shard_map.50 = (f32[43,24,64]{2,1,0:T(8,128)S(1)}, f32[29,24,32]{2,1,0:T(8,128)S(1)}, bf16[8,16,128]{2,1,0:T(8,128)(2,1)S(1)}, bf16[8,16,128]{2,1,0:T(8,128)(2,1)S(1)}) custom-call(f32[43,16,64]{2,1,0:T(8,128)S(1)} %get-tuple-element.32.refs_0_, f32[29,16,32]{2,1,0:T(8,128)S(1)} %get-tuple-element.33.refs_1_, ...), custom_call_target="tpu_custom_call" | custom-call | flops 100000000 | bytes 1000000 | tf_op jit(solution)/shard_map/pallas_call | solution.py:535
  17.7 1.1 %collective-permute-start.4 = (bf16[8,16,128]{2,1,0:T(8,128)(2,1)S(1)}, bf16[8,16,128]{2,1,0:T(8,128)(2,1)S(1)}, u32[]{:S(2)}, u32[]{:S(2)}) collective-permute-start(bf16[8,16,128]{2,1,0:T(8,128)(2,1)S(1)} %get-tuple-element.38), channel_id=1, source_target_pairs={{0,2},{1,3},{4,6},{5,7},{2,0},{3,1},{6,4},{7,5},{8,10},{9,11},{12,... | collective-permute-start | bytes 98312 | tf_op jit(solution)/shard_map/ppermute | solution.py:551
  18.8 1.9 %collective-permute-start.5 = (bf16[8,16,128]{2,1,0:T(8,128)(2,1)S(1)}, bf16[8,16,128]{2,1,0:T(8,128)(2,1)S(1)}, u32[]{:S(2)}, u32[]{:S(2)}) collective-permute-start(bf16[8,16,128]{2,1,0:T(8,128)(2,1)S(1)} %get-tuple-element.39), channel_id=1, source_target_pairs={{2,4},{3,5},{4,2},{5,3},{10,12},{11,13},{12,10},{13,11},{18,20},{1... | collective-permute-start | bytes 98312 | tf_op jit(solution)/shard_map/ppermute | solution.py:551
  20.7 2.2 %shard_map.51 = (f32[64,8,256]{2,1,0:T(8,128)S(1)}, f32[280,256]{1,0:T(8,128)S(1)}) custom-call(bf16[37,16,128]{2,1,0:T(8,128)(2,1)S(1)} %collective-permute-done.2.refs_2_.refs_0_, bf16[37,16,128]{2,1,0:T(8,128)(2,1)S(1)} %collective-permute-done.3.refs_3_.refs_1_, f32[43,24,64]{2,1,0:T(8,128)S(1)} %get-tuple-element.41.refs_2_, ...), custom_call_target="tpu_custom_call" | custom-call | flops 1000000000 | bytes 1000000 | tf_op jit(solution)/shard_map/pallas_call | solution.py:535
  23.0 0.0 collective-permute-done.4.refs_1_
  23.0 1.6 %collective-permute-done.5.refs_2_ = bf16[8,16,128]{2,1,0:T(8,128)(2,1)S(1)} collective-permute-done((bf16[8,16,128]{2,1,0:T(8,128)(2,1)S(1)}, bf16[8,16,128]{2,1,0:T(8,128)(2,1)S(1)}, u32[]{:S(2)}, u32[]{:S(2)}) %collective-permute-start.5) | collective-permute-done | bytes 32800 | tf_op jit(solution)/shard_map/ppermute | solution.py:551
  24.6 2.3 %shard_map.52 = f32[64,16,128]{2,1,0:T(8,128)} custom-call(f32[29,24,32]{2,1,0:T(8,128)S(1)} %get-tuple-element.37.refs_0_, bf16[8,16,128]{2,1,0:T(8,128)(2,1)S(1)} %collective-permute-done.4.refs_1_, bf16[8,16,128]{2,1,0:T(8,128)(2,1)S(1)} %collective-permute-done.5.refs_2_, bf16[9,3,128,128]{3,2,1,0:T(8,128)(2,1)S(1)} %get-tuple-element.40.refs_3_, ...), custom_call_target="tpu_custom_call" | custom-call | flops 100000000 | bytes 1000000 | tf_op jit(solution)/shard_map/pallas_call | solution.py:535
Async XLA Ops:
  2.0 6.8 %collective-permute-start = (bf16[9,16,128]{2,1,0:T(8,128)(2,1)S(1)}, bf16[9,16,128]{2,1,0:T(8,128)(2,1)S(1)}, u32[]{:S(2)}, u32[]{:S(2)}) collective-permute-start(bf16[9,16,128]{2,1,0:T(8,128)(2,1)S(1)} %get-tuple-element.28), channel_id=1, source_target_pairs={{8,16},{16,8},{9,17},{17,9},{10,18},{18,10},{11,19},{19,11},{12,20... | collective-permute-start | bytes 110600 | tf_op jit(solution)/shard_map/ppermute | solution.py:551
  5.4 4.0 %collective-permute-start.1 = (bf16[9,16,128]{2,1,0:T(8,128)(2,1)S(1)}, bf16[9,16,128]{2,1,0:T(8,128)(2,1)S(1)}, u32[]{:S(2)}, u32[]{:S(2)}) collective-permute-start(bf16[9,16,128]{2,1,0:T(8,128)(2,1)S(1)} %get-tuple-element.29), channel_id=1, source_target_pairs={{0,8},{16,24},{8,0},{24,16},{1,9},{17,25},{9,1},{25,17},{2,10},{18... | collective-permute-start | bytes 110600 | tf_op jit(solution)/shard_map/ppermute | solution.py:551
  10.0 7.0 %collective-permute-start.2 = (bf16[37,16,128]{2,1,0:T(8,128)(2,1)S(1)}, bf16[37,16,128]{2,1,0:T(8,128)(2,1)S(1)}, u32[]{:S(2)}, u32[]{:S(2)}) collective-permute-start(bf16[37,16,128]{2,1,0:T(8,128)(2,1)S(1)} %get-tuple-element.34), channel_id=1, source_target_pairs={{1,2},{3,4},{5,6},{2,1},{4,3},{6,5},{9,10},{11,12},{13,14},{10,9},... | collective-permute-start | bytes 454664 | tf_op jit(solution)/shard_map/ppermute | solution.py:551
  12.0 5.1 %collective-permute-start.3 = (bf16[37,16,128]{2,1,0:T(8,128)(2,1)S(1)}, bf16[37,16,128]{2,1,0:T(8,128)(2,1)S(1)}, u32[]{:S(2)}, u32[]{:S(2)}) collective-permute-start(bf16[37,16,128]{2,1,0:T(8,128)(2,1)S(1)} %get-tuple-element.35), channel_id=1, source_target_pairs={{0,1},{2,3},{4,5},{6,7},{1,0},{3,2},{5,4},{7,6},{8,9},{10,11},{12,... | collective-permute-start | bytes 454664 | tf_op jit(solution)/shard_map/ppermute | solution.py:551
  17.7 5.3 %collective-permute-start.4 = (bf16[8,16,128]{2,1,0:T(8,128)(2,1)S(1)}, bf16[8,16,128]{2,1,0:T(8,128)(2,1)S(1)}, u32[]{:S(2)}, u32[]{:S(2)}) collective-permute-start(bf16[8,16,128]{2,1,0:T(8,128)(2,1)S(1)} %get-tuple-element.38), channel_id=1, source_target_pairs={{0,2},{1,3},{4,6},{5,7},{2,0},{3,1},{6,4},{7,5},{8,10},{9,11},{12,... | collective-permute-start | bytes 98312 | tf_op jit(solution)/shard_map/ppermute | solution.py:551
  18.8 5.8 %collective-permute-start.5 = (bf16[8,16,128]{2,1,0:T(8,128)(2,1)S(1)}, bf16[8,16,128]{2,1,0:T(8,128)(2,1)S(1)}, u32[]{:S(2)}, u32[]{:S(2)}) collective-permute-start(bf16[8,16,128]{2,1,0:T(8,128)(2,1)S(1)} %get-tuple-element.39), channel_id=1, source_target_pairs={{2,4},{3,5},{4,2},{5,3},{10,12},{11,13},{12,10},{13,11},{18,20},{1... | collective-permute-start | bytes 98312 | tf_op jit(solution)/shard_map/ppermute | solution.py:551

commit v6 on v5

--- a/solution.py
+++ b/solution.py
@@ -25,10 +25,8 @@
 
 
 def exact_dot(v, matrix):
-    high, low = split_pair(v)
-    return jnp.dot(high.astype(BF16), matrix, preferred_element_type=F32) + jnp.dot(
-        low.astype(BF16), matrix, preferred_element_type=F32
-    )
+    pair = pair_lanes(v).astype(BF16)
+    return jnp.dot(pair, jnp.concatenate([matrix, matrix], axis=0), preferred_element_type=F32)
 
 
 def transfer_matrix(fine, coarse, transpose):
@@ -264,16 +262,14 @@
         pack(second_out, cells_y, my - 4)
 
 
-def join_y_kernel(at, mid_x, coarse_x, first_in, second_in, mid_xy, coarse_xy, first_out, second_out, low, high, buf, side, from_low, from_high):
-    my, cy = mid_x.shape[1] // 2, mid_x.shape[1] // 4
-    rows_m, rows_c = mid_x.shape[0], coarse_x.shape[0]
-    mz, cz = mid_x.shape[2], coarse_x.shape[2]
-    low[...], high[...] = by_order(up_first("gy", 1, 1), first_in[...].astype(F32), second_in[...].astype(F32))
-    mid_xy[...] = jnp.zeros_like(mid_xy)
-    mid_xy[:, 4 : 7 + my, :] = mid_x[:, 0 : my + 3, :]
-    for part, first, last, top, left in quarters(rows_m, at, mz):
-        mid_xy[first:last, 0:7, :] += low[part, top : top + 7, left : left + mz]
-        mid_xy[first:last, 4 + my : 11 + my, :] += high[part, top : top + 7, left : left + mz]
+def join_y_kernel(
+    at, rows_m, coarse_x, first_in, second_in, coarse_xy, first_out, second_out,
+    low, high, buf, side, from_low, from_high,
+):
+    cy = coarse_x.shape[1] // 4
+    rows_c, cz = coarse_x.shape[0], coarse_x.shape[2]
+    flag = up_first("gy", 1, 1)
+    low[at:], high[at:] = by_order(flag, first_in[at:].astype(F32), second_in[at:].astype(F32))
     ninths = ninth_rows(rows_m, rows_c, at, 2 * cz)
     at += -(-rows_m // 4)
     for source, target in ((low, from_low), (high, from_high)):
@@ -407,7 +403,22 @@
     return weights_of(blocks, dx)[group * WIDE : (group + 1) * WIDE]
 
 
-def rim_kernel(first_in, second_in, mid_xy, own, fine_w, mid_w, fine_acc, mid_acc, rim, stage_f, lhs_f, stage, mid_lhs, sums):
+def join_mid(first_in, second_in, mid_x, mid_xy, got):
+    my, mz = mid_x.shape[1] // 2, mid_x.shape[2]
+    count = got.shape[1]
+    at = first_in.shape[0] - count
+    got[0], got[1] = by_order(up_first("gy", 1, 1), *(v[at:].astype(F32) for v in (first_in, second_in)))
+    mid_xy[...] = jnp.zeros_like(mid_xy)
+    mid_xy[:, 4 : 7 + my, :] = mid_x[:, 0 : my + 3, :]
+    for part, first, last, top, left in quarters(mid_x.shape[0], 0, mz):
+        mid_xy[first:last, 0:7, :] += got[0, part, top : top + 7, left : left + mz]
+        mid_xy[first:last, 4 + my : 11 + my, :] += got[1, part, top : top + 7, left : left + mz]
+
+
+def rim_kernel(
+    first_in, second_in, mid_x, own, fine_w, mid_w, fine_acc, mid_acc,
+    rim, stage_f, lhs_f, stage, mid_lhs, sums, mid_xy, got,
+):
     cells_x = own.shape[0] // 8
     quarter = cells_x // 4
     tiles = rim.shape[1]
@@ -432,6 +443,7 @@
             rows = lhs_f[side, dx % 2, start : start + n, :]
             part = jnp.dot(rows, group_weights(fine_w, dx, group), preferred_element_type=F32)
             sums[i] = part if dx == 0 else sums[i] + part
+    join_mid(first_in, second_in, mid_x, mid_xy, got)
     rows = mid_xy.shape[0]
     gather_staged(mid_xy, rows, 4, 3, mid_xy.shape[2], stage, mid_lhs)
     convolve(mid_lhs, mid_w, rows - 8, mid_acc)
@@ -610,15 +622,14 @@
     )
     half = (cx + 16) // 4
     message = ((half, frame, cells_z), BF16)
-    mid_xy, coarse_xy, last_first, last_second = call(
-        functools.partial(join_y_kernel, (cells_x + 8) // 4),
+    coarse_xy, last_first, last_second = call(
+        functools.partial(join_y_kernel, (cells_x + 8) // 4, mx + 11),
         [
-            ((mx + 11, frame + 8, mz), F32),
             ((cx + 13, frame + 8, cz), F32),
             message,
             message,
         ],
-        [mid_x, coarse_x, first, second],
+        [coarse_x, first, second],
         [
             ((rows, frame, cells_z), F32),
             ((rows, frame, cells_z), F32),
@@ -634,7 +645,7 @@
     fine_acc, mid_acc = call(
         rim_kernel,
         [((cells_x, 8, WIDE), F32), (((mx + 3) * 8, WIDE), F32)],
-        [first, second, mid_xy, own_acc, fine_w, mid_w],
+        [first, second, mid_x, own_acc, fine_w, mid_w],
         [
             ((2, (cells_x + 8) // 4, frame, cells_z), F32),
             ((2, quarter + 8, 8, WIDE), F32),
@@ -642,6 +653,8 @@
             ((mx + 11, 16, WIDE), F32),
             ((2, (mx + 12) * 8, 3 * WIDE), BF16),
             ((4, quarter * 8, WIDE), F32),
+            ((mx + 11, frame + 8, mz), F32),
+            ((2, rows - (cells_x + 8) // 4, frame, cells_z), F32),
         ],
         flops=10**9,
     )

time: 27.1 us -> 27.1 us (level)
  transfers between devices with their start and end apart: 6 -> 6, of which waited for: 3 -> 3; matrix products, arithmetic and copies ran while one was open for 0% -> 0% of each run, Pallas kernels for 28% -> 29%
where the time goes in v6:
time: 27.1 us; the launch traced here: 26.7 us
  Pallas kernels  13 us (48%)
  starting transfers between devices  10.1 us (37%)
  waiting for transfers between devices  3.39 us (13%)
    pallas_call x7, Pallas kernels, call(): pl.pallas_call(body, out_shape=[pltpu.VMEM(s, d) for s, d in outs] if vme...  13 us
    ppermute x6, starting transfers between devices, swap(): received.append(lax.ppermute(message, axis, pairs))  10.1 us
    ppermute x6, waiting for transfers between devices, swap(): received.append(lax.ppermute(message, axis, pairs))  3.39 us
  transfers between devices with their start and end apart: 6, of which 3 were waited for; matrix products, arithmetic and copies ran while one was open for 0% of the time, Pallas kernels for 29%

profile of v6, /device:TPU:20, one launch (start us, length us, event | category | flops | bytes accessed | tf_op | source)
XLA Modules:
  0.0 26.7 jit_solution(14529533189401033806)
XLA Ops:
  0.0 1.9 %shard_map.46 = (bf16[9,16,128]{2,1,0:T(8,128)(2,1)S(1)}, bf16[9,16,128]{2,1,0:T(8,128)(2,1)S(1)}, bf16[64,16,128]{2,1,0:T(8,128)(2,1)S(1)}, f32[35,16,64]{2,1,0...) custom-call(f32[64,16,128]{2,1,0:T(8,128)} %refs_0_.1, bf16[9,9,9]{2,1,0:T(8,128)(2,1)} %refs_1_.1, ...), custom_call_target="tpu_custom_call" | custom-call | flops 100000000 | bytes 1000000 | tf_op jit(solution)/shard_map/pallas_call | solution.py:547
  1.9 3.4 %collective-permute-start = (bf16[9,16,128]{2,1,0:T(8,128)(2,1)S(1)}, bf16[9,16,128]{2,1,0:T(8,128)(2,1)S(1)}, u32[]{:S(2)}, u32[]{:S(2)}) collective-permute-start(bf16[9,16,128]{2,1,0:T(8,128)(2,1)S(1)} %get-tuple-element.27), channel_id=1, source_target_pairs={{8,16},{16,8},{9,17},{17,9},{10,18},{18,10},{11,19},{19,11},{12,20... | collective-permute-start | bytes 110600 | tf_op jit(solution)/shard_map/ppermute | solution.py:563
  5.3 0.1 collective-permute-start.1
  5.3 2.0 %shard_map.47 = (bf16[9,9,128,128]{3,2,1,0:T(8,128)(2,1)S(1)}, bf16[9,5,128,128]{3,2,1,0:T(8,128)(2,1)S(1)}, bf16[9,3,128,128]{3,2,1,0:T(8,128)(2,1)S(1)}) custom-call(f32[27,16,128]{2,1,0:T(8,128)S(1)} %get-tuple-element.29.refs_0_), custom_call_target="tpu_custom_call" | custom-call | flops 1000000000 | bytes 1000000 | tf_op jit(solution)/shard_map/pallas_call | solution.py:547
  7.3 1.3 %collective-permute-done.refs_3_ = bf16[9,16,128]{2,1,0:T(8,128)(2,1)S(1)} collective-permute-done((bf16[9,16,128]{2,1,0:T(8,128)(2,1)S(1)}, bf16[9,16,128]{2,1,0:T(8,128)(2,1)S(1)}, u32[]{:S(2)}, u32[]{:S(2)}) %collective-permute-start) | collective-permute-done | bytes 36896 | tf_op jit(solution)/shard_map/ppermute | solution.py:563
  8.7 0.6 %collective-permute-done.1.refs_4_ = bf16[9,16,128]{2,1,0:T(8,128)(2,1)S(1)} collective-permute-done((bf16[9,16,128]{2,1,0:T(8,128)(2,1)S(1)}, bf16[9,16,128]{2,1,0:T(8,128)(2,1)S(1)}, u32[]{:S(2)}, u32[]{:S(2)}) %collective-permute-start.1) | collective-permute-done | bytes 36896 | tf_op jit(solution)/shard_map/ppermute | solution.py:563
  9.3 0.6 %shard_map.48 = (f32[72,24,128]{2,1,0:T(8,128)S(1)}, f32[43,16,64]{2,1,0:T(8,128)S(1)}, f32[29,16,32]{2,1,0:T(8,128)S(1)}, bf16[37,16,128]{2,1,0:T(8,128)(2,1)S(1)}, bf16[37,16,128]{2,1,0:T(8,128)(2,1)S(1)}) custom-call(bf16[64,16,128]{2,1,0:T(8,128)(2,1)S(1)} %get-tuple-element.24.refs_0_, f32[35,16,64]{2,1,0:T(8,128)S(1)} %get-tuple-element.25.refs_1_, ...), custom_call_target="tpu_custom_call" | custom-call | flops 100000000 | bytes 1000000 | tf_op jit(solution)/shard_map/pallas_call | solution.py:547
  9.9 1.9 %collective-permute-start.2 = (bf16[37,16,128]{2,1,0:T(8,128)(2,1)S(1)}, bf16[37,16,128]{2,1,0:T(8,128)(2,1)S(1)}, u32[]{:S(2)}, u32[]{:S(2)}) collective-permute-start(bf16[37,16,128]{2,1,0:T(8,128)(2,1)S(1)} %get-tuple-element.32), channel_id=1, source_target_pairs={{1,2},{3,4},{5,6},{2,1},{4,3},{6,5},{9,10},{11,12},{13,14},{10,9},... | collective-permute-start | bytes 454664 | tf_op jit(solution)/shard_map/ppermute | solution.py:563
  11.8 1.7 %collective-permute-start.3 = (bf16[37,16,128]{2,1,0:T(8,128)(2,1)S(1)}, bf16[37,16,128]{2,1,0:T(8,128)(2,1)S(1)}, u32[]{:S(2)}, u32[]{:S(2)}) collective-permute-start(bf16[37,16,128]{2,1,0:T(8,128)(2,1)S(1)} %get-tuple-element.33), channel_id=1, source_target_pairs={{0,1},{2,3},{4,5},{6,7},{1,0},{3,2},{5,4},{7,6},{8,9},{10,11},{12,... | collective-permute-start | bytes 454664 | tf_op jit(solution)/shard_map/ppermute | solution.py:563
  13.6 3.3 %shard_map.49.refs_3_ = f32[512,256]{1,0:T(8,128)S(1)} custom-call(f32[72,24,128]{2,1,0:T(8,128)S(1)} %get-tuple-element.34.refs_0_, bf16[9,9,128,128]{3,2,1,0:T(8,128)(2,1)S(1)} %get-tuple-element.30.refs_5_.refs_1_.refs_4_), custom_call_target="tpu_custom_call" | custom-call | flops 1000000000 | bytes 1000000 | tf_op jit(solution)/shard_map/pallas_call | solution.py:547
  16.9 0.0 collective-permute-done.2.refs_1_.refs_0_
  16.9 0.0 collective-permute-done.3.refs_2_.refs_1_
  16.9 0.5 %shard_map.50 = (f32[29,24,32]{2,1,0:T(8,128)S(1)}, bf16[8,16,128]{2,1,0:T(8,128)(2,1)S(1)}, bf16[8,16,128]{2,1,0:T(8,128)(2,1)S(1)}) custom-call(f32[29,16,32]{2,1,0:T(8,128)S(1)} %get-tuple-element.31.refs_0_, bf16[37,16,128]{2,1,0:T(8,128)(2,1)S(1)} %collective-permute-done.2.refs_1_.refs_0_, ...), custom_call_target="tpu_custom_call" | custom-call | flops 100000000 | bytes 1000000 | tf_op jit(solution)/shard_map/pallas_call | solution.py:547
  17.4 1.1 %collective-permute-start.4 = (bf16[8,16,128]{2,1,0:T(8,128)(2,1)S(1)}, bf16[8,16,128]{2,1,0:T(8,128)(2,1)S(1)}, u32[]{:S(2)}, u32[]{:S(2)}) collective-permute-start(bf16[8,16,128]{2,1,0:T(8,128)(2,1)S(1)} %get-tuple-element.36), channel_id=1, source_target_pairs={{0,2},{1,3},{4,6},{5,7},{2,0},{3,1},{6,4},{7,5},{8,10},{9,11},{12,... | collective-permute-start | bytes 98312 | tf_op jit(solution)/shard_map/ppermute | solution.py:563
  18.6 1.9 %collective-permute-start.5 = (bf16[8,16,128]{2,1,0:T(8,128)(2,1)S(1)}, bf16[8,16,128]{2,1,0:T(8,128)(2,1)S(1)}, u32[]{:S(2)}, u32[]{:S(2)}) collective-permute-start(bf16[8,16,128]{2,1,0:T(8,128)(2,1)S(1)} %get-tuple-element.37), channel_id=1, source_target_pairs={{2,4},{3,5},{4,2},{5,3},{10,12},{11,13},{12,10},{13,11},{18,20},{1... | collective-permute-start | bytes 98312 | tf_op jit(solution)/shard_map/ppermute | solution.py:563
  20.5 2.4 %shard_map.51 = (f32[64,8,256]{2,1,0:T(8,128)S(1)}, f32[280,256]{1,0:T(8,128)S(1)}) custom-call(bf16[37,16,128]{2,1,0:T(8,128)(2,1)S(1)} %collective-permute-done.2.refs_1_.refs_0_, bf16[37,16,128]{2,1,0:T(8,128)(2,1)S(1)} %collective-permute-done.3.refs_2_.refs_1_, f32[43,16,64]{2,1,0:T(8,128)S(1)} %get-tuple-element.39.refs_2_, ...), custom_call_target="tpu_custom_call" | custom-call | flops 1000000000 | bytes 1000000 | tf_op jit(solution)/shard_map/pallas_call | solution.py:547
  22.9 0.0 collective-permute-done.4.refs_1_
  22.9 1.4 %collective-permute-done.5.refs_2_ = bf16[8,16,128]{2,1,0:T(8,128)(2,1)S(1)} collective-permute-done((bf16[8,16,128]{2,1,0:T(8,128)(2,1)S(1)}, bf16[8,16,128]{2,1,0:T(8,128)(2,1)S(1)}, u32[]{:S(2)}, u32[]{:S(2)}) %collective-permute-start.5) | collective-permute-done | bytes 32800 | tf_op jit(solution)/shard_map/ppermute | solution.py:563
  24.4 2.3 %shard_map.52 = f32[64,16,128]{2,1,0:T(8,128)} custom-call(f32[29,24,32]{2,1,0:T(8,128)S(1)} %get-tuple-element.35.refs_0_, bf16[8,16,128]{2,1,0:T(8,128)(2,1)S(1)} %collective-permute-done.4.refs_1_, bf16[8,16,128]{2,1,0:T(8,128)(2,1)S(1)} %collective-permute-done.5.refs_2_, bf16[9,3,128,128]{3,2,1,0:T(8,128)(2,1)S(1)} %get-tuple-element.38.refs_3_, ...), custom_call_target="tpu_custom_call" | custom-call | flops 100000000 | bytes 1000000 | tf_op jit(solution)/shard_map/pallas_call | solution.py:547
Async XLA Ops:
  1.9 6.8 %collective-permute-start = (bf16[9,16,128]{2,1,0:T(8,128)(2,1)S(1)}, bf16[9,16,128]{2,1,0:T(8,128)(2,1)S(1)}, u32[]{:S(2)}, u32[]{:S(2)}) collective-permute-start(bf16[9,16,128]{2,1,0:T(8,128)(2,1)S(1)} %get-tuple-element.27), channel_id=1, source_target_pairs={{8,16},{16,8},{9,17},{17,9},{10,18},{18,10},{11,19},{19,11},{12,20... | collective-permute-start | bytes 110600 | tf_op jit(solution)/shard_map/ppermute | solution.py:563
  5.3 4.0 %collective-permute-start.1 = (bf16[9,16,128]{2,1,0:T(8,128)(2,1)S(1)}, bf16[9,16,128]{2,1,0:T(8,128)(2,1)S(1)}, u32[]{:S(2)}, u32[]{:S(2)}) collective-permute-start(bf16[9,16,128]{2,1,0:T(8,128)(2,1)S(1)} %get-tuple-element.28), channel_id=1, source_target_pairs={{0,8},{16,24},{8,0},{24,16},{1,9},{17,25},{9,1},{25,17},{2,10},{18... | collective-permute-start | bytes 110600 | tf_op jit(solution)/shard_map/ppermute | solution.py:563
  9.9 7.0 %collective-permute-start.2 = (bf16[37,16,128]{2,1,0:T(8,128)(2,1)S(1)}, bf16[37,16,128]{2,1,0:T(8,128)(2,1)S(1)}, u32[]{:S(2)}, u32[]{:S(2)}) collective-permute-start(bf16[37,16,128]{2,1,0:T(8,128)(2,1)S(1)} %get-tuple-element.32), channel_id=1, source_target_pairs={{1,2},{3,4},{5,6},{2,1},{4,3},{6,5},{9,10},{11,12},{13,14},{10,9},... | collective-permute-start | bytes 454664 | tf_op jit(solution)/shard_map/ppermute | solution.py:563
  11.8 5.1 %collective-permute-start.3 = (bf16[37,16,128]{2,1,0:T(8,128)(2,1)S(1)}, bf16[37,16,128]{2,1,0:T(8,128)(2,1)S(1)}, u32[]{:S(2)}, u32[]{:S(2)}) collective-permute-start(bf16[37,16,128]{2,1,0:T(8,128)(2,1)S(1)} %get-tuple-element.33), channel_id=1, source_target_pairs={{0,1},{2,3},{4,5},{6,7},{1,0},{3,2},{5,4},{7,6},{8,9},{10,11},{12,... | collective-permute-start | bytes 454664 | tf_op jit(solution)/shard_map/ppermute | solution.py:563
  17.4 5.5 %collective-permute-start.4 = (bf16[8,16,128]{2,1,0:T(8,128)(2,1)S(1)}, bf16[8,16,128]{2,1,0:T(8,128)(2,1)S(1)}, u32[]{:S(2)}, u32[]{:S(2)}) collective-permute-start(bf16[8,16,128]{2,1,0:T(8,128)(2,1)S(1)} %get-tuple-element.36), channel_id=1, source_target_pairs={{0,2},{1,3},{4,6},{5,7},{2,0},{3,1},{6,4},{7,5},{8,10},{9,11},{12,... | collective-permute-start | bytes 98312 | tf_op jit(solution)/shard_map/ppermute | solution.py:563
  18.6 5.8 %collective-permute-start.5 = (bf16[8,16,128]{2,1,0:T(8,128)(2,1)S(1)}, bf16[8,16,128]{2,1,0:T(8,128)(2,1)S(1)}, u32[]{:S(2)}, u32[]{:S(2)}) collective-permute-start(bf16[8,16,128]{2,1,0:T(8,128)(2,1)S(1)} %get-tuple-element.37), channel_id=1, source_target_pairs={{2,4},{3,5},{4,2},{5,3},{10,12},{11,13},{12,10},{13,11},{18,20},{1... | collective-permute-start | bytes 98312 | tf_op jit(solution)/shard_map/ppermute | solution.py:563

commit v7 on v6

--- a/solution.py
+++ b/solution.py
@@ -210,19 +210,17 @@
     return parts
 
 
-def join_x_kernel(charges, mid_own, coarse_own, first_in, second_in, fine_x, mid_x, coarse_x, first_out, second_out, buf, got):
+def join_x_kernel(charges, mid_own, coarse_own, first_in, second_in, mid_x, coarse_x, first_out, second_out, buf, got, edge):
     before, after = by_order(up_first("gx", 1, 1), *(v[...].astype(F32) for v in (first_in, second_in)))
     cells_x, cells_y, _ = charges.shape
     mx, cx = cells_x // 2, cells_x // 4
     mz, cz = mid_own.shape[2], coarse_own.shape[2]
     my = cells_y // 2
-    rows_x = cells_x + 8
-    own = slice(4, 4 + cells_y)
-    for edge in (0, 4 + cells_y):
-        fine_x[:, edge : edge + 4, :] = jnp.zeros((rows_x, 4, charges.shape[2]), F32)
-    fine_x[0:4, own, :] = before[0:4]
-    fine_x[4 : 4 + cells_x, own, :] = charges[...].astype(F32)
-    fine_x[4 + cells_x : rows_x, own, :] = after[0:4]
+    ends = ((0, slice(0, 4)), (4, slice(cells_y - 4, cells_y)))
+    for top, y in ends:
+        edge[0:4, top : top + 4, :] = before[0:4, y]
+        edge[4 : 4 + cells_x, top : top + 4, :] = charges[...].astype(F32)[:, y]
+        edge[4 + cells_x : 8 + cells_x, top : top + 4, :] = after[0:4, y]
     got[0], got[1] = before[4:9], after[4:9]
     mid_x[...] = rows_at(mid_own[...], -1, -5, mx + 11)
     coarse_x[...] = rows_at(coarse_own[...], -2, -6, cx + 13)
@@ -237,7 +235,7 @@
 
     def pack(out, fine_at, mid_at):
         for part, first, last, top, left in fine_parts(cells_x + 8):
-            buf[part, top : top + 4, left:] = fine_x[first:last, fine_at : fine_at + 4, :]
+            buf[part, top : top + 4, left:] = edge[first:last, fine_at : fine_at + 4, :]
         at = (cells_x + 8) // 4
         for part, first, last, top, left in quarters(mx + 11, at, mz):
             buf[part, top : top + 7, left : left + mz] = mid_x[first:last, mid_at : mid_at + 7, :]
@@ -253,13 +251,13 @@
 
     @pl.when(flag)
     def _():
-        pack(first_out, cells_y, my - 4)
-        pack(second_out, 4, 0)
+        pack(first_out, 4, my - 4)
+        pack(second_out, 0, 0)
 
     @pl.when(jnp.logical_not(flag))
     def _():
-        pack(first_out, 4, 0)
-        pack(second_out, cells_y, my - 4)
+        pack(first_out, 0, 0)
+        pack(second_out, 4, my - 4)
 
 
 def join_y_kernel(
@@ -393,8 +391,15 @@
         acc[...] = part if dx == 0 else acc[...] + part
 
 
-def own_kernel(fine_x, weights, acc, lhs):
-    rows = fine_x.shape[0]
+def own_kernel(charges, first_in, second_in, weights, acc, lhs, fine_x):
+    rows, cells_x, cells_y = fine_x.shape[0], charges.shape[0], charges.shape[1]
+    before, after = by_order(up_first("gx", 1, 1), *(v[0:4].astype(F32) for v in (first_in, second_in)))
+    own = slice(4, 4 + cells_y)
+    for edge in (0, 4 + cells_y):
+        fine_x[:, edge : edge + 4, :] = jnp.zeros((rows, 4, charges.shape[2]), F32)
+    fine_x[0:4, own, :] = before
+    fine_x[4 : 4 + cells_x, own, :] = charges[...].astype(F32)
+    fine_x[4 + cells_x : rows, own, :] = after
     gather_rows(fine_x, rows, 2, 5, fine_x.shape[2], lhs)
     convolve(lhs, weights, rows - 8, acc)
 
@@ -599,25 +604,25 @@
     fine_w, mid_w, coarse_w = bands(lines, 0, ((cells_z, 5), (mz, 3), (cz, 2)))
     rows = (cells_x + 8) // 4 + (mx + 14) // 4 + (cx + 16) // 4
     packed = ((rows, frame, cells_z), BF16)
-    fine_x, mid_x, coarse_x, first, second = call(
+    first_x, second_x = first, second
+    mid_x, coarse_x, first, second = call(
         join_x_kernel,
         [
-            ((cells_x + 8, cells_y + 8, cells_z), F32),
             ((mx + 11, frame, mz), F32),
             ((cx + 13, frame, cz), F32),
             packed,
             packed,
         ],
         [fine_own, mid_own, coarse_own, first, second],
-        [((rows, frame, cells_z), F32), ((2, 5, frame, cells_z), F32)],
+        [((rows, frame, cells_z), F32), ((2, 5, frame, cells_z), F32), ((cells_x + 8, 8, cells_z), F32)],
         after=(fine_w,),
     )
     first, second = swap(first, second, "gy", 1, ny, 1)
     (own_acc,) = call(
         own_kernel,
         [((cells_x * 8, WIDE), F32)],
-        [fine_x, fine_w],
-        [((2, (cells_x + 8) * 8, 5 * WIDE), BF16)],
+        [fine_own, first_x, second_x, fine_w],
+        [((2, (cells_x + 8) * 8, 5 * WIDE), BF16), ((cells_x + 8, cells_y + 8, cells_z), F32)],
         flops=10**9,
     )
     half = (cx + 16) // 4

time: 27.1 us -> 27 us (level)
  no operation moved by 1% of the time
where the time goes in v7:
time: 27 us; the launch traced here: 26.6 us
  Pallas kernels  13 us (48%)
  starting transfers between devices  10.1 us (37%)
  waiting for transfers between devices  3.39 us (13%)
    pallas_call x7, Pallas kernels, call(): pl.pallas_call(body, out_shape=[pltpu.VMEM(s, d) for s, d in outs] if vme...  13 us
    ppermute x6, starting transfers between devices, swap(): received.append(lax.ppermute(message, axis, pairs))  10.1 us
    ppermute x6, waiting for transfers between devices, swap(): received.append(lax.ppermute(message, axis, pairs))  3.39 us
  transfers between devices with their start and end apart: 6, of which 3 were waited for; matrix products, arithmetic and copies ran while one was open for 0% of the time, Pallas kernels for 29%

profile of v7, /device:TPU:20, one launch (start us, length us, event | category | flops | bytes accessed | tf_op | source)
XLA Modules:
  0.0 26.6 jit_solution(6837263254080269119)
XLA Ops:
  0.0 1.9 %shard_map.46 = (bf16[9,16,128]{2,1,0:T(8,128)(2,1)S(1)}, bf16[9,16,128]{2,1,0:T(8,128)(2,1)S(1)}, bf16[64,16,128]{2,1,0:T(8,128)(2,1)S(1)}, f32[35,16,64]{2,1,0...) custom-call(f32[64,16,128]{2,1,0:T(8,128)} %refs_0_.1, bf16[9,9,9]{2,1,0:T(8,128)(2,1)} %refs_1_.1, ...), custom_call_target="tpu_custom_call" | custom-call | flops 100000000 | bytes 1000000 | tf_op jit(solution)/shard_map/pallas_call | solution.py:552
  1.9 3.4 %collective-permute-start = (bf16[9,16,128]{2,1,0:T(8,128)(2,1)S(1)}, bf16[9,16,128]{2,1,0:T(8,128)(2,1)S(1)}, u32[]{:S(2)}, u32[]{:S(2)}) collective-permute-start(bf16[9,16,128]{2,1,0:T(8,128)(2,1)S(1)} %get-tuple-element.26), channel_id=1, source_target_pairs={{8,16},{16,8},{9,17},{17,9},{10,18},{18,10},{11,19},{19,11},{12,20... | collective-permute-start | bytes 110600 | tf_op jit(solution)/shard_map/ppermute | solution.py:568
  5.3 0.1 collective-permute-start.1
  5.3 2.0 %shard_map.47 = (bf16[9,9,128,128]{3,2,1,0:T(8,128)(2,1)S(1)}, bf16[9,5,128,128]{3,2,1,0:T(8,128)(2,1)S(1)}, bf16[9,3,128,128]{3,2,1,0:T(8,128)(2,1)S(1)}) custom-call(f32[27,16,128]{2,1,0:T(8,128)S(1)} %get-tuple-element.28.refs_0_), custom_call_target="tpu_custom_call" | custom-call | flops 1000000000 | bytes 1000000 | tf_op jit(solution)/shard_map/pallas_call | solution.py:552
  7.3 1.3 %collective-permute-done.refs_3_.refs_1_ = bf16[9,16,128]{2,1,0:T(8,128)(2,1)S(1)} collective-permute-done((bf16[9,16,128]{2,1,0:T(8,128)(2,1)S(1)}, bf16[9,16,128]{2,1,0:T(8,128)(2,1)S(1)}, u32[]{:S(2)}, u32[]{:S(2)}) %collective-permute-start) | collective-permute-done | bytes 36896 | tf_op jit(solution)/shard_map/ppermute | solution.py:568
  8.7 0.6 %collective-permute-done.1.refs_4_.refs_2_ = bf16[9,16,128]{2,1,0:T(8,128)(2,1)S(1)} collective-permute-done((bf16[9,16,128]{2,1,0:T(8,128)(2,1)S(1)}, bf16[9,16,128]{2,1,0:T(8,128)(2,1)S(1)}, u32[]{:S(2)}, u32[]{:S(2)}) %collective-permute-start.1) | collective-permute-done | bytes 36896 | tf_op jit(solution)/shard_map/ppermute | solution.py:568
  9.3 0.5 %shard_map.48 = (f32[43,16,64]{2,1,0:T(8,128)S(1)}, f32[29,16,32]{2,1,0:T(8,128)S(1)}, bf16[37,16,128]{2,1,0:T(8,128)(2,1)S(1)}, bf16[37,16,128]{2,1,0:T(8,128)(2,1)S(1)}) custom-call(bf16[64,16,128]{2,1,0:T(8,128)(2,1)S(1)} %get-tuple-element.23.refs_0_, f32[35,16,64]{2,1,0:T(8,128)S(1)} %get-tuple-element.24.refs_1_, ...), custom_call_target="tpu_custom_call" | custom-call | flops 100000000 | bytes 1000000 | tf_op jit(solution)/shard_map/pallas_call | solution.py:552
  9.8 1.9 %collective-permute-start.2 = (bf16[37,16,128]{2,1,0:T(8,128)(2,1)S(1)}, bf16[37,16,128]{2,1,0:T(8,128)(2,1)S(1)}, u32[]{:S(2)}, u32[]{:S(2)}) collective-permute-start(bf16[37,16,128]{2,1,0:T(8,128)(2,1)S(1)} %get-tuple-element.31), channel_id=1, source_target_pairs={{1,2},{3,4},{5,6},{2,1},{4,3},{6,5},{9,10},{11,12},{13,14},{10,9},... | collective-permute-start | bytes 454664 | tf_op jit(solution)/shard_map/ppermute | solution.py:568
  11.8 1.7 %collective-permute-start.3 = (bf16[37,16,128]{2,1,0:T(8,128)(2,1)S(1)}, bf16[37,16,128]{2,1,0:T(8,128)(2,1)S(1)}, u32[]{:S(2)}, u32[]{:S(2)}) collective-permute-start(bf16[37,16,128]{2,1,0:T(8,128)(2,1)S(1)} %get-tuple-element.32), channel_id=1, source_target_pairs={{0,1},{2,3},{4,5},{6,7},{1,0},{3,2},{5,4},{7,6},{8,9},{10,11},{12,... | collective-permute-start | bytes 454664 | tf_op jit(solution)/shard_map/ppermute | solution.py:568
  13.5 3.3 %shard_map.49.refs_3_ = f32[512,256]{1,0:T(8,128)S(1)} custom-call(bf16[64,16,128]{2,1,0:T(8,128)(2,1)S(1)} %get-tuple-element.23.refs_0_, bf16[9,16,128]{2,1,0:T(8,128)(2,1)S(1)} %collective-permute-done.refs_3_.refs_1_, bf16[9,16,128]{2,1,0:T(8,128)(2,1)S(1)} %collective-permute-done.1.refs_4_.refs_2_, ...), custom_call_target="tpu_custom_call" | custom-call | flops 1000000000 | bytes 1000000 | tf_op jit(solution)/shard_map/pallas_call | solution.py:552
  16.9 0.0 collective-permute-done.2.refs_1_.refs_0_
  16.9 0.0 collective-permute-done.3.refs_2_.refs_1_
  16.9 0.5 %shard_map.50 = (f32[29,24,32]{2,1,0:T(8,128)S(1)}, bf16[8,16,128]{2,1,0:T(8,128)(2,1)S(1)}, bf16[8,16,128]{2,1,0:T(8,128)(2,1)S(1)}) custom-call(f32[29,16,32]{2,1,0:T(8,128)S(1)} %get-tuple-element.30.refs_0_, bf16[37,16,128]{2,1,0:T(8,128)(2,1)S(1)} %collective-permute-done.2.refs_1_.refs_0_, ...), custom_call_target="tpu_custom_call" | custom-call | flops 100000000 | bytes 1000000 | tf_op jit(solution)/shard_map/pallas_call | solution.py:552
  17.4 1.1 %collective-permute-start.4 = (bf16[8,16,128]{2,1,0:T(8,128)(2,1)S(1)}, bf16[8,16,128]{2,1,0:T(8,128)(2,1)S(1)}, u32[]{:S(2)}, u32[]{:S(2)}) collective-permute-start(bf16[8,16,128]{2,1,0:T(8,128)(2,1)S(1)} %get-tuple-element.34), channel_id=1, source_target_pairs={{0,2},{1,3},{4,6},{5,7},{2,0},{3,1},{6,4},{7,5},{8,10},{9,11},{12,... | collective-permute-start | bytes 98312 | tf_op jit(solution)/shard_map/ppermute | solution.py:568
  18.5 1.9 %collective-permute-start.5 = (bf16[8,16,128]{2,1,0:T(8,128)(2,1)S(1)}, bf16[8,16,128]{2,1,0:T(8,128)(2,1)S(1)}, u32[]{:S(2)}, u32[]{:S(2)}) collective-permute-start(bf16[8,16,128]{2,1,0:T(8,128)(2,1)S(1)} %get-tuple-element.35), channel_id=1, source_target_pairs={{2,4},{3,5},{4,2},{5,3},{10,12},{11,13},{12,10},{13,11},{18,20},{1... | collective-permute-start | bytes 98312 | tf_op jit(solution)/shard_map/ppermute | solution.py:568
  20.4 2.4 %shard_map.51 = (f32[64,8,256]{2,1,0:T(8,128)S(1)}, f32[280,256]{1,0:T(8,128)S(1)}) custom-call(bf16[37,16,128]{2,1,0:T(8,128)(2,1)S(1)} %collective-permute-done.2.refs_1_.refs_0_, bf16[37,16,128]{2,1,0:T(8,128)(2,1)S(1)} %collective-permute-done.3.refs_2_.refs_1_, f32[43,16,64]{2,1,0:T(8,128)S(1)} %get-tuple-element.37.refs_2_, ...), custom_call_target="tpu_custom_call" | custom-call | flops 1000000000 | bytes 1000000 | tf_op jit(solution)/shard_map/pallas_call | solution.py:552
  22.9 0.0 collective-permute-done.4.refs_1_
  22.9 1.4 %collective-permute-done.5.refs_2_ = bf16[8,16,128]{2,1,0:T(8,128)(2,1)S(1)} collective-permute-done((bf16[8,16,128]{2,1,0:T(8,128)(2,1)S(1)}, bf16[8,16,128]{2,1,0:T(8,128)(2,1)S(1)}, u32[]{:S(2)}, u32[]{:S(2)}) %collective-permute-start.5) | collective-permute-done | bytes 32800 | tf_op jit(solution)/shard_map/ppermute | solution.py:568
  24.3 2.3 %shard_map.52 = f32[64,16,128]{2,1,0:T(8,128)} custom-call(f32[29,24,32]{2,1,0:T(8,128)S(1)} %get-tuple-element.33.refs_0_, bf16[8,16,128]{2,1,0:T(8,128)(2,1)S(1)} %collective-permute-done.4.refs_1_, bf16[8,16,128]{2,1,0:T(8,128)(2,1)S(1)} %collective-permute-done.5.refs_2_, bf16[9,3,128,128]{3,2,1,0:T(8,128)(2,1)S(1)} %get-tuple-element.36.refs_3_, ...), custom_call_target="tpu_custom_call" | custom-call | flops 100000000 | bytes 1000000 | tf_op jit(solution)/shard_map/pallas_call | solution.py:552
Async XLA Ops:
  1.9 6.8 %collective-permute-start = (bf16[9,16,128]{2,1,0:T(8,128)(2,1)S(1)}, bf16[9,16,128]{2,1,0:T(8,128)(2,1)S(1)}, u32[]{:S(2)}, u32[]{:S(2)}) collective-permute-start(bf16[9,16,128]{2,1,0:T(8,128)(2,1)S(1)} %get-tuple-element.26), channel_id=1, source_target_pairs={{8,16},{16,8},{9,17},{17,9},{10,18},{18,10},{11,19},{19,11},{12,20... | collective-permute-start | bytes 110600 | tf_op jit(solution)/shard_map/ppermute | solution.py:568
  5.3 4.0 %collective-permute-start.1 = (bf16[9,16,128]{2,1,0:T(8,128)(2,1)S(1)}, bf16[9,16,128]{2,1,0:T(8,128)(2,1)S(1)}, u32[]{:S(2)}, u32[]{:S(2)}) collective-permute-start(bf16[9,16,128]{2,1,0:T(8,128)(2,1)S(1)} %get-tuple-element.27), channel_id=1, source_target_pairs={{0,8},{16,24},{8,0},{24,16},{1,9},{17,25},{9,1},{25,17},{2,10},{18... | collective-permute-start | bytes 110600 | tf_op jit(solution)/shard_map/ppermute | solution.py:568
  9.8 7.0 %collective-permute-start.2 = (bf16[37,16,128]{2,1,0:T(8,128)(2,1)S(1)}, bf16[37,16,128]{2,1,0:T(8,128)(2,1)S(1)}, u32[]{:S(2)}, u32[]{:S(2)}) collective-permute-start(bf16[37,16,128]{2,1,0:T(8,128)(2,1)S(1)} %get-tuple-element.31), channel_id=1, source_target_pairs={{1,2},{3,4},{5,6},{2,1},{4,3},{6,5},{9,10},{11,12},{13,14},{10,9},... | collective-permute-start | bytes 454664 | tf_op jit(solution)/shard_map/ppermute | solution.py:568
  11.8 5.1 %collective-permute-start.3 = (bf16[37,16,128]{2,1,0:T(8,128)(2,1)S(1)}, bf16[37,16,128]{2,1,0:T(8,128)(2,1)S(1)}, u32[]{:S(2)}, u32[]{:S(2)}) collective-permute-start(bf16[37,16,128]{2,1,0:T(8,128)(2,1)S(1)} %get-tuple-element.32), channel_id=1, source_target_pairs={{0,1},{2,3},{4,5},{6,7},{1,0},{3,2},{5,4},{7,6},{8,9},{10,11},{12,... | collective-permute-start | bytes 454664 | tf_op jit(solution)/shard_map/ppermute | solution.py:568
  17.4 5.5 %collective-permute-start.4 = (bf16[8,16,128]{2,1,0:T(8,128)(2,1)S(1)}, bf16[8,16,128]{2,1,0:T(8,128)(2,1)S(1)}, u32[]{:S(2)}, u32[]{:S(2)}) collective-permute-start(bf16[8,16,128]{2,1,0:T(8,128)(2,1)S(1)} %get-tuple-element.34), channel_id=1, source_target_pairs={{0,2},{1,3},{4,6},{5,7},{2,0},{3,1},{6,4},{7,5},{8,10},{9,11},{12,... | collective-permute-start | bytes 98312 | tf_op jit(solution)/shard_map/ppermute | solution.py:568
  18.5 5.8 %collective-permute-start.5 = (bf16[8,16,128]{2,1,0:T(8,128)(2,1)S(1)}, bf16[8,16,128]{2,1,0:T(8,128)(2,1)S(1)}, u32[]{:S(2)}, u32[]{:S(2)}) collective-permute-start(bf16[8,16,128]{2,1,0:T(8,128)(2,1)S(1)} %get-tuple-element.35), channel_id=1, source_target_pairs={{2,4},{3,5},{4,2},{5,3},{10,12},{11,13},{12,10},{13,11},{18,20},{1... | collective-permute-start | bytes 98312 | tf_op jit(solution)/shard_map/ppermute | solution.py:568
